TPU v7x, 32 devices: a whole 2x2x4 slice. The times are simulated.
32 devices in a mesh: dp: 4 (over z), ctx: 8 (over y, x, core).
Axes of the slice: x: 2, y: 2, z: 4, core: 2. Of those that a mesh axis runs over, the one named last changes fastest.
Arguments:
- inputs: bfloat16 [8, 1024, 2048], P('dp', 'ctx'), may hold values from -6 to 6
- lengths: int32 [8], P('dp'), may hold values from 64 to 1024, as said below
- attention_gain: bfloat16 [2048], replicated, may hold values from 0.25 to 1.75
- query_weight: bfloat16 [2048, 2048], P(('dp', 'ctx')), may hold values from -0.125 to 0.125
- key_matrix: bfloat16 [2048, 512], P(('dp', 'ctx')), may hold values from -0.125 to 0.125
- value_matrix: bfloat16 [2048, 512], P(('dp', 'ctx')), may hold values from -0.125 to 0.125
- out_weight: bfloat16 [2048, 2048], P(('dp', 'ctx')), may hold values from -0.75 to 0.75
- query_gain: bfloat16 [64], replicated, may hold values from 0.25 to 1.75
- key_gain: bfloat16 [64], replicated, may hold values from 0.25 to 1.75
- feedforward_gain: bfloat16 [2048], replicated, may hold values from 0.25 to 1.75
- gate_weight: bfloat16 [2048, 8192], P(('dp', 'ctx')), may hold values from -0.125 to 0.125
- up_weight: bfloat16 [2048, 8192], P(('dp', 'ctx')), may hold values from -0.125 to 0.125
- down_weight: bfloat16 [2048, 8192], P(('dp', 'ctx')), may hold values from -0.0625 to 0.0625
- cotangent: bfloat16 [8, 1024, 2048], P('dp', 'ctx'), may hold values from -6 to 6
Outputs:
- outputs: bfloat16 [8, 1024, 2048], P('dp', 'ctx')
- input_gradient: bfloat16 [8, 1024, 2048], P('dp', 'ctx')
- attention_gain_gradient: float32 [2048], replicated
- query_weight_gradient: float32 [2048, 2048], P(('dp', 'ctx'))
- key_weight_gradient: float32 [2048, 512], P(('dp', 'ctx'))
- value_weight_gradient: float32 [2048, 512], P(('dp', 'ctx'))
- out_weight_gradient: float32 [2048, 2048], P(('dp', 'ctx'))
- query_gain_gradient: float32 [64], replicated
- key_gain_gradient: float32 [64], replicated
- feedforward_gain_gradient: float32 [2048], replicated
- gate_weight_gradient: float32 [2048, 8192], P(('dp', 'ctx'))
- up_weight_gradient: float32 [2048, 8192], P(('dp', 'ctx'))
- down_weight_gradient: float32 [2048, 8192], P(('dp', 'ctx'))
Inputs may be any that keep to these rules, and one draw needn't show every extreme that they name: `lengths`: in each aligned block of 2 rows one row has length 1024; some row has length 64.
All inputs are finite; a program needn't handle non-finite values.
Results may differ from a plain program's by a relative error of at most 0.02.
Values may be sent and summed in bfloat16 or wider, within the bound.
No kernel may reach another device: no remote copies, remote signals or barrier semaphores. Data moves between devices by JAX's collectives and lax.ppermute only.
A program may use at most 768 MiB of HBM per device.

v0:
```python
import jax
import jax.numpy as jnp
from jax import lax
from jax.sharding import PartitionSpec as P

QUERY_HEADS_TOTAL = 32
KEY_VALUE_HEADS = 8
HEAD_SIZE = 64


epsilon = 1e-06


def rms_scale(value_rows):
    return lax.rsqrt(jnp.mean(value_rows * value_rows, axis=-1, keepdims=True) + epsilon)


def rotary_tables(positions, width):
    inverse = 10000.0 ** (-(jnp.arange(width // 2, dtype=jnp.float32) * 2.0) / width)
    angle_table = positions.astype(jnp.float32)[:, None] * inverse[None, :]
    return (jnp.cos(angle_table), jnp.sin(angle_table))


def rotate(value_rows, cosine, sine):
    half = value_rows.shape[-1] // 2
    first = value_rows[..., :half]
    second = value_rows[..., half:]
    return jnp.concatenate(
        [first * cosine - second * sine, second * cosine + first * sine], axis=-1
    )


def contract_rows(left, right):
    return lax.dot_general(
        left, right, (((0,), (0,)), ((), ())), preferred_element_type=jnp.float32
    )


def contract_cols(left, right):
    return lax.dot_general(
        left, right, (((1,), (1,)), ((), ())), preferred_element_type=jnp.float32
    )


def body(
    inputs,
    lengths,
    attention_gain,
    query_weight,
    key_matrix,
    value_matrix,
    out_weight,
    query_gain,
    key_gain,
    feedforward_gain,
    gate_weight,
    up_weight,
    down_weight,
    cotangent,
):
    row_total, slot_count, width = inputs.shape
    count_of_tokens = row_total * slot_count
    sequence_total = slot_count * lax.axis_size("ctx")
    key_tile_block = min(512, sequence_total)
    block_count = sequence_total // key_tile_block
    group_count = QUERY_HEADS_TOTAL // KEY_VALUE_HEADS
    factor = HEAD_SIZE ** (-0.5)
    slot_positions = lax.axis_index("ctx") * slot_count + jnp.arange(slot_count, dtype=jnp.int32)
    cosine, sine = rotary_tables(jnp.tile(slot_positions, row_total), HEAD_SIZE)
    cosine = cosine[:, None, :]
    sine = sine[:, None, :]
    flat = inputs.reshape(count_of_tokens, width).astype(jnp.float32)
    first_scale = rms_scale(flat)
    normed = flat * first_scale
    hidden_state = (normed * attention_gain).astype(jnp.bfloat16)
    full_query, full_key, full_value, full_out = (
        lax.all_gather(query_weight, ("dp", "ctx"), axis=0, tiled=True),
        lax.all_gather(key_matrix, ("dp", "ctx"), axis=0, tiled=True),
        lax.all_gather(value_matrix, ("dp", "ctx"), axis=0, tiled=True),
        lax.all_gather(out_weight, ("dp", "ctx"), axis=0, tiled=True),
    )
    raw_queries = jnp.dot(hidden_state, full_query, preferred_element_type=jnp.float32)
    unrotated_keys = jnp.dot(hidden_state, full_key, preferred_element_type=jnp.float32)
    flattened_values = jnp.dot(hidden_state, full_value, preferred_element_type=jnp.float32).astype(
        jnp.bfloat16
    )

    def prepare(query_raw, unrotated_key, gain_of_query, gain_of_key):
        query_heads = query_raw.reshape(count_of_tokens, QUERY_HEADS_TOTAL, HEAD_SIZE)
        key_head_rows = unrotated_key.reshape(count_of_tokens, KEY_VALUE_HEADS, HEAD_SIZE)
        rotated_query = rotate(query_heads * rms_scale(query_heads) * gain_of_query, cosine, sine)
        rotated_key = rotate(key_head_rows * rms_scale(key_head_rows) * gain_of_key, cosine, sine)
        return (
            rotated_query.reshape(count_of_tokens, QUERY_HEADS_TOTAL * HEAD_SIZE),
            rotated_key.reshape(count_of_tokens, KEY_VALUE_HEADS * HEAD_SIZE),
        )

    (rotated_queries, rotated_keys), prepare_pull = jax.vjp(
        prepare,
        raw_queries,
        unrotated_keys,
        query_gain.astype(jnp.float32),
        key_gain.astype(jnp.float32),
    )
    grouped_queries = rotated_queries.astype(jnp.bfloat16).reshape(
        row_total, slot_count, KEY_VALUE_HEADS, group_count, HEAD_SIZE
    )
    flattened_keys = rotated_keys.astype(jnp.bfloat16).reshape(
        row_total, slot_count, KEY_VALUE_HEADS * HEAD_SIZE
    )
    flattened_values = flattened_values.reshape(row_total, slot_count, KEY_VALUE_HEADS * HEAD_SIZE)
    gathered_keys, gathered_values = (
        lax.all_gather(flattened_keys, "ctx", axis=1, tiled=True),
        lax.all_gather(flattened_values, "ctx", axis=1, tiled=True),
    )

    def score_block(all_keys, start_offset):
        key_piece = lax.dynamic_slice_in_dim(all_keys, start_offset, key_tile_block, 1).reshape(
            row_total, key_tile_block, KEY_VALUE_HEADS, HEAD_SIZE
        )
        scores = (
            jnp.einsum(
                "rqhgd,rkhd->rhgqk", grouped_queries, key_piece, preferred_element_type=jnp.float32
            )
            * factor
        )
        key_pos = start_offset + jnp.arange(key_tile_block, dtype=jnp.int32)
        allowed = (key_pos[None, None, :] <= slot_positions[None, :, None]) & (
            key_pos[None, None, :] < lengths[:, None, None]
        )
        return (jnp.where(allowed[:, None, None, :, :], scores, -1e30), key_piece)

    def value_block(all_values, start_offset):
        return lax.dynamic_slice_in_dim(all_values, start_offset, key_tile_block, 1).reshape(
            row_total, key_tile_block, KEY_VALUE_HEADS, HEAD_SIZE
        )

    def statistics(carry, index):
        top, total = carry
        scores, key_piece = score_block(gathered_keys, index * key_tile_block)
        new_top = jnp.maximum(top, jnp.max(scores, axis=-1))
        total = total * jnp.exp(top - new_top) + jnp.sum(
            jnp.exp(scores - new_top[..., None]), axis=-1
        )
        return ((new_top, total), None)

    statistic_shape = (row_total, KEY_VALUE_HEADS, group_count, slot_count)
    (top, total), unused = lax.scan(
        statistics,
        (jnp.full(statistic_shape, -1e30, jnp.float32), jnp.zeros(statistic_shape, jnp.float32)),
        jnp.arange(block_count, dtype=jnp.int32),
    )
    log_total = top + jnp.log(total)

    def weighted(accum, index):
        start_offset = index * key_tile_block
        scores, key_piece = score_block(gathered_keys, start_offset)
        probs = jnp.exp(scores - log_total[..., None]).astype(jnp.bfloat16)
        value_piece = value_block(gathered_values, start_offset)
        return (
            accum
            + jnp.einsum(
                "rhgqk,rkhd->rqhgd", probs, value_piece, preferred_element_type=jnp.float32
            ),
            None,
        )

    accum, unused = lax.scan(
        weighted,
        jnp.zeros((row_total, slot_count, KEY_VALUE_HEADS, group_count, HEAD_SIZE), jnp.float32),
        jnp.arange(block_count, dtype=jnp.int32),
    )
    attended = accum.reshape(count_of_tokens, QUERY_HEADS_TOTAL * HEAD_SIZE).astype(jnp.bfloat16)
    mixed = flat + contract_cols(attended, full_out)
    second_scale = rms_scale(mixed)
    normed_again = mixed * second_scale
    hidden_again = (normed_again * feedforward_gain).astype(jnp.bfloat16)
    feed_width = gate_weight.shape[1]
    pieces = (
        lax.all_gather(gate_weight, ("dp", "ctx"), axis=0, tiled=True),
        lax.all_gather(up_weight, ("dp", "ctx"), axis=0, tiled=True),
    )
    columns = hidden_again
    gate = jnp.dot(columns, pieces[0], preferred_element_type=jnp.float32)
    upward = jnp.dot(columns, pieces[1], preferred_element_type=jnp.float32)
    sigmoid_gate = jax.nn.sigmoid(gate)
    silu_gate = gate * sigmoid_gate
    inner = (silu_gate * upward).astype(jnp.bfloat16)
    feed_out = contract_cols(inner, lax.all_gather(down_weight, ("dp", "ctx"), axis=0, tiled=True))
    outputs = (mixed + feed_out).astype(jnp.bfloat16).reshape(row_total, slot_count, width)
    grad_output = cotangent.reshape(count_of_tokens, width)
    columns = grad_output
    grad_inner = jnp.dot(
        columns,
        lax.all_gather(down_weight, ("dp", "ctx"), axis=0, tiled=True),
        preferred_element_type=jnp.float32,
    )
    down_weight_gradient = lax.psum_scatter(
        contract_rows(grad_output, inner), ("dp", "ctx"), scatter_dimension=0, tiled=True
    )
    grad_gate = (grad_inner * upward * sigmoid_gate * (1.0 + gate * (1.0 - sigmoid_gate))).astype(
        jnp.bfloat16
    )
    grad_up = (grad_inner * silu_gate).astype(jnp.bfloat16)
    pieces = lax.all_gather((gate_weight, up_weight), ("dp", "ctx"), axis=0, tiled=True)
    grad_hidden_again = contract_cols(grad_gate, pieces[0]) + contract_cols(grad_up, pieces[1])
    columns = hidden_again
    inner_gradient = lax.psum_scatter(
        jnp.concatenate(
            [contract_rows(columns, grad_gate), contract_rows(columns, grad_up)], axis=1
        ),
        ("dp", "ctx"),
        scatter_dimension=0,
        tiled=True,
    )
    gate_weight_gradient = inner_gradient[:, :feed_width]
    up_weight_gradient = inner_gradient[:, feed_width:]
    feedforward_gain_local = jnp.sum(grad_hidden_again * normed_again, axis=0)
    scaled_again = grad_hidden_again * feedforward_gain
    grad_mixed = grad_output.astype(jnp.float32) + second_scale * (
        scaled_again - normed_again * jnp.mean(scaled_again * normed_again, axis=-1, keepdims=True)
    )
    grad_branch = grad_mixed.astype(jnp.bfloat16)
    back_query, back_key, back_value, back_out = (
        lax.all_gather(query_weight, ("dp", "ctx"), axis=0, tiled=True),
        lax.all_gather(key_matrix, ("dp", "ctx"), axis=0, tiled=True),
        lax.all_gather(value_matrix, ("dp", "ctx"), axis=0, tiled=True),
        lax.all_gather(out_weight, ("dp", "ctx"), axis=0, tiled=True),
    )
    back_keys, back_values = (gathered_keys, gathered_values)
    attended_gradient = jnp.dot(grad_branch, back_out, preferred_element_type=jnp.float32).astype(
        jnp.bfloat16
    )
    grouped_gradient = attended_gradient.reshape(
        row_total, slot_count, KEY_VALUE_HEADS, group_count, HEAD_SIZE
    )

    def delta_block(delta, index):
        start_offset = index * key_tile_block
        scores, key_piece = score_block(back_keys, start_offset)
        probs = jnp.exp(scores - log_total[..., None])
        value_piece = value_block(back_values, start_offset)
        grad_probs = jnp.einsum(
            "rqhgd,rkhd->rhgqk", grouped_gradient, value_piece, preferred_element_type=jnp.float32
        )
        return (delta + jnp.sum(probs * grad_probs, axis=-1), None)

    delta, unused = lax.scan(
        delta_block,
        jnp.zeros(statistic_shape, jnp.float32),
        jnp.arange(block_count, dtype=jnp.int32),
    )

    def gradient_block(carry, index):
        query_gradient, every_key_gradient, every_value_gradient = carry
        start_offset = index * key_tile_block
        scores, key_piece = score_block(back_keys, start_offset)
        probs = jnp.exp(scores - log_total[..., None])
        value_piece = value_block(back_values, start_offset)
        grad_probs = jnp.einsum(
            "rqhgd,rkhd->rhgqk", grouped_gradient, value_piece, preferred_element_type=jnp.float32
        )
        grad_scores = (probs * (grad_probs - delta[..., None])).astype(jnp.bfloat16)
        query_gradient = (
            query_gradient
            + jnp.einsum(
                "rhgqk,rkhd->rqhgd", grad_scores, key_piece, preferred_element_type=jnp.float32
            )
            * factor
        )
        key_summand = (
            jnp.einsum(
                "rhgqk,rqhgd->rkhd",
                grad_scores,
                grouped_queries,
                preferred_element_type=jnp.float32,
            )
            * factor
        )
        value_summand = jnp.einsum(
            "rhgqk,rqhgd->rkhd",
            probs.astype(jnp.bfloat16),
            grouped_gradient,
            preferred_element_type=jnp.float32,
        )
        every_key_gradient = lax.dynamic_update_slice_in_dim(
            every_key_gradient,
            key_summand.reshape(row_total, key_tile_block, KEY_VALUE_HEADS * HEAD_SIZE),
            start_offset,
            1,
        )
        every_value_gradient = lax.dynamic_update_slice_in_dim(
            every_value_gradient,
            value_summand.reshape(row_total, key_tile_block, KEY_VALUE_HEADS * HEAD_SIZE),
            start_offset,
            1,
        )
        return ((query_gradient, every_key_gradient, every_value_gradient), None)

    complete_shape = (row_total, sequence_total, KEY_VALUE_HEADS * HEAD_SIZE)
    (query_gradient, every_key_gradient, every_value_gradient), unused = lax.scan(
        gradient_block,
        (
            jnp.zeros(
                (row_total, slot_count, KEY_VALUE_HEADS, group_count, HEAD_SIZE), jnp.float32
            ),
            jnp.zeros(complete_shape, jnp.float32),
            jnp.zeros(complete_shape, jnp.float32),
        ),
        jnp.arange(block_count, dtype=jnp.int32),
    )
    local_key_gradient, local_value_gradient = (
        lax.psum_scatter(
            every_key_gradient.astype(jnp.bfloat16), "ctx", scatter_dimension=1, tiled=True
        ).astype(jnp.float32),
        lax.psum_scatter(
            every_value_gradient.astype(jnp.bfloat16), "ctx", scatter_dimension=1, tiled=True
        ).astype(jnp.float32),
    )
    raw_query_term, raw_key_term, query_gain_local, key_gain_local = prepare_pull(
        (
            query_gradient.reshape(count_of_tokens, QUERY_HEADS_TOTAL * HEAD_SIZE),
            local_key_gradient.reshape(count_of_tokens, KEY_VALUE_HEADS * HEAD_SIZE),
        )
    )
    grad_raw_queries = raw_query_term.astype(jnp.bfloat16)
    grad_raw_keys = raw_key_term.astype(jnp.bfloat16)
    unrotated_value_gradient = local_value_gradient.reshape(
        count_of_tokens, KEY_VALUE_HEADS * HEAD_SIZE
    ).astype(jnp.bfloat16)
    grad_hidden = (
        contract_cols(grad_raw_queries, back_query)
        + contract_cols(grad_raw_keys, back_key)
        + contract_cols(unrotated_value_gradient, back_value)
    )
    attention_gradient = lax.psum_scatter(
        jnp.concatenate(
            [
                contract_rows(hidden_state, grad_raw_queries),
                contract_rows(hidden_state, grad_raw_keys),
                contract_rows(hidden_state, unrotated_value_gradient),
                contract_rows(grad_branch, attended),
            ],
            axis=1,
        ),
        ("dp", "ctx"),
        scatter_dimension=0,
        tiled=True,
    )
    query_cols = QUERY_HEADS_TOTAL * HEAD_SIZE
    key_value_columns = KEY_VALUE_HEADS * HEAD_SIZE
    query_weight_gradient = attention_gradient[:, :query_cols]
    key_weight_gradient = attention_gradient[:, query_cols : query_cols + key_value_columns]
    value_weight_gradient = attention_gradient[
        :, query_cols + key_value_columns : query_cols + 2 * key_value_columns
    ]
    out_weight_gradient = attention_gradient[:, query_cols + 2 * key_value_columns :]
    attention_gain_local = jnp.sum(grad_hidden * normed, axis=0)
    scaled_first = grad_hidden * attention_gain
    input_gradient = (
        grad_mixed
        + first_scale
        * (scaled_first - normed * jnp.mean(scaled_first * normed, axis=-1, keepdims=True))
    ).astype(jnp.bfloat16)
    attention_gain_gradient, query_gain_gradient, key_gain_gradient, feedforward_gain_gradient = (
        lax.psum(
            (attention_gain_local, query_gain_local, key_gain_local, feedforward_gain_local),
            ("dp", "ctx"),
        )
    )
    return (
        outputs,
        input_gradient.reshape(row_total, slot_count, width),
        attention_gain_gradient,
        query_weight_gradient,
        key_weight_gradient,
        value_weight_gradient,
        out_weight_gradient,
        query_gain_gradient,
        key_gain_gradient,
        feedforward_gain_gradient,
        gate_weight_gradient,
        up_weight_gradient,
        down_weight_gradient,
    )


def solution(mesh):
    placed = (
        P("dp", "ctx", None),
        P("dp"),
        P(),
        P(("dp", "ctx"), None),
        P(("dp", "ctx"), None),
        P(("dp", "ctx"), None),
        P(("dp", "ctx"), None),
        P(),
        P(),
        P(),
        P(("dp", "ctx"), None),
        P(("dp", "ctx"), None),
        P(("dp", "ctx"), None),
        P("dp", "ctx", None),
    )
    return jax.shard_map(
        body,
        mesh=mesh,
        in_specs=placed,
        out_specs=(
            P("dp", "ctx", None),
            P("dp", "ctx", None),
            P(),
            P(("dp", "ctx"), None),
            P(("dp", "ctx"), None),
            P(("dp", "ctx"), None),
            P(("dp", "ctx"), None),
            P(),
            P(),
            P(),
            P(("dp", "ctx"), None),
            P(("dp", "ctx"), None),
            P(("dp", "ctx"), None),
        ),
        check_vma=False,
    )
```

profile of v0, /device:TPU:0, one launch (start us, length us, event | category | flops | bytes accessed | tf_op | source)
XLA Modules:
  0.0 4329.6 jit_solution(10448454011093264970)
XLA Ops:
  12.9 57.1 %all-gather.14.cloned.1.call-done = bf16[2048,512]{1,0:T(8,128)(2,1)} async-done(((bf16[64,512]{1,0:T(8,128)(2,1)}), bf16[2048,512]{1,0:T(8,128)(2,1)}) %all-gather.14.cloned.1.call-update) | async-done | bytes 2097168 | tf_op jit(solution)/shard_map/all_gather | solution.py:78
  70.0 3.9 copy.77
  78.5 49.6 %all-gather.10.cloned.1.call-done = bf16[2048,512]{1,0:T(8,128)(2,1)} async-done(((bf16[64,512]{1,0:T(8,128)(2,1)}), bf16[2048,512]{1,0:T(8,128)(2,1)}) %all-gather.10.cloned.1.call-update) | async-done | bytes 2097168 | tf_op jit(solution)/shard_map/all_gather | solution.py:79
  134.4 72.9 %all-gather.18.cloned.1.call-done = bf16[2048,2048]{1,0:T(8,128)(2,1)} async-done(((bf16[64,2048]{1,0:T(8,128)(2,1)}), bf16[2048,2048]{1,0:T(8,128)(2,1)}) %all-gather.18.cloned.1.call-update) | async-done | bytes 8388624 | tf_op jit(solution)/shard_map/all_gather | solution.py:77
  207.3 12.4 copy.79
  219.7 5.8 multiply_reduce_fusion.7
  227.9 8.5 all-gather.16.cloned.1.call-done
  236.4 41.2 while.50
  239.4 7.4 fusion.147
  246.8 10.2 exponential_reduce_fusion.2
  260.1 7.4 fusion.147
  267.4 10.2 exponential_reduce_fusion.2
  277.7 21.1 while.51
  281.3 6.5 bitcast_add_fusion.4
  291.2 7.7 bitcast_add_fusion.4
  301.9 45.3 %all-gather.20.cloned.1.call-done = bf16[2048,2048]{1,0:T(8,128)(2,1)} async-done(((bf16[64,2048]{1,0:T(8,128)(2,1)}), bf16[2048,2048]{1,0:T(8,128)(2,1)}) %all-gather.20.cloned.1.call-update) | async-done | bytes 8388624 | tf_op jit(solution)/shard_map/all_gather | solution.py:80
  347.2 5.9 multiply_reduce_fusion.6
  354.7 188.8 %all-gather.22.cloned.1.call-done = bf16[2048,8192]{1,0:T(8,128)(2,1)} async-done(((bf16[64,8192]{1,0:T(8,128)(2,1)}), bf16[2048,8192]{1,0:T(8,128)(2,1)}) %all-gather.22.cloned.1.call-update) | async-done | bytes 33554448 | tf_op jit(solution)/shard_map/all_gather | solution.py:180
  543.4 17.9 fusion.54
  561.4 177.9 %all-gather.24.cloned.1.call-done = bf16[2048,8192]{1,0:T(8,128)(2,1)} async-done(((bf16[64,8192]{1,0:T(8,128)(2,1)}), bf16[2048,8192]{1,0:T(8,128)(2,1)}) %all-gather.24.cloned.1.call-update) | async-done | bytes 33554448 | tf_op jit(solution)/shard_map/all_gather | solution.py:181
  739.3 18.4 fusion.55
  757.7 177.4 %all-gather.26.cloned.1.call-done = bf16[2048,8192]{1,0:T(8,128)(2,1)} async-done(((bf16[64,8192]{1,0:T(8,128)(2,1)}), bf16[2048,8192]{1,0:T(8,128)(2,1)}) %all-gather.26.cloned.1.call-update) | async-done | bytes 33554448 | tf_op jit(solution)/shard_map/all_gather | solution.py:189
  935.1 28.4 multiply_convert_fusion
  963.5 25.3 fusion.59
  988.8 17.0 fusion.56
  1005.8 18.9 multiply_reduce_fusion
  1028.5 5.7 convolution_convert_fusion
  1034.2 3.2 reshape.590
  1037.4 4.5 copy.87
  1041.9 22.8 while.52
  1047.5 5.7 fusion.158
  1058.9 5.7 fusion.158
  1067.8 98.4 %while.53 = (s32[]{:T(128)}, f32[2,128,8,4,64]{1,4,3,2,0:T(8,128)}, bf16[2,1024,512]{1,2,0:T(8,128)(2,1)}, bf16[2,1024,512]{2,1,0:T(8,128)(2,1)}, s32[2]{0:T(128...) while((s32[]{:T(128)}, f32[2,128,8,4,64]{1,4,3,2,0:T(8,128)}, ...), condition=%wide.region_15.16_spmd.clone, body=%wide.region_14.15_spmd.clone.sunk | while | flops 2729117184 | bytes 167355856 | solution.py:301
  1071.0 9.5 fusion.169
  1080.9 10.5 fusion.170
  1091.4 6.4 bitcast_add_fusion.5
  1097.8 4.0 bitcast_multiply_fusion.4
  1103.3 8.8 fusion.171
  1119.7 9.5 fusion.169
  1129.6 10.5 fusion.170
  1140.1 6.9 bitcast_add_fusion.5
  1147.1 4.0 bitcast_multiply_fusion.4
  1152.6 8.8 fusion.171
  1166.2 4.8 copy.111
  1174.2 26.5 fusion.58
  1200.7 87.0 %pad_maximum_fusion = f32[2048,16384]{1,0:T(8,128)} fusion(f32[2048,8192]{1,0:T(8,128)} %fusion.59, f32[2048,8192]{1,0:T(8,128)} %fusion.58), kind=kLoop, calls=%fused_computation.68 | loop fusion | flops 33554432 | bytes 268435456 | tf_op jit(solution)/shard_map/concatenate | solution.py:209
  1289.4 3.0 copy.88
  1292.3 3.4 reshape_reshape.9
  1300.5 8.2 fusion.60
  1308.7 8.4 fusion.38
  1320.0 3.9 convolution_bitcast_fusion.1
  1325.6 28.6 pad_maximum_fusion.1
  1354.2 39.4 copy.113
  1395.0 26.8 convolution_bitcast_fusion
  1421.9 61.6 %copy.115 = f32[2048,8192]{1,0:T(8,128)} copy(f32[2048,8192]{0,1:T(8,128)} %convolution_bitcast_fusion) | data formatting | bytes 134217728
  1484.7 7.9 fusion.57
  1492.6 18.5 fusion.36
  1511.1 2.5 convolution_add_fusion.1
  1516.0 44.1 %all-reduce.5 = (f32[2048]{0:T(1024)}, f32[64]{0:T(128)}, f32[64]{0:T(128)}, f32[2048]{0:T(1024)}) all-reduce(f32[2048]{0:T(1024)S(1)} %get-tuple-element.538, f32[64]{0:T(128)S(1)} %copy-done.67, f32[64]{0:T(128)S(1)} %copy-done.66, f32[2048]{0:T(1024)S(1)} %copy-done.60), channel_id=1, replica_groups=mesh['dp'=4,'ctx'=8] {'dp','ctx'}, use_global_device_ids=true, to_apply=%region_22.23 | all-reduce | flops 4224 | bytes 33792 | tf_op jit(solution)/shard_map/psum | solution.py:366
  1560.1 3.2 add_convert_fusion
  1563.3 1602.9 %all-reduce.8.cloned.1.call-done = f32[2048,16384]{1,0:T(8,128)} async-done(((f32[2048,16384]{1,0:T(8,128)}), f32[2048,16384]{1,0:T(8,128)}) %all-reduce.8.cloned.1.call-update) | async-done | bytes 134217744
  3166.2 4.9 fusion.49
  3171.1 438.7 %reduce-scatter.15.cloned.1.call-done = f32[64,5120]{1,0:T(8,128)} async-done(((f32[2048,5120]{1,0:T(8,128)}), f32[64,5120]{1,0:T(8,128)}) %reduce-scatter.15.cloned.1.call-update) | async-done | bytes 1310736
  3613.8 709.0 %reduce-scatter.17.cloned.1.call-done = f32[64,8192]{1,0:T(8,128)} async-done(((f32[2048,8192]{1,0:T(8,128)}), f32[64,8192]{1,0:T(8,128)}) %reduce-scatter.17.cloned.1.call-update) | async-done | bytes 2097168
  (320 shorter events, 90.3 us)
Async XLA Ops:
  7.2 5.4 copy-start.8
  7.2 62.8 %all-gather.14.cloned.1.call-start = ((), (), s32[]{:S(2)}) async-start(), calls=%async_computation.6 | async-start | bytes 2162688 | tf_op jit(solution)/shard_map/all_gather | solution.py:78
  7.9 120.2 %all-gather.10.cloned.1.call-start = ((), (), s32[]{:S(2)}) async-start(), calls=%async_computation.4 | async-start | bytes 2162688 | tf_op jit(solution)/shard_map/all_gather | solution.py:79
  8.7 198.6 %all-gather.18.cloned.1.call-start = ((), (), s32[]{:S(2)}) async-start(), calls=%async_computation.8 | async-start | bytes 8650752 | tf_op jit(solution)/shard_map/all_gather | solution.py:77
  9.4 227.0 %all-gather.16.cloned.1.call-start = ((), (), s32[]{:S(2)}) async-start(), calls=%async_computation.7 | async-start | bytes 2359296 | tf_op jit(solution)/shard_map/all_gather | solution.py:113
  10.1 68.0 %copy-start.48 = (f32[2048]{0:T(1024)}, f32[2048]{0:T(1024)S(1)}, u32[]{:S(2)}) copy-start(f32[2048]{0:T(1024)S(1)} %convert_element_type.136) | copy-start | bytes 24580
  10.8 65.5 %copy-start.61 = (f32[64]{0:T(128)}, f32[64]{0:T(128)S(1)}, u32[]{:S(2)}) copy-start(f32[64]{0:T(128)S(1)} %convert_element_type.141) | copy-start | bytes 772
  12.4 65.8 %copy-start.58 = (f32[256]{0:T(256)}, f32[256]{0:T(256)S(1)}, u32[]{:S(2)}) copy-start(f32[256]{0:T(256)S(1)} %get-tuple-element.654) | copy-start | bytes 3076
  12.6 213.4 %copy-start.38 = (f32[256,32]{0,1:T(8,128)}, f32[256,32]{0,1:T(8,128)S(1)}, u32[]{:S(2)}) copy-start(f32[256,32]{0,1:T(8,128)S(1)} %get-tuple-element.651) | copy-start | bytes 98308
  12.6 213.4 %copy-start.40 = (f32[256,32]{0,1:T(8,128)}, f32[256,32]{0,1:T(8,128)S(1)}, u32[]{:S(2)}) copy-start(f32[256,32]{0,1:T(8,128)S(1)} %get-tuple-element.652) | copy-start | bytes 98308
  12.9 206.8 %copy-start.11 = (bf16[2,128,2048]{2,1,0:T(8,128)(2,1)}, bf16[2,128,2048]{2,1,0:T(8,128)(2,1)S(1)}, u32[]{:S(2)}) copy-start(bf16[2,128,2048]{2,1,0:T(8,128)(2,1)S(1)} %multiply_convert_fusion.4) | copy-start | bytes 3145732
  78.1 199.6 %all-gather.12.cloned.1.call-start = ((), (), s32[]{:S(2)}) async-start(), calls=%async_computation.5 | async-start | bytes 2359296 | tf_op jit(solution)/shard_map/all_gather | solution.py:114
  130.4 4.0 copy-start.68
  130.4 4.0 copy-start.65
  131.3 215.9 %all-gather.20.cloned.1.call-start = ((), (), s32[]{:S(2)}) async-start(), calls=%async_computation.9 | async-start | bytes 8650752 | tf_op jit(solution)/shard_map/all_gather | solution.py:80
  131.9 411.6 %all-gather.22.cloned.1.call-start = ((), (), s32[]{:S(2)}) async-start(), calls=%async_computation.10 | async-start | bytes 34603008 | tf_op jit(solution)/shard_map/all_gather | solution.py:180
  132.6 606.7 %all-gather.24.cloned.1.call-start = ((), (), s32[]{:S(2)}) async-start(), calls=%async_computation.11 | async-start | bytes 34603008 | tf_op jit(solution)/shard_map/all_gather | solution.py:181
  133.4 801.8 %all-gather.26.cloned.1.call-start = ((), (), s32[]{:S(2)}) async-start(), calls=%async_computation.12 | async-start | bytes 34603008 | tf_op jit(solution)/shard_map/all_gather | solution.py:189
  134.1 1183.0 %reduce-scatter.13.cloned.1.call-start = ((), (), s32[]{:S(2)}) async-start(), calls=%async_computation.14 | async-start | bytes 2359296
  134.4 91.2 %copy-start.63 = (f32[64]{0:T(128)}, f32[64]{0:T(128)S(1)}, u32[]{:S(2)}) copy-start(f32[64]{0:T(128)S(1)} %convert_element_type.145) | copy-start | bytes 772
  227.3 9.1 copy-start.45
  298.9 3.0 copy-start.46
  298.9 3.0 copy-start.54
  298.9 48.3 %copy-start.9 = (bf16[2,128,2048]{2,1,0:T(8,128)(2,1)S(1)}, bf16[2,128,2048]{2,1,0:T(8,128)(2,1)}, u32[]{:S(2)}) copy-start(bf16[2,128,2048]{2,1,0:T(8,128)(2,1)} %param.22) | copy-start | bytes 3145732
  301.9 51.2 %copy-start.30 = (bf16[2,128,8,4,64]{1,0,4,3,2:T(2,128)(2,1)}, bf16[2,128,8,4,64]{1,0,4,3,2:T(2,128)(2,1)S(1)}, u32[]{:S(2)}) copy-start(bf16[2,128,8,4,64]{1,0,4,3,2:T(2,128)(2,1)S(1)} %copy.82) | copy-start | bytes 3145732
  354.7 608.8 %copy-start.19 = (bf16[256,2048]{1,0:T(8,128)(2,1)}, bf16[256,2048]{1,0:T(8,128)(2,1)S(1)}, u32[]{:S(2)}) copy-start(bf16[256,2048]{1,0:T(8,128)(2,1)S(1)} %multiply_convert_fusion.3) | copy-start | bytes 3145732
  561.4 373.8 %copy-start.28 = (bf16[2,128,2048]{2,1,0:T(8,128)(2,1)S(1)}, bf16[2,128,2048]{2,1,0:T(8,128)(2,1)}, u32[]{:S(2)}) copy-start(bf16[2,128,2048]{2,1,0:T(8,128)(2,1)} %param.35) | copy-start | bytes 3145732
  988.8 17.0 copy-start.23
  1037.4 4.5 copy-start.3
  1037.4 4.5 copy-start.42
  1037.4 4.5 copy-start.47
  1037.4 4.5 copy-start.55
  1071.0 9.9 copy-start.6
  1091.4 6.4 copy-start
  1097.8 4.1 copy-start.24
  1112.2 4.7 copy-start.2
  1119.7 9.9 copy-start.6
  1140.1 7.0 copy-start
  1147.1 4.0 copy-start.24
  1161.5 4.8 copy-start.2
  1173.0 147.0 %reduce-scatter.11.cloned.1.call-start = ((), (), s32[]{:S(2)}) async-start(), calls=%async_computation.13 | async-start | bytes 2359296 | tf_op jit(solution)/shard_map/reduce_scatter | solution.py:316
  1200.7 1965.5 %all-reduce.8.cloned.1.call-start = ((), (), s32[]{:S(2)}) async-start(), calls=%async_computation.17 | async-start | bytes 268435456
  1287.8 2322.0 %reduce-scatter.15.cloned.1.call-start = ((), (), s32[]{:S(2)}) async-start(), calls=%async_computation.15 | async-start | bytes 43253760
  1292.3 3.4 copy-start.39
  1292.3 3.4 copy-start.41
  1300.5 8.2 copy-start.15
  1300.5 8.2 copy-start.31
  1317.1 2.2 copy-start.27
  1317.1 2.3 copy-start.51
  1317.1 2.3 copy-start.62
  1320.0 4.0 copy-start.57
  1320.0 4.8 copy-start.13
  1393.6 2929.2 %reduce-scatter.17.cloned.1.call-start = ((), (), s32[]{:S(2)}) async-start(), calls=%async_computation.16 | async-start | bytes 69206016
  1492.6 18.5 copy-start.21
  1492.6 18.5 copy-start.35
  1511.1 2.6 copy-start.10
  1511.1 2.6 copy-start.36
  1511.1 2.6 copy-start.37
  1511.1 2.6 copy-start.49
  1511.1 2.6 copy-start.59
  1513.7 2.3 copy-start.60
  1513.7 2.3 copy-start.66
  1513.8 2.2 copy-start.67
  1513.8 46.4 %copy-start.16 = (f32[256,2048]{1,0:T(8,128)S(1)}, f32[256,2048]{1,0:T(8,128)}, u32[]{:S(2)}) copy-start(f32[256,2048]{1,0:T(8,128)} %copy-done.14) | copy-start | bytes 6291460
  (27 other events, 35.8 us)
Sparse Core Ops, SparseCore 0:
  10.9 59.0 all-gather.13
  72.8 55.2 all-gather.9
  131.0 76.2 all-gather.17
  209.6 26.7 all-gather.15
  238.7 28.1 all-gather.11
  269.7 77.4 all-gather.19
  350.0 193.3 all-gather.21
  546.3 192.9 all-gather.23
  742.1 192.9 all-gather.25
  1173.1 39.3 reduce-scatter.12
  1216.1 41.2 reduce-scatter.10
  1287.9 1878.2 all-reduce.7
  3168.5 441.2 reduce-scatter.14
  3612.6 710.1 reduce-scatter.16
where the time goes:
time: 4340 us; the launch traced here: 4330 us
  waiting for transfers between devices  3530 us (81%)
  matrix products  378 us (9%)
  local copies, waits for them, and re-layouts  197 us (5%)
  other arithmetic  155 us (4%)
  blocking collectives  44.1 us (1%)
    unnamed x18, waiting for transfers between devices  2760 us
    all_gather x1, waiting for transfers between devices, body(): lax.all_gather(gate_weight, ('dp', 'ctx'), axis=0, tiled=True)  189 us
    all_gather x1, waiting for transfers between devices, body(): lax.all_gather(up_weight, ('dp', 'ctx'), axis=0, tiled=True)  178 us
    all_gather x1, waiting for transfers between devices, body(): lax.all_gather(down_weight, ('dp', 'ctx'), axis=0, tiled=True)  177 us
    unnamed x130, local copies, waits for them, and re-layouts  127 us
    dot_general x7, matrix products, contract_rows(): lax.dot_general(left, right, (((0,), (0,)), ((), ())), preferred_element_...  99.9 us
    concatenate x1, other arithmetic, body(): jnp.concatenate([contract_rows(columns, grad_gate), contract_rows(columns...  87 us
  transfers between devices with their start and end apart: 14, of which 11 were waited for; matrix products, arithmetic and copies ran while one was open for 11% of the time, Pallas kernels for 0%

commit v1 on v0

v1 whole, which is shorter than its diff:
```python
import functools

import jax
import jax.numpy as jnp
from jax import lax
from jax.experimental import pallas as pl
from jax.experimental.pallas import tpu as pltpu
from jax.sharding import PartitionSpec as P

QUERY_HEADS_TOTAL = 32
KEY_VALUE_HEADS = 8
HEAD_SIZE = 64
FACTOR = HEAD_SIZE ** (-0.5)

epsilon = 1e-06
f32 = jnp.float32
bf16 = jnp.bfloat16


def rms_scale(value_rows):
    return lax.rsqrt(jnp.mean(value_rows * value_rows, axis=-1, keepdims=True) + epsilon)


def rotary_tables(positions, width):
    inverse = 10000.0 ** (-(jnp.arange(width // 2, dtype=f32) * 2.0) / width)
    angle_table = positions.astype(f32)[:, None] * inverse[None, :]
    return (jnp.cos(angle_table), jnp.sin(angle_table))


def rotate(value_rows, cosine, sine):
    half = value_rows.shape[-1] // 2
    first = value_rows[..., :half]
    second = value_rows[..., half:]
    return jnp.concatenate(
        [first * cosine - second * sine, second * cosine + first * sine], axis=-1
    )


def dot_nn(left, right):
    return jnp.dot(left, right, preferred_element_type=f32)


def dot_tn(left, right):
    return lax.dot_general(left, right, (((0,), (0,)), ((), ())), preferred_element_type=f32)


def dot_nt(left, right):
    return lax.dot_general(left, right, (((1,), (1,)), ((), ())), preferred_element_type=f32)


def hop(value, bit):
    return lax.ppermute(value, "ctx", [(i, i ^ bit) for i in range(lax.axis_size("ctx"))])


def gather_tokens(value):
    if lax.axis_size("ctx") != 8:
        return lax.all_gather(value, "ctx", axis=0)
    half = value.shape[0] // 2
    by_x, by_y = hop(value, 2), hop(value, 4)
    far = jnp.concatenate([hop(by_x[:half], 4), hop(by_y[half:], 2)], axis=0)
    return jnp.stack(
        [value, hop(value, 1), by_x, hop(by_x, 1), by_y, hop(by_y, 1), far, hop(far, 1)], axis=0
    )


def scatter_tokens(parts):
    if lax.axis_size("ctx") != 8:
        whole = parts.astype(bf16).reshape(-1, parts.shape[-1])
        return lax.psum_scatter(whole, "ctx", scatter_dimension=0, tiled=True).astype(f32)
    half = parts.shape[1] // 2
    own = [parts[2 * k] + hop(parts[2 * k + 1], 1).astype(f32) for k in (3, 2, 1, 0)]
    far, y_sum, x_sum, total = own
    far = far.astype(bf16)
    from_x, from_y = hop(far[:half], 2), hop(far[half:], 4)
    y_sum = jnp.concatenate([y_sum[:half] + from_x.astype(f32), y_sum[half:]], axis=0)
    x_sum = jnp.concatenate([x_sum[:half], x_sum[half:] + from_y.astype(f32)], axis=0)
    return total + hop(x_sum.astype(bf16), 2).astype(f32) + hop(y_sum.astype(bf16), 4).astype(f32)


def spread_columns(packed):
    rows, parts, columns = packed.shape
    return lax.all_to_all(
        packed.reshape(rows, parts * columns), "ctx", split_axis=1, concat_axis=0, tiled=True
    )


def gather_rows(block):
    return lax.all_gather(block, "dp", axis=0, tiled=True)


def scatter_rows(gradient):
    return lax.psum_scatter(gradient.astype(bf16), "dp", scatter_dimension=0, tiled=True)


def collect_columns(block):
    parts = lax.axis_size("ctx")
    columns = block.shape[1]
    out = lax.all_to_all(block, "ctx", split_axis=0, concat_axis=1, tiled=True)
    return out.reshape(out.shape[0], parts, columns).astype(f32)


def heads_to_rows(block, heads):
    return jnp.concatenate(
        [block[:, h * HEAD_SIZE : (h + 1) * HEAD_SIZE] for h in range(heads)], axis=0
    )


def columns_to_heads(block, heads, slots):
    return jnp.concatenate(
        [block[:, h * slots : (h + 1) * slots].T for h in range(heads)], axis=1
    )


def masked_scores(key_block, query_rows, start, query_block, slots, length):
    scores = dot_nt(key_block, query_rows)
    key_pos = start + lax.broadcasted_iota(jnp.int32, scores.shape, 0)
    query_pos = query_block * slots + lax.rem(
        lax.broadcasted_iota(jnp.int32, scores.shape, 1), slots
    )
    return jnp.where((key_pos <= query_pos) & (key_pos < length), scores, -1e30)


def attend_kernel(
    blocks, slots, heads, chunk, base_ref, len_ref, q_ref, k_ref, v_ref, o_ref, lse_ref, k_all, v_t
):
    row, query_block = pl.program_id(0), pl.program_id(1)
    base, length = base_ref[0], len_ref[row]

    @pl.when(query_block == 0)
    def _():
        for j in range(blocks):
            at = lax.bitwise_xor(base, j)
            k_all[j * slots : (j + 1) * slots, :] = k_ref[at, 0]
            v_t[:, j * slots : (j + 1) * slots] = v_ref[at, 0].T

    count = lax.div(
        jnp.minimum((query_block + 1) * slots, length) + (chunk - 1), jnp.int32(chunk)
    )
    query_rows = heads_to_rows(q_ref[0, 0], heads) * FACTOR
    columns = heads * slots

    def step(j, carry):
        top, total, accum = carry
        start = pl.multiple_of(j * chunk, chunk)
        scores = masked_scores(
            k_all[pl.ds(start, chunk), :], query_rows, start, query_block, slots, length
        )
        new_top = jnp.maximum(top, jnp.max(scores, axis=0, keepdims=True))
        probs = jnp.exp(scores - new_top)
        alpha = jnp.exp(top - new_top)
        total = total * alpha + jnp.sum(probs, axis=0, keepdims=True)
        accum = accum * alpha + dot_nn(v_t[:, pl.ds(start, chunk)], probs.astype(bf16))
        return new_top, total, accum

    top, total, accum = lax.fori_loop(
        0,
        count,
        step,
        (
            jnp.full((1, columns), -1e30, f32),
            jnp.zeros((1, columns), f32),
            jnp.zeros((HEAD_SIZE, columns), f32),
        ),
    )
    o_ref[0, 0] = columns_to_heads(accum / total, heads, slots).astype(bf16)
    lse_ref[0, 0] = top + jnp.log(total)


def attend_back_kernel(
    blocks, slots, heads, chunk,
    base_ref, len_ref, q_ref, k_ref, v_ref, o_ref, do_ref, lse_ref,
    dq_ref, dk_ref, dv_ref, k_all, v_all, k_t, dk_all, dv_all,
):
    row, query_block = pl.program_id(0), pl.program_id(1)
    base, length = base_ref[0], len_ref[row]

    @pl.when(query_block == 0)
    def _():
        for j in range(blocks):
            at = lax.bitwise_xor(base, j)
            keys = k_ref[at, 0]
            k_all[j * slots : (j + 1) * slots, :] = keys
            k_t[:, j * slots : (j + 1) * slots] = keys.T
            v_all[j * slots : (j + 1) * slots, :] = v_ref[at, 0]
        dk_all[...] = jnp.zeros_like(dk_all)
        dv_all[...] = jnp.zeros_like(dv_all)

    count = lax.div(
        jnp.minimum((query_block + 1) * slots, length) + (chunk - 1), jnp.int32(chunk)
    )
    query_rows = heads_to_rows(q_ref[0, 0], heads) * FACTOR
    grad_rows = heads_to_rows(do_ref[0, 0], heads)
    products = do_ref[0, 0].astype(f32) * o_ref[0, 0].astype(f32)
    delta = jnp.concatenate(
        [
            jnp.sum(products[:, h * HEAD_SIZE : (h + 1) * HEAD_SIZE].T, axis=0, keepdims=True)
            for h in range(heads)
        ],
        axis=1,
    )
    log_total = lse_ref[0, 0]

    def step(j, dq_t):
        start = pl.multiple_of(j * chunk, chunk)
        at = pl.ds(start, chunk)
        scores = masked_scores(k_all[at, :], query_rows, start, query_block, slots, length)
        probs = jnp.exp(scores - log_total)
        grad_probs = dot_nt(v_all[at, :], grad_rows)
        grad_scores = (probs * (grad_probs - delta)).astype(bf16)
        dv_all[at, :] += dot_nn(probs.astype(bf16), grad_rows)
        dk_all[at, :] += dot_nn(grad_scores, query_rows)
        return dq_t + dot_nn(k_t[:, at], grad_scores)

    dq_t = lax.fori_loop(0, count, step, jnp.zeros((HEAD_SIZE, heads * slots), f32))
    dq_ref[0, 0] = columns_to_heads(dq_t * FACTOR, heads, slots)

    @pl.when(query_block == blocks - 1)
    def _():
        for j in range(blocks):
            at = lax.bitwise_xor(base, j)
            dk_ref[at, 0] = dk_all[j * slots : (j + 1) * slots, :]
            dv_ref[at, 0] = dv_all[j * slots : (j + 1) * slots, :]


def attention_specs(blocks, slots, width):
    own = lambda r, i, base, lens: (lax.bitwise_xor(base[0], i), r, 0, 0)
    whole = lambda r, i, base, lens: (0, r, 0, 0)
    return (
        pl.BlockSpec((1, 1, slots, width), own),
        pl.BlockSpec((blocks, 1, slots, HEAD_SIZE), whole),
        pl.BlockSpec((1, 1, 1, width // HEAD_SIZE * slots), own),
    )


def attend(base, lengths, queries, keys, values):
    blocks, rows, slots, width = queries.shape
    heads = width // HEAD_SIZE
    chunk = 2 * slots
    query_spec, key_spec, lse_spec = attention_specs(blocks, slots, width)
    total = blocks * slots
    work = rows * heads * total * total // 2
    return pl.pallas_call(
        functools.partial(attend_kernel, blocks, slots, heads, chunk),
        grid_spec=pltpu.PrefetchScalarGridSpec(
            num_scalar_prefetch=2,
            grid=(rows, blocks),
            in_specs=[query_spec, key_spec, key_spec],
            out_specs=[query_spec, lse_spec],
            scratch_shapes=[
                pltpu.VMEM((total, HEAD_SIZE), bf16),
                pltpu.VMEM((HEAD_SIZE, total), bf16),
            ],
        ),
        out_shape=[
            jax.ShapeDtypeStruct(queries.shape, bf16),
            jax.ShapeDtypeStruct((blocks, rows, 1, heads * slots), f32),
        ],
        compiler_params=pltpu.CompilerParams(vmem_limit_bytes=32 * 2**20),
        cost_estimate=pl.CostEstimate(
            flops=16 * HEAD_SIZE * work, bytes_accessed=4 * queries.size, transcendentals=work
        ),
        name="attend",
    )(base, lengths, queries, keys, values)


def attend_back(base, lengths, queries, keys, values, attended, gradient, log_total):
    blocks, rows, slots, width = queries.shape
    heads = width // HEAD_SIZE
    chunk = 2 * slots
    query_spec, key_spec, lse_spec = attention_specs(blocks, slots, width)
    total = blocks * slots
    work = rows * heads * total * total // 2
    return pl.pallas_call(
        functools.partial(attend_back_kernel, blocks, slots, heads, chunk),
        grid_spec=pltpu.PrefetchScalarGridSpec(
            num_scalar_prefetch=2,
            grid=(rows, blocks),
            in_specs=[query_spec, key_spec, key_spec, query_spec, query_spec, lse_spec],
            out_specs=[query_spec, key_spec, key_spec],
            scratch_shapes=[
                pltpu.VMEM((total, HEAD_SIZE), bf16),
                pltpu.VMEM((total, HEAD_SIZE), bf16),
                pltpu.VMEM((HEAD_SIZE, total), bf16),
                pltpu.VMEM((total, HEAD_SIZE), f32),
                pltpu.VMEM((total, HEAD_SIZE), f32),
            ],
        ),
        out_shape=[
            jax.ShapeDtypeStruct(queries.shape, f32),
            jax.ShapeDtypeStruct(keys.shape, f32),
            jax.ShapeDtypeStruct(values.shape, f32),
        ],
        compiler_params=pltpu.CompilerParams(vmem_limit_bytes=32 * 2**20),
        cost_estimate=pl.CostEstimate(
            flops=40 * HEAD_SIZE * work, bytes_accessed=12 * queries.size, transcendentals=work
        ),
        name="attend_back",
    )(base, lengths, queries, keys, values, attended, gradient, log_total)


def body(
    inputs,
    lengths,
    attention_gain,
    query_weight,
    key_matrix,
    value_matrix,
    out_weight,
    query_gain,
    key_gain,
    feedforward_gain,
    gate_weight,
    up_weight,
    down_weight,
    cotangent,
):
    rows, slots, width = inputs.shape
    tokens = rows * slots
    parts = lax.axis_size("ctx")
    heads = QUERY_HEADS_TOTAL // parts
    share = parts // KEY_VALUE_HEADS
    query_cols = heads * HEAD_SIZE
    weight_rows = query_weight.shape[0]
    feed = gate_weight.shape[1] // parts
    all_tokens = parts * tokens
    if parts == 8:
        base = lax.axis_index("ctx").astype(jnp.int32)
    else:
        base = jnp.int32(0)

    key_blocks = [
        jnp.repeat(w.reshape(weight_rows, KEY_VALUE_HEADS, HEAD_SIZE), share, axis=1)
        for w in (key_matrix, value_matrix)
    ]
    attention_pack = jnp.concatenate(
        [query_weight.reshape(weight_rows, parts, query_cols)]
        + key_blocks
        + [out_weight.reshape(weight_rows, parts, query_cols)],
        axis=2,
    )
    attention_block = spread_columns(attention_pack)
    gate_weight, up_weight, down_weight, attention_block = lax.optimization_barrier(
        (gate_weight, up_weight, down_weight, attention_block)
    )
    feed_block = spread_columns(
        jnp.concatenate(
            [w.reshape(weight_rows, parts, feed) for w in (gate_weight, up_weight)], axis=2
        )
    )
    down_block = spread_columns(down_weight.reshape(weight_rows, parts, feed))
    attention_full = gather_rows(attention_block)
    feed_full = gather_rows(feed_block)
    down_full = gather_rows(down_block)
    qkv_cols = query_cols + 2 * HEAD_SIZE
    qkv_full = attention_full[:, :qkv_cols]
    out_full = attention_full[:, qkv_cols:]

    flat = inputs.reshape(tokens, width).astype(f32)
    first_scale = rms_scale(flat)
    normed = flat * first_scale
    hidden = gather_tokens((normed * attention_gain).astype(bf16)).reshape(all_tokens, width)
    raw = dot_nn(hidden, qkv_full)
    positions = (
        lax.bitwise_xor(base, jnp.arange(parts, dtype=jnp.int32))[:, None] * slots
        + jnp.arange(slots, dtype=jnp.int32)[None, :]
    )
    cosine, sine = [
        jnp.broadcast_to(
            t.reshape(parts, 1, slots, 1, HEAD_SIZE // 2),
            (parts, rows, slots, 1, HEAD_SIZE // 2),
        ).reshape(all_tokens, 1, HEAD_SIZE // 2)
        for t in rotary_tables(positions.reshape(-1), HEAD_SIZE)
    ]

    def prepare(query_raw, key_raw, gain_of_query, gain_of_key):
        query_heads = query_raw.reshape(all_tokens, heads, HEAD_SIZE)
        key_heads = key_raw.reshape(all_tokens, 1, HEAD_SIZE)
        rotated_query = rotate(query_heads * rms_scale(query_heads) * gain_of_query, cosine, sine)
        rotated_key = rotate(key_heads * rms_scale(key_heads) * gain_of_key, cosine, sine)
        return (
            rotated_query.reshape(all_tokens, query_cols),
            rotated_key.reshape(all_tokens, HEAD_SIZE),
        )

    (rotated_queries, rotated_keys), prepare_pull = jax.vjp(
        prepare,
        raw[:, :query_cols],
        raw[:, query_cols : query_cols + HEAD_SIZE],
        query_gain.astype(f32),
        key_gain.astype(f32),
    )
    queries = rotated_queries.astype(bf16).reshape(parts, rows, slots, query_cols)
    keys = rotated_keys.astype(bf16).reshape(parts, rows, slots, HEAD_SIZE)
    values = raw[:, query_cols + HEAD_SIZE :].astype(bf16).reshape(parts, rows, slots, HEAD_SIZE)
    base_array = base.reshape(1)
    attended, log_total = attend(base_array, lengths, queries, keys, values)
    attended_rows = attended.reshape(all_tokens, query_cols)
    out_part = dot_nt(attended_rows, out_full).astype(bf16)
    mixed = flat + scatter_tokens(out_part.reshape(parts, tokens, width))

    second_scale = rms_scale(mixed)
    normed_again = mixed * second_scale
    hidden_again = gather_tokens((normed_again * feedforward_gain).astype(bf16)).reshape(
        all_tokens, width
    )
    cotangent_flat = cotangent.reshape(tokens, width)
    cotangents = gather_tokens(cotangent_flat).reshape(all_tokens, width)
    gate_up = dot_nn(hidden_again, feed_full)
    gate, upward = gate_up[:, :feed], gate_up[:, feed:]
    sigmoid_gate = jax.nn.sigmoid(gate)
    silu_gate = gate * sigmoid_gate
    inner = (silu_gate * upward).astype(bf16)
    down_gradient = scatter_rows(dot_tn(cotangents, inner))
    grad_inner = dot_nn(cotangents, down_full)
    grad_gate = (grad_inner * upward * sigmoid_gate * (1.0 + gate * (1.0 - sigmoid_gate))).astype(
        bf16
    )
    grad_up = (grad_inner * silu_gate).astype(bf16)
    grad_gate_up = jnp.concatenate([grad_gate, grad_up], axis=1)
    hidden_again_part = dot_nt(grad_gate_up, feed_full).astype(bf16)
    grad_hidden_again = scatter_tokens(hidden_again_part.reshape(parts, tokens, width))
    feed_gradient = scatter_rows(dot_tn(hidden_again, grad_gate_up))
    feed_out = scatter_tokens(dot_nt(inner, down_full).astype(bf16).reshape(parts, tokens, width))
    outputs = (mixed + feed_out).astype(bf16).reshape(rows, slots, width)
    down_weight_gradient = collect_columns(down_gradient).reshape(weight_rows, parts * feed)
    feed_collected = collect_columns(feed_gradient)
    gate_weight_gradient = feed_collected[:, :, :feed].reshape(weight_rows, parts * feed)
    up_weight_gradient = feed_collected[:, :, feed:].reshape(weight_rows, parts * feed)

    feedforward_gain_local = jnp.sum(grad_hidden_again * normed_again, axis=0)
    scaled_again = grad_hidden_again * feedforward_gain
    grad_mixed = cotangent_flat.astype(f32) + second_scale * (
        scaled_again - normed_again * jnp.mean(scaled_again * normed_again, axis=-1, keepdims=True)
    )

    grad_branch = gather_tokens(grad_mixed.astype(bf16)).reshape(all_tokens, width)
    attended_gradient = dot_nn(grad_branch, out_full).astype(bf16)
    grad_queries, grad_keys, grad_values = attend_back(
        base_array,
        lengths,
        queries,
        keys,
        values,
        attended,
        attended_gradient.reshape(parts, rows, slots, query_cols),
        log_total,
    )
    raw_query_term, raw_key_term, query_gain_local, key_gain_local = prepare_pull(
        (
            grad_queries.reshape(all_tokens, query_cols),
            grad_keys.reshape(all_tokens, HEAD_SIZE),
        )
    )
    grad_raw = jnp.concatenate(
        [raw_query_term, raw_key_term, grad_values.reshape(all_tokens, HEAD_SIZE)], axis=1
    ).astype(bf16)
    hidden_part = dot_nt(grad_raw, qkv_full).astype(bf16)
    grad_hidden = scatter_tokens(hidden_part.reshape(parts, tokens, width))
    attention_gradient = scatter_rows(
        jnp.concatenate([dot_tn(hidden, grad_raw), dot_tn(grad_branch, attended_rows)], axis=1)
    )
    attention_collected = collect_columns(attention_gradient)
    query_weight_gradient = attention_collected[:, :, :query_cols].reshape(weight_rows, -1)
    key_weight_gradient, value_weight_gradient = [
        attention_collected[:, :, start : start + HEAD_SIZE]
        .reshape(weight_rows, KEY_VALUE_HEADS, share, HEAD_SIZE)
        .sum(axis=2)
        .reshape(weight_rows, KEY_VALUE_HEADS * HEAD_SIZE)
        for start in (query_cols, query_cols + HEAD_SIZE)
    ]
    out_weight_gradient = attention_collected[:, :, qkv_cols:].reshape(weight_rows, -1)

    attention_gain_local = jnp.sum(grad_hidden * normed, axis=0)
    scaled_first = grad_hidden * attention_gain
    input_gradient = (
        grad_mixed
        + first_scale
        * (scaled_first - normed * jnp.mean(scaled_first * normed, axis=-1, keepdims=True))
    ).astype(bf16)
    attention_gain_gradient, query_gain_gradient, key_gain_gradient, feedforward_gain_gradient = (
        lax.psum(
            (attention_gain_local, query_gain_local, key_gain_local, feedforward_gain_local),
            ("dp", "ctx"),
        )
    )
    return (
        outputs,
        input_gradient.reshape(rows, slots, width),
        attention_gain_gradient,
        query_weight_gradient,
        key_weight_gradient,
        value_weight_gradient,
        out_weight_gradient,
        query_gain_gradient,
        key_gain_gradient,
        feedforward_gain_gradient,
        gate_weight_gradient,
        up_weight_gradient,
        down_weight_gradient,
    )


def solution(mesh):
    weight = P(("dp", "ctx"), None)
    token = P("dp", "ctx", None)
    placed = (
        token, P("dp"), P(), weight, weight, weight, weight, P(), P(), P(), weight, weight, weight, token,
    )
    returned = (
        token, token, P(), weight, weight, weight, weight, P(), P(), P(), weight, weight, weight,
    )
    return jax.shard_map(
        body, mesh=mesh, in_specs=placed, out_specs=returned, check_vma=False
    )
```

time: 4340 us -> 880 us (0.20)
  waiting for transfers between devices: 3530 us -> 330 us
  matrix products: 378 us -> 151 us
  other arithmetic: 155 us -> 60 us
  local copies, waits for them, and re-layouts: 197 us -> 125 us
  starting transfers between devices: 0.73 us -> 65.4 us
  Pallas kernels: 0 us -> 49.1 us
    unnamed x18 -> x6, waiting for transfers between devices: 2760 us -> 0.1 us
    all_gather x9 -> x3, waiting for transfers between devices: 778 us -> 0.01 us  [gather_rows(): return lax.all_gather(block, 'dp', axis=0, tiled=True)]
    dot_general x39 -> x12, matrix products: 378 us -> 151 us  [the longest x4 59.2 us: dot_nn(): return jnp.dot(left, right, preferred_element_type=f32)]
    ppermute x0 -> x64, waiting for transfers between devices: none -> 207 us  [hop(): lax.ppermute(value, 'ctx', [(i, i ^ bit) for i in range(lax.axis_size('ct...]
    concatenate x2 -> x11, other arithmetic: 116 us -> 6.21 us  [the longest x4 2.65 us: scatter_tokens(): jnp.concatenate([y_sum[:half] + from_x.astype(f32), y_sum[half:]], axis=0)]
    reduce_scatter x1 -> x3, waiting for transfers between devices: 0.01 us -> 90 us  [scatter_rows(): lax.psum_scatter(gradient.astype(bf16), 'dp', scatter_dimension=0, tiled=...]
    unnamed x130 -> x171, local copies, waits for them, and re-layouts: 127 us -> 61.8 us
    pallas_call x0 -> x2, Pallas kernels: none -> 49.1 us  [the longest x1 27.3 us: attend_back(): pl.pallas_call(functools.partial(attend_back_kernel, blocks, slots, heads...]
  transfers between devices with their start and end apart: 14 -> 75, of which waited for: 11 -> 28; matrix products, arithmetic and copies ran while one was open for 11% -> 31% of each run, Pallas kernels for 0% -> 6%
where the time goes in v1:
time: 880 us; the launch traced here: 871 us
  waiting for transfers between devices  330 us (38%)
  matrix products  151 us (17%)
  local copies, waits for them, and re-layouts  125 us (14%)
  blocking collectives  75.7 us (9%)
  starting transfers between devices  65.4 us (7%)
  other arithmetic  60 us (7%)
  Pallas kernels  49.1 us (6%)
  between operations  15.9 us (2%)
    ppermute x64, waiting for transfers between devices, hop(): lax.ppermute(value, 'ctx', [(i, i ^ bit) for i in range(lax.axis_size('ct...  207 us
    reduce_scatter x3, waiting for transfers between devices, scatter_rows(): lax.psum_scatter(gradient.astype(bf16), 'dp', scatter_dimension=0, tiled=...  90 us
    unnamed x171, local copies, waits for them, and re-layouts  61.8 us
    psum x1, blocking collectives, body(): lax.psum((attention_gain_local, query_gain_local, key_gain_local, feedfor...  59.4 us
    dot_general x4, matrix products, dot_nn(): return jnp.dot(left, right, preferred_element_type=f32)  59.2 us
    dot_general x4, matrix products, dot_tn(): lax.dot_general(left, right, (((0,), (0,)), ((), ())), preferred_element_...  46.8 us
    dot_general x4, matrix products, dot_nt(): lax.dot_general(left, right, (((1,), (1,)), ((), ())), preferred_element_...  45 us
    ppermute x64, starting transfers between devices, hop(): lax.ppermute(value, 'ctx', [(i, i ^ bit) for i in range(lax.axis_size('ct...  44.4 us
  transfers between devices with their start and end apart: 75, of which 28 were waited for; matrix products, arithmetic and copies ran while one was open for 31% of the time, Pallas kernels for 6%

profile of v1, /device:TPU:0, one launch (start us, length us, event | category | flops | bytes accessed | tf_op | source)
XLA Modules:
  0.0 871.4 jit_solution(11566219162329223969)
XLA Ops:
  11.5 16.4 %all_to_all.90 = bf16[64,8,640]{2,0,1:T(8,128)(2,1)} all-to-all(bf16[64,8,640]{2,0,1:T(8,128)(2,1)S(1)} %copy.75), channel_id=1, replica_groups=mesh['dp'=4,'ctx'=8] {'ctx'}, dimensions={1} | all-to-all | bytes 1310720 | tf_op jit(solution)/shard_map/all_to_all | solution.py:82
  29.9 2.5 copy.79
  32.3 3.6 all-to-all-start.1
  52.9 2.8 fusion.7
  55.6 29.1 %collective-permute-done.1 = bf16[256,2048]{1,0:T(8,128)(2,1)} collective-permute-done((bf16[256,2048]{1,0:T(8,128)(2,1)}, bf16[256,2048]{1,0:T(8,128)(2,1)}, u32[]{:S(2)}, u32[]{:S(2)}) %collective-permute-start.1) | collective-permute-done | bytes 1048608 | tf_op jit(solution)/shard_map/ppermute | solution.py:52
  92.0 2.3 bitcast_dynamic-update-slice_fusion.30
  94.3 2.3 bitcast_dynamic-update-slice_fusion.29
  96.6 3.3 collective-permute-done.5
  102.5 15.4 %collective-permute-done.6 = bf16[128,2048]{1,0:T(8,128)(2,1)} collective-permute-done((bf16[128,2048]{1,0:T(8,128)(2,1)}, bf16[128,2048]{1,0:T(8,128)(2,1)}, u32[]{:S(2)}, u32[]{:S(2)}) %collective-permute-start.6) | collective-permute-done | bytes 524320 | tf_op jit(solution)/shard_map/ppermute | solution.py:52
  120.7 2.3 bitcast_dynamic-update-slice_fusion.27
  126.2 6.4 fusion.5
  141.9 2.4 copy.78.q_ref
  144.7 21.8 %attend.1 = (bf16[8,2,128,256]{3,2,1,0:T(8,128)(2,1)S(1)}, f32[8,2,1,512]{3,2,1,0:T(1,128)S(1)}) custom-call(s32[1]{0:T(128)} %bitcast.1.base_ref, s32[2]{0:T(128)S(1)} %copy-done.11, bf16[8,2,128,256]{3,2,1,0:T(8,128)(2,1)S(1)} %copy.78.q_ref, bf16[8,2,128,64]{3,2,1,0:T(8,128)(2,1)S(1)} %bitcast.198, bf16[8,2,128,64]{3,2,1,0:T(8,128)(2,1)S(1)} %bitcast.200), custom_call_target="tpu_custom_call" | custom-call | flops 4294967296 | bytes 2097152 | tf_op jit(solution)/shard_map/attend/pallas_call | solution.py:242
  166.6 4.0 convolution_convert_fusion.4
  170.6 2.5 fusion.31
  175.7 2.3 bitcast_dynamic-update-slice_fusion.15
  179.1 4.2 all-to-all-start.2
  190.9 2.4 bitcast_dynamic-update-slice_fusion.14
  194.3 5.4 convert_add_fusion.9
  201.3 2.3 bitcast_dynamic-update-slice_fusion.13
  203.7 5.8 collective-permute-done.37
  212.1 8.2 collective-permute-done.11
  223.0 10.9 %collective-permute-done.14 = bf16[128,2048]{1,0:T(8,128)(2,1)S(1)} collective-permute-done((bf16[128,2048]{1,0:T(8,128)(2,1)S(1)}, bf16[128,2048]{1,0:T(8,128)(2,1)S(1)}, u32[]{:S(2)}, u32[]{:S(2)}) %collective-permute-start.14) | collective-permute-done | bytes 524320 | tf_op jit(solution)/shard_map/ppermute | solution.py:52
  237.5 2.3 bitcast_dynamic-update-slice_fusion.12
  239.8 2.3 bitcast_dynamic-update-slice_fusion.11
  242.1 16.2 %collective-permute-done.12 = bf16[256,2048]{1,0:T(8,128)(2,1)S(1)} collective-permute-done((bf16[256,2048]{1,0:T(8,128)(2,1)S(1)}, bf16[256,2048]{1,0:T(8,128)(2,1)S(1)}, u32[]{:S(2)}, u32[]{:S(2)}) %collective-permute-start.12) | collective-permute-done | bytes 1048608 | tf_op jit(solution)/shard_map/ppermute | solution.py:52
  264.1 2.4 bitcast_dynamic-update-slice_fusion.10
  268.7 18.0 %collective-permute-done.17 = bf16[256,2048]{1,0:T(8,128)(2,1)S(1)} collective-permute-done((bf16[256,2048]{1,0:T(8,128)(2,1)S(1)}, bf16[256,2048]{1,0:T(8,128)(2,1)S(1)}, u32[]{:S(2)}, u32[]{:S(2)}) %collective-permute-start.17) | collective-permute-done | bytes 1048608 | tf_op jit(solution)/shard_map/ppermute | solution.py:52
  287.2 2.6 collective-permute-start.22
  292.5 5.6 collective-permute-done.21
  303.7 24.4 %fusion.38 = f32[2048,2048]{0,1:T(8,128)} fusion(bf16[2048,2048]{1,0:T(8,128)(2,1)} %bitcast.27, bf16[2048,2048]{1,0:T(8,128)(2,1)} %all-gather.6.cloned.1.call-done), kind=kOutput, calls=%fused_computation.191 | convolution fusion | flops 17179869184 | bytes 33554432 | tf_op jit(solution)/shard_map/dot_general | solution.py:40
  328.1 22.4 %multiply_convert_fusion.1 = (bf16[2048,1024]{0,1:T(8,128)(2,1)}, bf16[2048,1024]{0,1:T(8,128)(2,1)}, bf16[2048,1024]{0,1:T(8,128)(2,1)}) fusion(f32[2048,2048]{0,1:T(8,128)} %fusion.38, bf16[2048,2048]{1,0:T(8,128)(2,1)} %bitcast.42, bf16[2048,1024]{1,0:T(8,128)(2,1)} %all-gather.8.cloned.1.call-done), kind=kOutput, calls=%fused_computation.2 | convolution fusion | flops 8621391872 | bytes 41943040 | tf_op jit(solution)/shard_map/dot_general | solution.py:40
  350.5 12.2 %convolution_convert_fusion.3 = bf16[2048,2048]{1,0:T(8,128)(2,1)S(1)} fusion(bf16[2048,1024]{0,1:T(8,128)(2,1)} %get-tuple-element.51, bf16[2048,1024]{1,0:T(8,128)(2,1)} %all-gather.8.cloned.1.call-done), kind=kOutput, calls=%fused_computation.9 | convolution fusion | flops 8594128896 | bytes 16777216 | tf_op jit(solution)/shard_map/dot_general | solution.py:48
  364.6 2.4 copy-done.21
  368.0 22.5 %convolution_convert_fusion.2 = bf16[2048,2048]{1,0:T(8,128)(2,1)S(1)} fusion(bf16[2048,2048]{1,0:T(8,128)(2,1)} %all-gather.6.cloned.1.call-done, bf16[2048,1024]{0,1:T(8,128)(2,1)} %get-tuple-element.50, bf16[2048,1024]{0,1:T(8,128)(2,1)} %get-tuple-element.49), kind=kOutput, calls=%fused_computation.8 | convolution fusion | flops 17200840704 | bytes 25165824 | tf_op jit(solution)/shard_map/dot_general | solution.py:48
  392.9 4.0 convert_add_fusion.7
  402.3 9.6 %collective-permute-done.27 = bf16[128,2048]{1,0:T(8,128)(2,1)S(1)} collective-permute-done((bf16[128,2048]{1,0:T(8,128)(2,1)S(1)}, bf16[128,2048]{1,0:T(8,128)(2,1)S(1)}, u32[]{:S(2)}, u32[]{:S(2)}) %collective-permute-start.27) | collective-permute-done | bytes 524320 | tf_op jit(solution)/shard_map/ppermute | solution.py:52
  413.6 8.9 %collective-permute-done.43 = bf16[128,2048]{1,0:T(8,128)(2,1)S(1)} collective-permute-done((bf16[128,2048]{1,0:T(8,128)(2,1)S(1)}, bf16[128,2048]{1,0:T(8,128)(2,1)S(1)}, u32[]{:S(2)}, u32[]{:S(2)}) %collective-permute-start.43) | collective-permute-done | bytes 524320 | tf_op jit(solution)/shard_map/ppermute | solution.py:52
  428.8 40.8 %collective-permute-done.44 = bf16[256,2048]{1,0:T(8,128)(2,1)S(1)} collective-permute-done((bf16[256,2048]{1,0:T(8,128)(2,1)S(1)}, bf16[256,2048]{1,0:T(8,128)(2,1)S(1)}, u32[]{:S(2)}, u32[]{:S(2)}) %collective-permute-start.44) | collective-permute-done | bytes 1048608 | tf_op jit(solution)/shard_map/ppermute | solution.py:52
  471.8 4.8 multiply_add_fusion
  480.9 13.0 %convolution_convert_fusion.5 = bf16[2048,1024]{1,0:T(8,128)(2,1)} fusion(bf16[2048,2048]{1,0:T(8,128)(2,1)} %bitcast.42, bf16[2048,1024]{0,1:T(8,128)(2,1)S(1)} %copy-done.64), kind=kOutput, calls=%fused_computation.12 | convolution fusion | flops 8592031744 | bytes 16777216 | tf_op jit(solution)/shard_map/dot_general | solution.py:44
  494.1 7.4 collective-permute-done.49
  507.6 6.5 collective-permute-done.53
  520.0 6.1 convolution_convert_fusion.8
  526.2 27.3 %attend_back.1 = (f32[8,2,128,256]{3,2,1,0:T(8,128)S(1)}, f32[8,2,128,64]{3,2,1,0:T(8,128)S(1)}, f32[8,2,128,64]{3,2,1,0:T(8,128)S(1)}) custom-call(s32[1]{0:T(128)} %bitcast.1.base_ref, s32[2]{0:T(128)S(1)} %copy-done.12, bf16[8,2,128,256]{3,2,1,0:T(8,128)(2,1)S(1)} %copy-done.6, bf16[8,2,128,64]{3,2,1,0:T(8,128)(2,1)S(1)} %bitcast.199, ...), custom_call_target="tpu_custom_call" | custom-call | flops 10737418240 | bytes 6291456 | tf_op jit(solution)/shard_map/attend_back/pallas_call | solution.py:273
  554.5 2.3 copy.82
  556.8 3.0 reshape_reshape.6
  561.4 2.4 copy.94
  563.8 2.3 copy.95
  575.9 5.9 convolution_convert_fusion.7
  581.8 3.5 convolution_convert_fusion.6
  587.3 24.4 %convolution_convert_fusion = bf16[2048,2048]{1,0:T(8,128)(2,1)} fusion(bf16[2048,2048]{1,0:T(8,128)(2,1)} %bitcast.27, bf16[2048,1024]{0,1:T(8,128)(2,1)} %get-tuple-element.50, bf16[2048,1024]{0,1:T(8,128)(2,1)} %get-tuple-element.49), kind=kOutput, calls=%fused_computation.6 | convolution fusion | flops 17200840704 | bytes 25165824 | tf_op jit(solution)/shard_map/dot_general | solution.py:44
  611.7 6.2 convolution_convert_fusion.1
  629.5 11.4 %collective-permute-done.59 = bf16[128,2048]{1,0:T(8,128)(2,1)S(1)} collective-permute-done((bf16[128,2048]{1,0:T(8,128)(2,1)S(1)}, bf16[128,2048]{1,0:T(8,128)(2,1)S(1)}, u32[]{:S(2)}, u32[]{:S(2)}) %collective-permute-start.59) | collective-permute-done | bytes 524320 | tf_op jit(solution)/shard_map/ppermute | solution.py:52
  643.1 3.6 all-to-all-start.5
  646.7 2.4 pad_maximum_fusion.14
  653.2 25.1 %all-to-all-done.5 = bf16[8,64,1024]{2,1,0:T(8,128)(2,1)S(1)} async-done(((bf16[8,64,1024]{2,1,0:T(8,128)(2,1)}), bf16[8,64,1024]{2,1,0:T(8,128)(2,1)S(1)}, u32[]{:S(2)}, u32[]{:S(2)}) %all-to-all-start.5) | async-done | bytes 1048608 | tf_op jit(solution)/shard_map/all_to_all | solution.py:98
  678.2 4.2 all-to-all-start.3
  683.7 2.9 multiply_reduce_fusion.2
  686.6 7.0 all-to-all-done.3
  693.6 90.0 %reduce-scatter.6.cloned.1.call-done = bf16[512,2048]{1,0:T(8,128)(2,1)} async-done(((bf16[2048,2048]{1,0:T(8,128)(2,1)}), bf16[512,2048]{1,0:T(8,128)(2,1)}) %reduce-scatter.6.cloned.1.call-update) | async-done | bytes 2097168 | tf_op jit(solution)/shard_map/reduce_scatter | solution.py:92
  783.6 4.5 all-to-all-start.4
  788.1 59.4 %all-reduce.4 = (f32[2048]{0:T(1024)}, f32[64]{0:T(128)}, f32[64]{0:T(128)}, f32[2048]{0:T(1024)}) all-reduce(f32[2048]{0:T(1024)S(1)} %get-tuple-element.33, f32[64]{0:T(128)S(1)} %get-tuple-element.37, f32[64]{0:T(128)S(1)} %get-tuple-element.35, f32[2048]{0:T(1024)S(1)} %get-tuple-element.31), channel_id=1, replica_groups=mesh['dp'=4,'ctx'=8] {'dp','ctx'}, use_global_device_ids=true, to_apply=%region_9.0 | all-reduce | flops 4224 | bytes 33792 | tf_op jit(solution)/shard_map/psum | solution.py:481
  847.5 4.5 add_convert_fusion
  (413 shorter events, 170.1 us)
Async XLA Ops:
  7.2 119.0 %all-gather.4.cloned.1.call-start = ((), (), s32[]{:S(2)}) async-start(), calls=%async_computation.9 | async-start | bytes 3276800 | tf_op jit(solution)/shard_map/all_gather | solution.py:88
  32.3 58.2 %all-to-all-start.1 = ((bf16[64,8,2048]{2,0,1:T(8,128)(2,1)}), bf16[64,8,2048]{2,0,1:T(8,128)(2,1)S(1)}, u32[]{:S(2)}, u32[]{:S(2)}) async-start(bf16[64,8,2048]{2,0,1:T(8,128)(2,1)} %copy.79), calls=%async_computation.1 | async-start | bytes 4194304 | tf_op jit(solution)/shard_map/all_to_all | solution.py:82
  36.0 267.8 %all-gather.6.cloned.1.call-start = ((), (), s32[]{:S(2)}) async-start(), calls=%async_computation.10 | async-start | bytes 10485760 | tf_op jit(solution)/shard_map/all_gather | solution.py:88
  37.5 54.4 %collective-permute-start = (bf16[256,2048]{1,0:T(8,128)(2,1)}, bf16[256,2048]{1,0:T(8,128)(2,1)}, u32[]{:S(2)}, u32[]{:S(2)}) collective-permute-start(bf16[256,2048]{1,0:T(8,128)(2,1)} %multiply_convert_fusion.4), channel_id=1, source_target_pairs={{0,1},{1,0},{2,3},{3,2},{4,5},{5,4},{6,7},{7,6},{8,9},{9,8},{10,11... | collective-permute-start | bytes 3145736 | tf_op jit(solution)/shard_map/ppermute | solution.py:52
  37.9 46.9 %collective-permute-start.1 = (bf16[256,2048]{1,0:T(8,128)(2,1)}, bf16[256,2048]{1,0:T(8,128)(2,1)}, u32[]{:S(2)}, u32[]{:S(2)}) collective-permute-start(bf16[256,2048]{1,0:T(8,128)(2,1)} %multiply_convert_fusion.4), channel_id=1, source_target_pairs={{0,2},{1,3},{2,0},{3,1},{4,6},{5,7},{6,4},{7,5},{8,10},{9,11},{10,... | collective-permute-start | bytes 3145736 | tf_op jit(solution)/shard_map/ppermute | solution.py:52
  39.5 48.5 %collective-permute-start.3 = (bf16[256,2048]{1,0:T(8,128)(2,1)}, bf16[256,2048]{1,0:T(8,128)(2,1)}, u32[]{:S(2)}, u32[]{:S(2)}) collective-permute-start(bf16[256,2048]{1,0:T(8,128)(2,1)} %multiply_convert_fusion.4), channel_id=1, source_target_pairs={{0,4},{1,5},{2,6},{3,7},{4,0},{5,1},{6,2},{7,3},{8,12},{9,13},{10,... | collective-permute-start | bytes 3145736 | tf_op jit(solution)/shard_map/ppermute | solution.py:52
  41.0 134.6 %collective-permute-start.33 = (bf16[256,2048]{1,0:T(8,128)(2,1)}, bf16[256,2048]{1,0:T(8,128)(2,1)}, u32[]{:S(2)}, u32[]{:S(2)}) collective-permute-start(bf16[256,2048]{1,0:T(8,128)(2,1)} %bitcast.33), channel_id=1, source_target_pairs={{0,2},{1,3},{2,0},{3,1},{4,6},{5,7},{6,4},{7,5},{8,10},{9,11},{10,... | collective-permute-start | bytes 3145736 | tf_op jit(solution)/shard_map/ppermute | solution.py:52
  41.6 147.9 %collective-permute-start.32 = (bf16[256,2048]{1,0:T(8,128)(2,1)}, bf16[256,2048]{1,0:T(8,128)(2,1)}, u32[]{:S(2)}, u32[]{:S(2)}) collective-permute-start(bf16[256,2048]{1,0:T(8,128)(2,1)} %bitcast.33), channel_id=1, source_target_pairs={{0,1},{1,0},{2,3},{3,2},{4,5},{5,4},{6,7},{7,6},{8,9},{9,8},{10,11... | collective-permute-start | bytes 3145736 | tf_op jit(solution)/shard_map/ppermute | solution.py:52
  86.6 13.3 %collective-permute-start.5 = (bf16[128,2048]{1,0:T(8,128)(2,1)}, bf16[128,2048]{1,0:T(8,128)(2,1)}, u32[]{:S(2)}, u32[]{:S(2)}) collective-permute-start(bf16[128,2048]{1,0:T(8,128)(2,1)} %slice.365), channel_id=1, source_target_pairs={{0,4},{1,5},{2,6},{3,7},{4,0},{5,1},{6,2},{7,3},{8,12},{9,13},{10,... | collective-permute-start | bytes 1572872 | tf_op jit(solution)/shard_map/ppermute | solution.py:52
  90.0 28.0 %collective-permute-start.6 = (bf16[128,2048]{1,0:T(8,128)(2,1)}, bf16[128,2048]{1,0:T(8,128)(2,1)}, u32[]{:S(2)}, u32[]{:S(2)}) collective-permute-start(bf16[128,2048]{1,0:T(8,128)(2,1)} %slice.366), channel_id=1, source_target_pairs={{0,2},{1,3},{2,0},{3,1},{4,6},{5,7},{6,4},{7,5},{8,10},{9,11},{10,... | collective-permute-start | bytes 1572872 | tf_op jit(solution)/shard_map/ppermute | solution.py:52
  91.9 27.2 %collective-permute-start.2 = (bf16[256,2048]{1,0:T(8,128)(2,1)}, bf16[256,2048]{1,0:T(8,128)(2,1)S(1)}, u32[]{:S(2)}, u32[]{:S(2)}) collective-permute-start(bf16[256,2048]{1,0:T(8,128)(2,1)} %collective-permute-done.1), channel_id=1, source_target_pairs={{0,1},{1,0},{2,3},{3,2},{4,5},{5,4},{6,7},{7,6},{8,9},{9,8},{10,11... | collective-permute-start | bytes 3145736 | tf_op jit(solution)/shard_map/ppermute | solution.py:52
  99.9 85.8 %collective-permute-start.35 = (bf16[256,2048]{1,0:T(8,128)(2,1)}, bf16[256,2048]{1,0:T(8,128)(2,1)}, u32[]{:S(2)}, u32[]{:S(2)}) collective-permute-start(bf16[256,2048]{1,0:T(8,128)(2,1)} %bitcast.33), channel_id=1, source_target_pairs={{0,4},{1,5},{2,6},{3,7},{4,0},{5,1},{6,2},{7,3},{8,12},{9,13},{10,... | collective-permute-start | bytes 3145736 | tf_op jit(solution)/shard_map/ppermute | solution.py:52
  175.2 18.1 %collective-permute-start.10 = (bf16[256,2048]{1,0:T(8,128)(2,1)}, bf16[256,2048]{1,0:T(8,128)(2,1)S(1)}, u32[]{:S(2)}, u32[]{:S(2)}) collective-permute-start(bf16[256,2048]{1,0:T(8,128)(2,1)} %get-tuple-element.75), channel_id=1, source_target_pairs={{0,1},{1,0},{2,3},{3,2},{4,5},{5,4},{6,7},{7,6},{8,9},{9,8},{10,11... | collective-permute-start | bytes 3145736 | tf_op jit(solution)/shard_map/ppermute | solution.py:52
  175.2 18.2 %collective-permute-start.13 = (bf16[256,2048]{1,0:T(8,128)(2,1)}, bf16[256,2048]{1,0:T(8,128)(2,1)}, u32[]{:S(2)}, u32[]{:S(2)}) collective-permute-start(bf16[256,2048]{1,0:T(8,128)(2,1)} %get-tuple-element.74), channel_id=1, source_target_pairs={{0,1},{1,0},{2,3},{3,2},{4,5},{5,4},{6,7},{7,6},{8,9},{9,8},{10,11... | collective-permute-start | bytes 3145736 | tf_op jit(solution)/shard_map/ppermute | solution.py:52
  175.7 18.6 %collective-permute-start.9 = (bf16[256,2048]{1,0:T(8,128)(2,1)}, bf16[256,2048]{1,0:T(8,128)(2,1)}, u32[]{:S(2)}, u32[]{:S(2)}) collective-permute-start(bf16[256,2048]{1,0:T(8,128)(2,1)} %get-tuple-element.76), channel_id=1, source_target_pairs={{0,1},{1,0},{2,3},{3,2},{4,5},{5,4},{6,7},{7,6},{8,9},{9,8},{10,11... | collective-permute-start | bytes 3145736 | tf_op jit(solution)/shard_map/ppermute | solution.py:52
  179.1 24.5 %all-to-all-start.2 = ((bf16[64,8,1024]{2,0,1:T(8,128)(2,1)}), bf16[64,8,1024]{2,0,1:T(8,128)(2,1)}, u32[]{:S(2)}, u32[]{:S(2)}) async-start(bf16[64,8,1024]{2,0,1:T(8,128)(2,1)} %bitcast.192), calls=%async_computation.2 | async-start | bytes 2097152 | tf_op jit(solution)/shard_map/all_to_all | solution.py:82
  183.4 144.7 %all-gather.8.cloned.1.call-start = ((), (), s32[]{:S(2)}) async-start(), calls=%async_computation.11 | async-start | bytes 5242880 | tf_op jit(solution)/shard_map/all_gather | solution.py:88
  185.7 23.8 %collective-permute-start.37 = (bf16[128,2048]{1,0:T(8,128)(2,1)}, bf16[128,2048]{1,0:T(8,128)(2,1)}, u32[]{:S(2)}, u32[]{:S(2)}) collective-permute-start(bf16[128,2048]{1,0:T(8,128)(2,1)} %slice.408), channel_id=1, source_target_pairs={{0,4},{1,5},{2,6},{3,7},{4,0},{5,1},{6,2},{7,3},{8,12},{9,13},{10,... | collective-permute-start | bytes 1572872 | tf_op jit(solution)/shard_map/ppermute | solution.py:52
  189.5 46.4 %collective-permute-start.38 = (bf16[128,2048]{1,0:T(8,128)(2,1)}, bf16[128,2048]{1,0:T(8,128)(2,1)}, u32[]{:S(2)}, u32[]{:S(2)}) collective-permute-start(bf16[128,2048]{1,0:T(8,128)(2,1)} %slice.409), channel_id=1, source_target_pairs={{0,2},{1,3},{2,0},{3,1},{4,6},{5,7},{6,4},{7,5},{8,10},{9,11},{10,... | collective-permute-start | bytes 1572872 | tf_op jit(solution)/shard_map/ppermute | solution.py:52
  193.3 44.1 %collective-permute-start.34 = (bf16[256,2048]{1,0:T(8,128)(2,1)}, bf16[256,2048]{1,0:T(8,128)(2,1)}, u32[]{:S(2)}, u32[]{:S(2)}) collective-permute-start(bf16[256,2048]{1,0:T(8,128)(2,1)} %collective-permute-done.33), channel_id=1, source_target_pairs={{0,1},{1,0},{2,3},{3,2},{4,5},{5,4},{6,7},{7,6},{8,9},{9,8},{10,11... | collective-permute-start | bytes 3145736 | tf_op jit(solution)/shard_map/ppermute | solution.py:52
  193.3 70.7 %collective-permute-start.36 = (bf16[256,2048]{1,0:T(8,128)(2,1)}, bf16[256,2048]{1,0:T(8,128)(2,1)}, u32[]{:S(2)}, u32[]{:S(2)}) collective-permute-start(bf16[256,2048]{1,0:T(8,128)(2,1)} %collective-permute-done.35), channel_id=1, source_target_pairs={{0,1},{1,0},{2,3},{3,2},{4,5},{5,4},{6,7},{7,6},{8,9},{9,8},{10,11... | collective-permute-start | bytes 3145736 | tf_op jit(solution)/shard_map/ppermute | solution.py:52
  200.8 19.5 %collective-permute-start.11 = (bf16[128,2048]{1,0:T(8,128)(2,1)}, bf16[128,2048]{1,0:T(8,128)(2,1)}, u32[]{:S(2)}, u32[]{:S(2)}) collective-permute-start(bf16[128,2048]{1,0:T(8,128)(2,1)} %get-tuple-element.102), channel_id=1, source_target_pairs={{0,4},{1,5},{2,6},{3,7},{4,0},{5,1},{6,2},{7,3},{8,12},{9,13},{10,... | collective-permute-start | bytes 1572872 | tf_op jit(solution)/shard_map/ppermute | solution.py:52
  203.7 439.4 %reduce-scatter.8.cloned.1.call-start = ((), (), s32[]{:S(2)}) async-start(), calls=%async_computation.14 | async-start | bytes 5242880 | tf_op jit(solution)/shard_map/reduce_scatter | solution.py:92
  210.6 31.5 %collective-permute-start.8 = (bf16[256,2048]{1,0:T(8,128)(2,1)}, bf16[256,2048]{1,0:T(8,128)(2,1)S(1)}, u32[]{:S(2)}, u32[]{:S(2)}) collective-permute-start(bf16[256,2048]{1,0:T(8,128)(2,1)} %get-tuple-element.73), channel_id=1, source_target_pairs={{0,1},{1,0},{2,3},{3,2},{4,5},{5,4},{6,7},{7,6},{8,9},{9,8},{10,11... | collective-permute-start | bytes 3145736 | tf_op jit(solution)/shard_map/ppermute | solution.py:52
  220.3 13.6 %collective-permute-start.14 = (bf16[128,2048]{1,0:T(8,128)(2,1)S(1)}, bf16[128,2048]{1,0:T(8,128)(2,1)S(1)}, u32[]{:S(2)}, u32[]{:S(2)}) collective-permute-start(bf16[128,2048]{1,0:T(8,128)(2,1)S(1)} %copy-done.44), channel_id=1, source_target_pairs={{0,2},{1,3},{2,0},{3,1},{4,6},{5,7},{6,4},{7,5},{8,10},{9,11},{10,... | collective-permute-start | bytes 1572872 | tf_op jit(solution)/shard_map/ppermute | solution.py:52
  233.9 24.4 %collective-permute-start.12 = (bf16[256,2048]{1,0:T(8,128)(2,1)S(1)}, bf16[256,2048]{1,0:T(8,128)(2,1)S(1)}, u32[]{:S(2)}, u32[]{:S(2)}) collective-permute-start(bf16[256,2048]{1,0:T(8,128)(2,1)S(1)} %pad_maximum_fusion.7), channel_id=1, source_target_pairs={{0,2},{1,3},{2,0},{3,1},{4,6},{5,7},{6,4},{7,5},{8,10},{9,11},{10,... | collective-permute-start | bytes 3145736 | tf_op jit(solution)/shard_map/ppermute | solution.py:52
  235.9 24.2 %collective-permute-start.15 = (bf16[256,2048]{1,0:T(8,128)(2,1)S(1)}, bf16[256,2048]{1,0:T(8,128)(2,1)S(1)}, u32[]{:S(2)}, u32[]{:S(2)}) collective-permute-start(bf16[256,2048]{1,0:T(8,128)(2,1)S(1)} %pad_maximum_fusion.8), channel_id=1, source_target_pairs={{0,4},{1,5},{2,6},{3,7},{4,0},{5,1},{6,2},{7,3},{8,12},{9,13},{10,... | collective-permute-start | bytes 3145736 | tf_op jit(solution)/shard_map/ppermute | solution.py:52
  237.4 30.1 %collective-permute-start.39 = (bf16[256,2048]{1,0:T(8,128)(2,1)S(1)}, bf16[256,2048]{1,0:T(8,128)(2,1)S(1)}, u32[]{:S(2)}, u32[]{:S(2)}) collective-permute-start(bf16[256,2048]{1,0:T(8,128)(2,1)S(1)} %constant_dynamic-update-slice_fusion.4), channel_id=1, source_target_pairs={{0,1},{1,0},{2,3},{3,2},{4,5},{5,4},{6,7},{7,6},{8,9},{9,8},{10,11... | collective-permute-start | bytes 3145736 | tf_op jit(solution)/shard_map/ppermute | solution.py:52
  263.4 23.3 %collective-permute-start.17 = (bf16[256,2048]{1,0:T(8,128)(2,1)S(1)}, bf16[256,2048]{1,0:T(8,128)(2,1)S(1)}, u32[]{:S(2)}, u32[]{:S(2)}) collective-permute-start(bf16[256,2048]{1,0:T(8,128)(2,1)S(1)} %get-tuple-element.46), channel_id=1, source_target_pairs={{0,2},{1,3},{2,0},{3,1},{4,6},{5,7},{6,4},{7,5},{8,10},{9,11},{10,... | collective-permute-start | bytes 3145736 | tf_op jit(solution)/shard_map/ppermute | solution.py:52
  263.7 23.5 %collective-permute-start.19 = (bf16[256,2048]{1,0:T(8,128)(2,1)S(1)}, bf16[256,2048]{1,0:T(8,128)(2,1)S(1)}, u32[]{:S(2)}, u32[]{:S(2)}) collective-permute-start(bf16[256,2048]{1,0:T(8,128)(2,1)S(1)} %get-tuple-element.46), channel_id=1, source_target_pairs={{0,4},{1,5},{2,6},{3,7},{4,0},{5,1},{6,2},{7,3},{8,12},{9,13},{10,... | collective-permute-start | bytes 3145736 | tf_op jit(solution)/shard_map/ppermute | solution.py:52
  264.1 26.3 %collective-permute-start.16 = (bf16[256,2048]{1,0:T(8,128)(2,1)S(1)}, bf16[256,2048]{1,0:T(8,128)(2,1)S(1)}, u32[]{:S(2)}, u32[]{:S(2)}) collective-permute-start(bf16[256,2048]{1,0:T(8,128)(2,1)S(1)} %get-tuple-element.46), channel_id=1, source_target_pairs={{0,1},{1,0},{2,3},{3,2},{4,5},{5,4},{6,7},{7,6},{8,9},{9,8},{10,11... | collective-permute-start | bytes 3145736 | tf_op jit(solution)/shard_map/ppermute | solution.py:52
  286.8 11.3 %collective-permute-start.21 = (bf16[128,2048]{1,0:T(8,128)(2,1)S(1)}, bf16[128,2048]{1,0:T(8,128)(2,1)S(1)}, u32[]{:S(2)}, u32[]{:S(2)}) collective-permute-start(bf16[128,2048]{1,0:T(8,128)(2,1)S(1)} %slice.390), channel_id=1, source_target_pairs={{0,4},{1,5},{2,6},{3,7},{4,0},{5,1},{6,2},{7,3},{8,12},{9,13},{10,... | collective-permute-start | bytes 1572872 | tf_op jit(solution)/shard_map/ppermute | solution.py:52
  287.2 11.0 %collective-permute-start.22 = (bf16[128,2048]{1,0:T(8,128)(2,1)S(1)}, bf16[128,2048]{1,0:T(8,128)(2,1)S(1)}, u32[]{:S(2)}, u32[]{:S(2)}) collective-permute-start(bf16[128,2048]{1,0:T(8,128)(2,1)S(1)} %slice.391), channel_id=1, source_target_pairs={{0,2},{1,3},{2,0},{3,1},{4,6},{5,7},{6,4},{7,5},{8,10},{9,11},{10,... | collective-permute-start | bytes 1572872 | tf_op jit(solution)/shard_map/ppermute | solution.py:52
  289.8 10.7 %collective-permute-start.20 = (bf16[256,2048]{1,0:T(8,128)(2,1)S(1)}, bf16[256,2048]{1,0:T(8,128)(2,1)S(1)}, u32[]{:S(2)}, u32[]{:S(2)}) collective-permute-start(bf16[256,2048]{1,0:T(8,128)(2,1)S(1)} %collective-permute-done.19), channel_id=1, source_target_pairs={{0,1},{1,0},{2,3},{3,2},{4,5},{5,4},{6,7},{7,6},{8,9},{9,8},{10,11... | collective-permute-start | bytes 3145736 | tf_op jit(solution)/shard_map/ppermute | solution.py:52
  367.0 24.5 %collective-permute-start.25 = (bf16[256,2048]{1,0:T(8,128)(2,1)}, bf16[256,2048]{1,0:T(8,128)(2,1)S(1)}, u32[]{:S(2)}, u32[]{:S(2)}) collective-permute-start(bf16[256,2048]{1,0:T(8,128)(2,1)} %get-tuple-element.69), channel_id=1, source_target_pairs={{0,1},{1,0},{2,3},{3,2},{4,5},{5,4},{6,7},{7,6},{8,9},{9,8},{10,11... | collective-permute-start | bytes 3145736 | tf_op jit(solution)/shard_map/ppermute | solution.py:52
  367.4 24.0 %collective-permute-start.26 = (bf16[256,2048]{1,0:T(8,128)(2,1)}, bf16[256,2048]{1,0:T(8,128)(2,1)S(1)}, u32[]{:S(2)}, u32[]{:S(2)}) collective-permute-start(bf16[256,2048]{1,0:T(8,128)(2,1)} %get-tuple-element.68), channel_id=1, source_target_pairs={{0,1},{1,0},{2,3},{3,2},{4,5},{5,4},{6,7},{7,6},{8,9},{9,8},{10,11... | collective-permute-start | bytes 3145736 | tf_op jit(solution)/shard_map/ppermute | solution.py:52
  367.5 24.5 %collective-permute-start.29 = (bf16[256,2048]{1,0:T(8,128)(2,1)}, bf16[256,2048]{1,0:T(8,128)(2,1)}, u32[]{:S(2)}, u32[]{:S(2)}) collective-permute-start(bf16[256,2048]{1,0:T(8,128)(2,1)} %get-tuple-element.67), channel_id=1, source_target_pairs={{0,1},{1,0},{2,3},{3,2},{4,5},{5,4},{6,7},{7,6},{8,9},{9,8},{10,11... | collective-permute-start | bytes 3145736 | tf_op jit(solution)/shard_map/ppermute | solution.py:52
  391.5 35.7 %collective-permute-start.40 = (bf16[256,2048]{1,0:T(8,128)(2,1)S(1)}, bf16[256,2048]{1,0:T(8,128)(2,1)S(1)}, u32[]{:S(2)}, u32[]{:S(2)}) collective-permute-start(bf16[256,2048]{1,0:T(8,128)(2,1)S(1)} %get-tuple-element.59), channel_id=1, source_target_pairs={{0,1},{1,0},{2,3},{3,2},{4,5},{5,4},{6,7},{7,6},{8,9},{9,8},{10,11... | collective-permute-start | bytes 3145736 | tf_op jit(solution)/shard_map/ppermute | solution.py:52
  392.7 77.9 %collective-permute-start.24 = (bf16[256,2048]{1,0:T(8,128)(2,1)S(1)}, bf16[256,2048]{1,0:T(8,128)(2,1)S(1)}, u32[]{:S(2)}, u32[]{:S(2)}) collective-permute-start(bf16[256,2048]{1,0:T(8,128)(2,1)S(1)} %get-tuple-element.66), channel_id=1, source_target_pairs={{0,1},{1,0},{2,3},{3,2},{4,5},{5,4},{6,7},{7,6},{8,9},{9,8},{10,11... | collective-permute-start | bytes 3145736 | tf_op jit(solution)/shard_map/ppermute | solution.py:52
  397.1 14.8 %collective-permute-start.27 = (bf16[128,2048]{1,0:T(8,128)(2,1)S(1)}, bf16[128,2048]{1,0:T(8,128)(2,1)S(1)}, u32[]{:S(2)}, u32[]{:S(2)}) collective-permute-start(bf16[128,2048]{1,0:T(8,128)(2,1)S(1)} %get-tuple-element.100), channel_id=1, source_target_pairs={{0,4},{1,5},{2,6},{3,7},{4,0},{5,1},{6,2},{7,3},{8,12},{9,13},{10,... | collective-permute-start | bytes 1572872 | tf_op jit(solution)/shard_map/ppermute | solution.py:52
  398.8 27.6 %collective-permute-start.30 = (bf16[128,2048]{1,0:T(8,128)(2,1)S(1)}, bf16[128,2048]{1,0:T(8,128)(2,1)S(1)}, u32[]{:S(2)}, u32[]{:S(2)}) collective-permute-start(bf16[128,2048]{1,0:T(8,128)(2,1)S(1)} %get-tuple-element.101), channel_id=1, source_target_pairs={{0,2},{1,3},{2,0},{3,1},{4,6},{5,7},{6,4},{7,5},{8,10},{9,11},{10,... | collective-permute-start | bytes 1572872 | tf_op jit(solution)/shard_map/ppermute | solution.py:52
  400.5 22.0 %collective-permute-start.43 = (bf16[128,2048]{1,0:T(8,128)(2,1)S(1)}, bf16[128,2048]{1,0:T(8,128)(2,1)S(1)}, u32[]{:S(2)}, u32[]{:S(2)}) collective-permute-start(bf16[128,2048]{1,0:T(8,128)(2,1)S(1)} %get-tuple-element.98), channel_id=1, source_target_pairs={{0,4},{1,5},{2,6},{3,7},{4,0},{5,1},{6,2},{7,3},{8,12},{9,13},{10,... | collective-permute-start | bytes 1572872 | tf_op jit(solution)/shard_map/ppermute | solution.py:52
  411.9 12.8 %collective-permute-start.46 = (bf16[128,2048]{1,0:T(8,128)(2,1)S(1)}, bf16[128,2048]{1,0:T(8,128)(2,1)S(1)}, u32[]{:S(2)}, u32[]{:S(2)}) collective-permute-start(bf16[128,2048]{1,0:T(8,128)(2,1)S(1)} %get-tuple-element.99), channel_id=1, source_target_pairs={{0,2},{1,3},{2,0},{3,1},{4,6},{5,7},{6,4},{7,5},{8,10},{9,11},{10,... | collective-permute-start | bytes 1572872 | tf_op jit(solution)/shard_map/ppermute | solution.py:52
  422.6 48.1 %collective-permute-start.28 = (bf16[256,2048]{1,0:T(8,128)(2,1)S(1)}, bf16[256,2048]{1,0:T(8,128)(2,1)S(1)}, u32[]{:S(2)}, u32[]{:S(2)}) collective-permute-start(bf16[256,2048]{1,0:T(8,128)(2,1)S(1)} %pad_maximum_fusion.9), channel_id=1, source_target_pairs={{0,2},{1,3},{2,0},{3,1},{4,6},{5,7},{6,4},{7,5},{8,10},{9,11},{10,... | collective-permute-start | bytes 3145736 | tf_op jit(solution)/shard_map/ppermute | solution.py:52
  424.7 44.9 %collective-permute-start.44 = (bf16[256,2048]{1,0:T(8,128)(2,1)S(1)}, bf16[256,2048]{1,0:T(8,128)(2,1)S(1)}, u32[]{:S(2)}, u32[]{:S(2)}) collective-permute-start(bf16[256,2048]{1,0:T(8,128)(2,1)S(1)} %pad_maximum_fusion.11), channel_id=1, source_target_pairs={{0,2},{1,3},{2,0},{3,1},{4,6},{5,7},{6,4},{7,5},{8,10},{9,11},{10,... | collective-permute-start | bytes 3145736 | tf_op jit(solution)/shard_map/ppermute | solution.py:52
  426.4 43.2 %collective-permute-start.47 = (bf16[256,2048]{1,0:T(8,128)(2,1)S(1)}, bf16[256,2048]{1,0:T(8,128)(2,1)S(1)}, u32[]{:S(2)}, u32[]{:S(2)}) collective-permute-start(bf16[256,2048]{1,0:T(8,128)(2,1)S(1)} %pad_maximum_fusion.12), channel_id=1, source_target_pairs={{0,4},{1,5},{2,6},{3,7},{4,0},{5,1},{6,2},{7,3},{8,12},{9,13},{10,... | collective-permute-start | bytes 3145736 | tf_op jit(solution)/shard_map/ppermute | solution.py:52
  427.2 44.6 %collective-permute-start.31 = (bf16[256,2048]{1,0:T(8,128)(2,1)S(1)}, bf16[256,2048]{1,0:T(8,128)(2,1)S(1)}, u32[]{:S(2)}, u32[]{:S(2)}) collective-permute-start(bf16[256,2048]{1,0:T(8,128)(2,1)S(1)} %pad_maximum_fusion.10), channel_id=1, source_target_pairs={{0,4},{1,5},{2,6},{3,7},{4,0},{5,1},{6,2},{7,3},{8,12},{9,13},{10,... | collective-permute-start | bytes 3145736 | tf_op jit(solution)/shard_map/ppermute | solution.py:52
  478.7 22.8 %collective-permute-start.49 = (bf16[256,2048]{1,0:T(8,128)(2,1)}, bf16[256,2048]{1,0:T(8,128)(2,1)S(1)}, u32[]{:S(2)}, u32[]{:S(2)}) collective-permute-start(bf16[256,2048]{1,0:T(8,128)(2,1)} %get-tuple-element.44), channel_id=1, source_target_pairs={{0,2},{1,3},{2,0},{3,1},{4,6},{5,7},{6,4},{7,5},{8,10},{9,11},{10,... | collective-permute-start | bytes 3145736 | tf_op jit(solution)/shard_map/ppermute | solution.py:52
  480.2 24.0 %collective-permute-start.51 = (bf16[256,2048]{1,0:T(8,128)(2,1)}, bf16[256,2048]{1,0:T(8,128)(2,1)S(1)}, u32[]{:S(2)}, u32[]{:S(2)}) collective-permute-start(bf16[256,2048]{1,0:T(8,128)(2,1)} %get-tuple-element.44), channel_id=1, source_target_pairs={{0,4},{1,5},{2,6},{3,7},{4,0},{5,1},{6,2},{7,3},{8,12},{9,13},{10,... | collective-permute-start | bytes 3145736 | tf_op jit(solution)/shard_map/ppermute | solution.py:52
  480.9 24.6 %collective-permute-start.48 = (bf16[256,2048]{1,0:T(8,128)(2,1)}, bf16[256,2048]{1,0:T(8,128)(2,1)S(1)}, u32[]{:S(2)}, u32[]{:S(2)}) collective-permute-start(bf16[256,2048]{1,0:T(8,128)(2,1)} %get-tuple-element.44), channel_id=1, source_target_pairs={{0,1},{1,0},{2,3},{3,2},{4,5},{5,4},{6,7},{7,6},{8,9},{9,8},{10,11... | collective-permute-start | bytes 3145736 | tf_op jit(solution)/shard_map/ppermute | solution.py:52
  494.0 157.0 %reduce-scatter.4.cloned.1.call-start = ((), (), s32[]{:S(2)}) async-start(), calls=%async_computation.12 | async-start | bytes 3276800 | tf_op jit(solution)/shard_map/reduce_scatter | solution.py:92
  501.6 12.6 %collective-permute-start.53 = (bf16[128,2048]{1,0:T(8,128)(2,1)S(1)}, bf16[128,2048]{1,0:T(8,128)(2,1)S(1)}, u32[]{:S(2)}, u32[]{:S(2)}) collective-permute-start(bf16[128,2048]{1,0:T(8,128)(2,1)S(1)} %slice.424), channel_id=1, source_target_pairs={{0,4},{1,5},{2,6},{3,7},{4,0},{5,1},{6,2},{7,3},{8,12},{9,13},{10,... | collective-permute-start | bytes 1572872 | tf_op jit(solution)/shard_map/ppermute | solution.py:52
  504.2 10.2 %collective-permute-start.54 = (bf16[128,2048]{1,0:T(8,128)(2,1)S(1)}, bf16[128,2048]{1,0:T(8,128)(2,1)S(1)}, u32[]{:S(2)}, u32[]{:S(2)}) collective-permute-start(bf16[128,2048]{1,0:T(8,128)(2,1)S(1)} %slice.425), channel_id=1, source_target_pairs={{0,2},{1,3},{2,0},{3,1},{4,6},{5,7},{6,4},{7,5},{8,10},{9,11},{10,... | collective-permute-start | bytes 1572872 | tf_op jit(solution)/shard_map/ppermute | solution.py:52
  505.0 9.5 %collective-permute-start.50 = (bf16[256,2048]{1,0:T(8,128)(2,1)S(1)}, bf16[256,2048]{1,0:T(8,128)(2,1)S(1)}, u32[]{:S(2)}, u32[]{:S(2)}) collective-permute-start(bf16[256,2048]{1,0:T(8,128)(2,1)S(1)} %collective-permute-done.49), channel_id=1, source_target_pairs={{0,1},{1,0},{2,3},{3,2},{4,5},{5,4},{6,7},{7,6},{8,9},{9,8},{10,11... | collective-permute-start | bytes 3145736 | tf_op jit(solution)/shard_map/ppermute | solution.py:52
  505.0 11.7 %collective-permute-start.52 = (bf16[256,2048]{1,0:T(8,128)(2,1)S(1)}, bf16[256,2048]{1,0:T(8,128)(2,1)S(1)}, u32[]{:S(2)}, u32[]{:S(2)}) collective-permute-start(bf16[256,2048]{1,0:T(8,128)(2,1)S(1)} %collective-permute-done.51), channel_id=1, source_target_pairs={{0,1},{1,0},{2,3},{3,2},{4,5},{5,4},{6,7},{7,6},{8,9},{9,8},{10,11... | collective-permute-start | bytes 3145736 | tf_op jit(solution)/shard_map/ppermute | solution.py:52
  587.2 196.3 %reduce-scatter.6.cloned.1.call-start = ((), (), s32[]{:S(2)}) async-start(), calls=%async_computation.13 | async-start | bytes 10485760 | tf_op jit(solution)/shard_map/reduce_scatter | solution.py:92
  626.7 14.3 %collective-permute-start.59 = (bf16[128,2048]{1,0:T(8,128)(2,1)S(1)}, bf16[128,2048]{1,0:T(8,128)(2,1)S(1)}, u32[]{:S(2)}, u32[]{:S(2)}) collective-permute-start(bf16[128,2048]{1,0:T(8,128)(2,1)S(1)} %get-tuple-element.92), channel_id=1, source_target_pairs={{0,4},{1,5},{2,6},{3,7},{4,0},{5,1},{6,2},{7,3},{8,12},{9,13},{10,... | collective-permute-start | bytes 1572872 | tf_op jit(solution)/shard_map/ppermute | solution.py:52
  626.7 55.7 %collective-permute-start.56 = (bf16[256,2048]{1,0:T(8,128)(2,1)}, bf16[256,2048]{1,0:T(8,128)(2,1)S(1)}, u32[]{:S(2)}, u32[]{:S(2)}) collective-permute-start(bf16[256,2048]{1,0:T(8,128)(2,1)} %get-tuple-element.52), channel_id=1, source_target_pairs={{0,1},{1,0},{2,3},{3,2},{4,5},{5,4},{6,7},{7,6},{8,9},{9,8},{10,11... | collective-permute-start | bytes 3145736 | tf_op jit(solution)/shard_map/ppermute | solution.py:52
  627.2 14.9 %collective-permute-start.62 = (bf16[128,2048]{1,0:T(8,128)(2,1)S(1)}, bf16[128,2048]{1,0:T(8,128)(2,1)S(1)}, u32[]{:S(2)}, u32[]{:S(2)}) collective-permute-start(bf16[128,2048]{1,0:T(8,128)(2,1)S(1)} %get-tuple-element.93), channel_id=1, source_target_pairs={{0,2},{1,3},{2,0},{3,1},{4,6},{5,7},{6,4},{7,5},{8,10},{9,11},{10,... | collective-permute-start | bytes 1572872 | tf_op jit(solution)/shard_map/ppermute | solution.py:52
  642.1 40.3 %collective-permute-start.60 = (bf16[256,2048]{1,0:T(8,128)(2,1)}, bf16[256,2048]{1,0:T(8,128)(2,1)}, u32[]{:S(2)}, u32[]{:S(2)}) collective-permute-start(bf16[256,2048]{1,0:T(8,128)(2,1)} %pad_maximum_fusion.13), channel_id=1, source_target_pairs={{0,2},{1,3},{2,0},{3,1},{4,6},{5,7},{6,4},{7,5},{8,10},{9,11},{10,... | collective-permute-start | bytes 3145736 | tf_op jit(solution)/shard_map/ppermute | solution.py:52
  643.1 35.1 %all-to-all-start.5 = ((bf16[8,64,1024]{2,1,0:T(8,128)(2,1)}), bf16[8,64,1024]{2,1,0:T(8,128)(2,1)S(1)}, u32[]{:S(2)}, u32[]{:S(2)}) async-start(bf16[8,64,1024]{2,1,0:T(8,128)(2,1)} %bitcast.219), calls=%async_computation.8 | async-start | bytes 2097152 | tf_op jit(solution)/shard_map/all_to_all | solution.py:98
  649.1 34.6 %collective-permute-start.63 = (bf16[256,2048]{1,0:T(8,128)(2,1)}, bf16[256,2048]{1,0:T(8,128)(2,1)}, u32[]{:S(2)}, u32[]{:S(2)}) collective-permute-start(bf16[256,2048]{1,0:T(8,128)(2,1)} %pad_maximum_fusion.14), channel_id=1, source_target_pairs={{0,4},{1,5},{2,6},{3,7},{4,0},{5,1},{6,2},{7,3},{8,12},{9,13},{10,... | collective-permute-start | bytes 3145736 | tf_op jit(solution)/shard_map/ppermute | solution.py:52
  678.2 15.4 %all-to-all-start.3 = ((bf16[8,64,640]{2,1,0:T(8,128)(2,1)}), bf16[8,64,640]{2,1,0:T(8,128)(2,1)}, u32[]{:S(2)}, u32[]{:S(2)}) async-start(bf16[8,64,640]{2,1,0:T(8,128)(2,1)} %bitcast.209), calls=%async_computation.4 | async-start | bytes 1310720 | tf_op jit(solution)/shard_map/all_to_all | solution.py:98
  783.6 75.1 %all-to-all-start.4 = ((bf16[8,64,2048]{2,1,0:T(8,128)(2,1)}), bf16[8,64,2048]{2,1,0:T(8,128)(2,1)}, u32[]{:S(2)}, u32[]{:S(2)}) async-start(bf16[8,64,2048]{2,1,0:T(8,128)(2,1)} %bitcast.211), calls=%async_computation.6 | async-start | bytes 4194304 | tf_op jit(solution)/shard_map/all_to_all | solution.py:98
  (79 other events, 867.2 us)
Sparse Core Ops, SparseCore 0:
  28.0 54.1 all-gather.3
  92.0 149.8 all-gather.5
  243.5 78.9 all-gather.7
  494.1 74.4 reduce-scatter.7
  587.3 49.6 reduce-scatter.3
  639.4 144.1 reduce-scatter.5

commit v2 on v1

v2 whole, which is shorter than its diff:
```python
import functools

import jax
import jax.numpy as jnp
from jax import lax
from jax.experimental import pallas as pl
from jax.experimental.pallas import tpu as pltpu
from jax.sharding import PartitionSpec as P

QUERY_HEADS_TOTAL = 32
KEY_VALUE_HEADS = 8
HEAD_SIZE = 64
FACTOR = HEAD_SIZE ** (-0.5)

NO_COST = pl.CostEstimate(flops=0, bytes_accessed=0, transcendentals=0)


epsilon = 1e-06
f32 = jnp.float32
bf16 = jnp.bfloat16


def rms_scale(value_rows):
    return lax.rsqrt(jnp.mean(value_rows * value_rows, axis=-1, keepdims=True) + epsilon)


def rotary_tables(positions, width):
    inverse = 10000.0 ** (-(jnp.arange(width // 2, dtype=f32) * 2.0) / width)
    angle_table = positions.astype(f32)[:, None] * inverse[None, :]
    return (jnp.cos(angle_table), jnp.sin(angle_table))


def dot_nn(left, right):
    return jnp.dot(left, right, preferred_element_type=f32)


def dot_tn(left, right):
    return lax.dot_general(left, right, (((0,), (0,)), ((), ())), preferred_element_type=f32)


def dot_nt(left, right):
    return lax.dot_general(left, right, (((1,), (1,)), ((), ())), preferred_element_type=f32)


def fence(values, *earlier):
    count = len(values)
    anywhere = pl.BlockSpec(memory_space=pl.ANY)
    return pl.pallas_call(
        lambda *refs: None,
        in_specs=[anywhere] * (count + len(earlier)),
        out_specs=[anywhere] * count,
        out_shape=[jax.ShapeDtypeStruct(v.shape, v.dtype) for v in values],
        input_output_aliases={i: i for i in range(count)},
        cost_estimate=NO_COST,
        name="fence",
    )(*values, *earlier)


def after(value, *earlier):
    return fence((value,), *earlier)[0]


RELATIVE = (0, 2, 4, 1, 3, 5, 6, 7)


def place_of(own, index, parts):
    if parts != 8:
        return index
    relative = lax.bitwise_xor(own, index)
    near = lax.shift_right_logical(relative, 1) + 3 * lax.bitwise_and(relative, 1)
    return jnp.where(relative < 6, near, relative)


def hop(value, bit):
    return lax.ppermute(value, "ctx", [(i, i ^ bit) for i in range(lax.axis_size("ctx"))])


def gather_tokens(value):
    return gather_tokens_and_start(value)[0]


def gather_tokens_and_start(value):
    if lax.axis_size("ctx") != 8:
        whole = lax.all_gather(value, "ctx", axis=0)
        return whole, (whole, whole)
    half = value.shape[0] // 2
    by_x, by_y = hop(value, 2), hop(value, 4)
    far = jnp.concatenate([hop(by_x[:half], 4), hop(by_y[half:], 2)], axis=0)
    whole = jnp.stack(
        [value, by_x, by_y, hop(value, 1), hop(by_x, 1), hop(by_y, 1), far, hop(far, 1)], axis=0
    )
    return whole, (by_x, by_y)


def partial_products(product, tokens):
    parts = lax.axis_size("ctx")
    if parts != 8:
        return product(0, parts, [(parts * tokens, bf16)], None, ())
    half = (tokens // 2, bf16)
    (far_other,) = product(7, 1, [(tokens, bf16)], None, ())
    far = product(6, 1, [half] * 2, hop(far_other, 1), ())
    (near_other,) = product(3, 3, [(3 * tokens, bf16)], None, (far[0],))
    own, *near = product(0, 3, [(tokens, f32)] + [half] * 4, hop(near_other, 1), ())
    return (own, *near, *far)


def finish_scatter(sums, tokens):
    if lax.axis_size("ctx") != 8:
        (whole,) = sums
        return lax.psum_scatter(whole, "ctx", scatter_dimension=0, tiled=True).astype(f32)
    own, x_first, x_last, y_first, y_last, far_first, far_last = sums
    from_x, from_y = hop(far_first, 2), hop(far_last, 4)
    x_last = (x_last.astype(f32) + from_y.astype(f32)).astype(bf16)
    y_first = (y_first.astype(f32) + from_x.astype(f32)).astype(bf16)
    x_part = jnp.concatenate([hop(x_first, 2), hop(x_last, 2)], axis=0)
    y_part = jnp.concatenate([hop(y_first, 4), hop(y_last, 4)], axis=0)
    return own + x_part.astype(f32) + y_part.astype(f32)


def sum_everywhere(value):
    if lax.axis_size("ctx") != 8 or lax.axis_size("dp") != 4:
        return lax.psum(value, ("dp", "ctx"))
    for bit in (1, 2, 4):
        value = value + hop(value, bit)
    for bit in (1, 2):
        value = value + lax.ppermute(value, "dp", [(i, i ^ bit) for i in range(4)])
    return value


def spread_columns(packed):
    rows, parts, columns = packed.shape
    return lax.all_to_all(
        packed.reshape(rows, parts * columns), "ctx", split_axis=1, concat_axis=0, tiled=True
    )


def gather_rows(block):
    return lax.all_gather(block, "dp", axis=0, tiled=True)


def scatter_rows(gradient):
    return lax.psum_scatter(gradient, "dp", scatter_dimension=0, tiled=True)


def collect_columns(block):
    parts = lax.axis_size("ctx")
    columns = block.shape[1]
    out = lax.all_to_all(block, "ctx", split_axis=0, concat_axis=1, tiled=True)
    return out.reshape(out.shape[0], parts, columns).astype(f32)


def collect_early(gradient):
    groups, parts = lax.axis_size("dp"), lax.axis_size("ctx")
    block = gradient.reshape(groups, parts, -1, gradient.shape[1])
    block = lax.all_to_all(block, "ctx", split_axis=1, concat_axis=1, tiled=True)
    return block.reshape(-1, gradient.shape[1])


def heads_to_columns(block, heads):
    return jnp.concatenate(
        [block[:, h * HEAD_SIZE : (h + 1) * HEAD_SIZE].T for h in range(heads)], axis=1
    )


def columns_to_heads(columns, heads, slots):
    return jnp.concatenate(
        [columns[:, h * slots : (h + 1) * slots].T for h in range(heads)], axis=1
    )


def columns_to_rows(columns, heads, slots):
    return jnp.concatenate(
        [columns[:, h * slots : (h + 1) * slots].T for h in range(heads)], axis=0
    )


def head_scale(raw):
    return lax.rsqrt(jnp.mean(raw * raw, axis=0, keepdims=True) + epsilon)


def prepare(raw, gain, cosine, sine):
    value = raw * head_scale(raw) * gain
    first, second = value[: HEAD_SIZE // 2], value[HEAD_SIZE // 2 :]
    return jnp.concatenate(
        [first * cosine - second * sine, second * cosine + first * sine], axis=0
    )


def prepare_back(gradient, raw, gain, cosine, sine):
    scale = head_scale(raw)
    unit = raw * scale
    first, second = gradient[: HEAD_SIZE // 2], gradient[HEAD_SIZE // 2 :]
    turned = jnp.concatenate(
        [first * cosine + second * sine, second * cosine - first * sine], axis=0
    )
    inside = turned * gain
    middle = jnp.mean(inside * unit, axis=0, keepdims=True)
    return scale * (inside - unit * middle), turned * unit


def fold(values):
    lanes = 128
    return sum(values[:, i : i + lanes] for i in range(0, values.shape[1], lanes))


def repeated(table, heads):
    return jnp.concatenate([table] * heads, axis=1)


def masked_scores(key_block, query_columns, start, query_block, slots, length):
    scores = dot_nn(key_block, query_columns)
    key_pos = start + lax.broadcasted_iota(jnp.int32, scores.shape, 0)
    query_pos = query_block * slots + lax.rem(
        lax.broadcasted_iota(jnp.int32, scores.shape, 1), slots
    )
    return jnp.where((key_pos <= query_pos) & (key_pos < length), scores, -1e30)


def chunks_needed(query_block, slots, length, chunk):
    return lax.div(
        jnp.minimum((query_block + 1) * slots, length) + (chunk - 1), jnp.int32(chunk)
    )


def attend_kernel(
    blocks, slots, heads, chunk,
    base_ref, len_ref, q_ref, kv_ref, qg_ref, kg_ref, cos_ref, sin_ref,
    o_ref, lse_ref, k_all, v_t,
):
    row, query_block = pl.program_id(0), pl.program_id(1)
    base, length = base_ref[0], len_ref[row]

    @pl.when(query_block == 0)
    def _():
        for j in range(blocks):
            at = place_of(base, jnp.int32(j), blocks)
            here = slice(j * slots, (j + 1) * slots)
            both = kv_ref[at, 0].T
            keys = prepare(both[:HEAD_SIZE], kg_ref[...], cos_ref[:, here], sin_ref[:, here])
            k_all[here, :] = keys.T.astype(bf16)
            v_t[:, here] = both[HEAD_SIZE:].astype(bf16)

    count = chunks_needed(query_block, slots, length, chunk)
    here = pl.ds(pl.multiple_of(query_block * slots, slots), slots)
    queries = prepare(
        heads_to_columns(q_ref[0, 0], heads),
        qg_ref[...],
        repeated(cos_ref[:, here], heads),
        repeated(sin_ref[:, here], heads),
    )
    queries = queries.astype(bf16) * FACTOR
    columns = heads * slots

    def step(j, carry):
        top, total, accum = carry
        start = pl.multiple_of(j * chunk, chunk)
        scores = masked_scores(
            k_all[pl.ds(start, chunk), :], queries, start, query_block, slots, length
        )
        new_top = jnp.maximum(top, jnp.max(scores, axis=0, keepdims=True))
        probs = jnp.exp(scores - new_top)
        alpha = jnp.exp(top - new_top)
        total = total * alpha + jnp.sum(probs, axis=0, keepdims=True)
        accum = accum * alpha + dot_nn(v_t[:, pl.ds(start, chunk)], probs.astype(bf16))
        return new_top, total, accum

    top, total, accum = lax.fori_loop(
        0,
        count,
        step,
        (
            jnp.full((1, columns), -1e30, f32),
            jnp.zeros((1, columns), f32),
            jnp.zeros((HEAD_SIZE, columns), f32),
        ),
    )
    o_ref[0, 0] = columns_to_heads(accum / total, heads, slots).astype(bf16)
    lse_ref[0, 0] = top + jnp.log(total)


def attend_back_kernel(
    blocks, slots, heads, chunk,
    base_ref, len_ref, q_ref, kv_ref, qg_ref, kg_ref, cos_ref, sin_ref, o_ref, do_ref, lse_ref,
    dq_ref, dkv_ref, dqg_ref, dkg_ref, k_all, v_all, k_t, dk_all, dv_all,
):
    row, query_block = pl.program_id(0), pl.program_id(1)
    base, length = base_ref[0], len_ref[row]

    @pl.when((row == 0) & (query_block == 0))
    def _():
        dqg_ref[...] = jnp.zeros_like(dqg_ref)
        dkg_ref[...] = jnp.zeros_like(dkg_ref)

    @pl.when(query_block == 0)
    def _():
        for j in range(blocks):
            at = place_of(base, jnp.int32(j), blocks)
            here = slice(j * slots, (j + 1) * slots)
            both = kv_ref[at, 0]
            keys = prepare(both.T[:HEAD_SIZE], kg_ref[...], cos_ref[:, here], sin_ref[:, here])
            k_t[:, here] = keys.astype(bf16)
            k_all[here, :] = keys.T.astype(bf16)
            v_all[here, :] = both[:, HEAD_SIZE:].astype(bf16)
        dk_all[...] = jnp.zeros_like(dk_all)
        dv_all[...] = jnp.zeros_like(dv_all)

    count = chunks_needed(query_block, slots, length, chunk)
    here = pl.ds(pl.multiple_of(query_block * slots, slots), slots)
    cosine, sine = repeated(cos_ref[:, here], heads), repeated(sin_ref[:, here], heads)
    raw = heads_to_columns(q_ref[0, 0], heads)
    queries = prepare(raw, qg_ref[...], cosine, sine).astype(bf16) * FACTOR
    query_rows = columns_to_rows(queries.astype(f32), heads, slots).astype(bf16)
    gradient = heads_to_columns(do_ref[0, 0].astype(f32), heads)
    grad_rows = columns_to_rows(gradient, heads, slots).astype(bf16)
    delta = jnp.sum(
        gradient * heads_to_columns(o_ref[0, 0].astype(f32), heads), axis=0, keepdims=True
    )
    gradient = gradient.astype(bf16)
    log_total = lse_ref[0, 0]

    def step(j, dq_t):
        start = pl.multiple_of(j * chunk, chunk)
        at = pl.ds(start, chunk)
        scores = masked_scores(k_all[at, :], queries, start, query_block, slots, length)
        probs = jnp.exp(scores - log_total)
        grad_probs = dot_nn(v_all[at, :], gradient)
        grad_scores = (probs * (grad_probs - delta)).astype(bf16)
        dv_all[at, :] += dot_nn(probs.astype(bf16), grad_rows)
        dk_all[at, :] += dot_nn(grad_scores, query_rows)
        return dq_t + dot_nn(k_t[:, at], grad_scores)

    dq_t = lax.fori_loop(0, count, step, jnp.zeros((HEAD_SIZE, heads * slots), f32))
    raw_term, gain_term = prepare_back(dq_t * FACTOR, raw, qg_ref[...], cosine, sine)
    dq_ref[0, 0] = columns_to_heads(raw_term, heads, slots).astype(bf16)
    dqg_ref[...] += fold(gain_term)

    @pl.when(query_block == blocks - 1)
    def _():
        for j in range(blocks):
            at = place_of(base, jnp.int32(j), blocks)
            here = slice(j * slots, (j + 1) * slots)
            raw_term, gain_term = prepare_back(
                dk_all[here, :].T,
                kv_ref[at, 0].T[:HEAD_SIZE],
                kg_ref[...],
                cos_ref[:, here],
                sin_ref[:, here],
            )
            dkg_ref[...] += fold(gain_term)
            dkv_ref[at, 0] = jnp.concatenate([raw_term.T, dv_all[here, :]], axis=1).astype(bf16)


def attention_specs(blocks, slots, width, total):
    own = lambda r, i, base, lens: (place_of(base[0], i, blocks), r, 0, 0)
    constant = lambda r, i, base, lens: (0, 0)
    both = 2 * HEAD_SIZE
    return (
        pl.BlockSpec((1, 1, slots, width), own),
        pl.BlockSpec((blocks, 1, slots, both), lambda r, i, base, lens: (0, r, 0, width // both)),
        pl.BlockSpec((blocks, 1, slots, both), lambda r, i, base, lens: (0, r, 0, 0)),
        pl.BlockSpec((HEAD_SIZE, 1), constant),
        pl.BlockSpec((HEAD_SIZE // 2, total), constant),
        pl.BlockSpec((1, 1, 1, width // HEAD_SIZE * slots), own),
        pl.BlockSpec((HEAD_SIZE, 128), constant),
    )


def attend(base, lengths, raw, query_gain, key_gain, cosine, sine):
    blocks, rows, slots, columns = raw.shape
    width = columns - 2 * HEAD_SIZE
    heads = width // HEAD_SIZE
    total = blocks * slots
    query_spec, raw_key_spec, _, gain_spec, table_spec, lse_spec, _ = attention_specs(
        blocks, slots, width, total
    )
    return pl.pallas_call(
        functools.partial(attend_kernel, blocks, slots, heads, 2 * slots),
        grid_spec=pltpu.PrefetchScalarGridSpec(
            num_scalar_prefetch=2,
            grid=(rows, blocks),
            in_specs=[query_spec, raw_key_spec, gain_spec, gain_spec, table_spec, table_spec],
            out_specs=[query_spec, lse_spec],
            scratch_shapes=[
                pltpu.VMEM((total, HEAD_SIZE), bf16),
                pltpu.VMEM((HEAD_SIZE, total), bf16),
            ],
        ),
        out_shape=[
            jax.ShapeDtypeStruct((blocks, rows, slots, width), bf16),
            jax.ShapeDtypeStruct((blocks, rows, 1, heads * slots), f32),
        ],
        compiler_params=pltpu.CompilerParams(vmem_limit_bytes=32 * 2**20),
        cost_estimate=NO_COST,
        name="attend",
    )(base, lengths, raw, raw, query_gain, key_gain, cosine, sine)


def attend_back(
    base, lengths, raw, query_gain, key_gain, cosine, sine, attended, gradient, log_total
):
    blocks, rows, slots, columns = raw.shape
    width = columns - 2 * HEAD_SIZE
    heads = width // HEAD_SIZE
    total = blocks * slots
    query_spec, raw_key_spec, key_spec, gain_spec, table_spec, lse_spec, sum_spec = (
        attention_specs(blocks, slots, width, total)
    )
    return pl.pallas_call(
        functools.partial(attend_back_kernel, blocks, slots, heads, 2 * slots),
        grid_spec=pltpu.PrefetchScalarGridSpec(
            num_scalar_prefetch=2,
            grid=(rows, blocks),
            in_specs=[query_spec, raw_key_spec, gain_spec, gain_spec, table_spec, table_spec]
            + [query_spec, query_spec, lse_spec],
            out_specs=[query_spec, key_spec, sum_spec, sum_spec],
            scratch_shapes=[
                pltpu.VMEM((total, HEAD_SIZE), bf16),
                pltpu.VMEM((total, HEAD_SIZE), bf16),
                pltpu.VMEM((HEAD_SIZE, total), bf16),
                pltpu.VMEM((total, HEAD_SIZE), f32),
                pltpu.VMEM((total, HEAD_SIZE), f32),
            ],
        ),
        out_shape=[
            jax.ShapeDtypeStruct((blocks, rows, slots, width), bf16),
            jax.ShapeDtypeStruct((blocks, rows, slots, 2 * HEAD_SIZE), bf16),
            jax.ShapeDtypeStruct((HEAD_SIZE, 128), f32),
            jax.ShapeDtypeStruct((HEAD_SIZE, 128), f32),
        ],
        compiler_params=pltpu.CompilerParams(vmem_limit_bytes=32 * 2**20),
        cost_estimate=NO_COST,
        name="attend_back",
    )(base, lengths, raw, raw, query_gain, key_gain, cosine, sine, attended, gradient, log_total)


def feed_kernel(hidden_ref, cotangent_ref, weight_ref, inner_ref, grad_ref):
    units = inner_ref.shape[1]
    hidden = hidden_ref[...]
    gate = dot_nn(hidden, weight_ref[:, :units])
    upward = dot_nn(hidden, weight_ref[:, units : 2 * units])
    grad_inner = dot_nn(cotangent_ref[...], weight_ref[:, 2 * units :])
    sigmoid_gate = jax.nn.sigmoid(gate)
    silu_gate = gate * sigmoid_gate
    inner_ref[...] = (silu_gate * upward).astype(bf16)
    grad_ref[:, :units] = (
        grad_inner * upward * sigmoid_gate * (1.0 + gate * (1.0 - sigmoid_gate))
    ).astype(bf16)
    grad_ref[:, units:] = (grad_inner * silu_gate).astype(bf16)


def feed_forward(hidden, cotangents, weights):
    count, width = hidden.shape
    units = weights.shape[1] // 3
    tile = 512
    rows = pl.BlockSpec((tile, width), lambda i: (i, 0))
    return pl.pallas_call(
        feed_kernel,
        grid=(count // tile,),
        in_specs=[rows, rows, pl.BlockSpec(weights.shape, lambda i: (0, 0))],
        out_specs=[
            pl.BlockSpec((tile, units), lambda i: (i, 0)),
            pl.BlockSpec((tile, 2 * units), lambda i: (i, 0)),
        ],
        out_shape=[
            jax.ShapeDtypeStruct((count, units), bf16),
            jax.ShapeDtypeStruct((count, 2 * units), bf16),
        ],
        compiler_params=pltpu.CompilerParams(vmem_limit_bytes=48 * 2**20),
        cost_estimate=NO_COST,
        name="feed_forward",
    )(hidden, cotangents, weights)


def product_kernel(count, adds, outs, *refs):
    rows, weights, rest = refs[:count], refs[count : 2 * count], refs[2 * count : 2 * count + adds]
    total = sum(dot_nt(r[...], w[...]) for r, w in zip(rows, weights))
    for add_ref in rest:
        total += add_ref[...].astype(f32)
    start = 0
    for out_ref in refs[-outs:]:
        out_ref[...] = total[start : start + out_ref.shape[0]].astype(out_ref.dtype)
        start += out_ref.shape[0]


def sum_of_products(lefts, weights, column, tokens, first, count, splits, add, before):
    rows = count * tokens
    width = weights[0].shape[0]
    tile = 512
    operands = list(lefts) + list(weights)
    specs = [pl.BlockSpec((rows, v.shape[1]), lambda i: (first // count, 0)) for v in lefts] + [
        pl.BlockSpec((tile, v.shape[1]), lambda i: (i, column)) for v in lefts
    ]
    if add is not None:
        operands.append(add)
        specs.append(pl.BlockSpec((rows, tile), lambda i: (0, i)))
    operands += before
    specs += [pl.BlockSpec(memory_space=pl.ANY)] * len(before)
    return pl.pallas_call(
        functools.partial(product_kernel, len(lefts), int(add is not None), len(splits)),
        grid=(width // tile,),
        in_specs=specs,
        out_specs=[pl.BlockSpec((r, tile), lambda i: (0, i)) for r, _ in splits],
        out_shape=[jax.ShapeDtypeStruct((r, width), dtype) for r, dtype in splits],
        compiler_params=pltpu.CompilerParams(vmem_limit_bytes=48 * 2**20),
        cost_estimate=NO_COST,
        name="sum_of_products",
    )(*operands)


def body(
    inputs,
    lengths,
    attention_gain,
    query_weight,
    key_matrix,
    value_matrix,
    out_weight,
    query_gain,
    key_gain,
    feedforward_gain,
    gate_weight,
    up_weight,
    down_weight,
    cotangent,
):
    rows, slots, width = inputs.shape
    tokens = rows * slots
    parts = lax.axis_size("ctx")
    heads = QUERY_HEADS_TOTAL // parts
    share = parts // KEY_VALUE_HEADS
    query_cols = heads * HEAD_SIZE
    weight_rows = query_weight.shape[0]
    feed = gate_weight.shape[1] // parts
    all_tokens = parts * tokens
    base = lax.axis_index("ctx").astype(jnp.int32)

    qkv_pack = jnp.concatenate(
        [query_weight.reshape(weight_rows, parts, query_cols)]
        + [
            jnp.repeat(w.reshape(weight_rows, KEY_VALUE_HEADS, HEAD_SIZE), share, axis=1)
            for w in (key_matrix, value_matrix)
        ],
        axis=2,
    )
    qkv_block = spread_columns(qkv_pack)
    out_block = spread_columns(out_weight.reshape(weight_rows, parts, query_cols))
    units = feed // 2
    feed_packs = [
        jnp.concatenate(
            [
                w.reshape(weight_rows, parts, feed)[:, :, start : start + units]
                for w in (gate_weight, up_weight, down_weight)
            ],
            axis=2,
        )
        for start in (0, units)
    ]
    flat = inputs.reshape(tokens, width).astype(f32)
    first_scale = rms_scale(flat)
    normed = flat * first_scale
    hidden, hidden_start = gather_tokens_and_start((normed * attention_gain).astype(bf16))
    hidden = hidden.reshape(all_tokens, width)
    first_block = spread_columns(after(feed_packs[0], out_block, *hidden_start))
    qkv_full = gather_rows(qkv_block)
    out_full = gather_rows(out_block)
    first_full = gather_rows(first_block)
    hidden = after(hidden, first_block)

    raw = dot_nn(hidden, qkv_full).reshape(parts, rows, slots, query_cols + 2 * HEAD_SIZE)
    cotangent_flat = cotangent.reshape(tokens, width)
    cotangents, cotangents_start = gather_tokens_and_start(after(cotangent_flat, first_block))
    cotangents = cotangents.reshape(all_tokens, width)
    last_block = spread_columns(after(feed_packs[1], *cotangents_start))
    cosine, sine = [
        t.T for t in rotary_tables(jnp.arange(parts * slots, dtype=jnp.int32), HEAD_SIZE)
    ]
    base_array = base.reshape(1)
    gains = [g.astype(f32).reshape(HEAD_SIZE, 1) for g in (query_gain, key_gain)]
    attended, log_total = attend(base_array, lengths, raw, *gains, cosine, sine)
    attended_rows = attended.reshape(all_tokens, query_cols)
    sums = partial_products(
        functools.partial(sum_of_products, [attended_rows], [out_full], 0, tokens), tokens
    )
    mixed = flat + finish_scatter(fence(sums, last_block), tokens)

    second_scale = rms_scale(mixed)
    normed_again = mixed * second_scale
    hidden_again = gather_tokens(
        after((normed_again * feedforward_gain).astype(bf16), first_full)
    ).reshape(all_tokens, width)
    last_full = gather_rows(after(last_block, first_full))
    fulls = [first_full, last_full]
    inners, grads, partials = [], [], []
    for which in range(2):
        if which == 1:
            fulls[1] = after(last_full, *partials[0])
        inner, grad = feed_forward(hidden_again, cotangents, fulls[which])
        inners.append(inner)
        grads.append(grad)
        partials.append(
            (dot_tn(hidden_again, grad).astype(bf16), dot_tn(cotangents, inner).astype(bf16))
        )
    first_gradients, last_gradients = [[scatter_rows(p) for p in pair] for pair in partials]
    sums = partial_products(
        functools.partial(sum_of_products, grads, fulls, 0, tokens), tokens
    )
    grad_hidden_again = after(finish_scatter(sums, tokens), first_gradients[1])
    feedforward_gain_local = jnp.sum(grad_hidden_again * normed_again, axis=0)
    scaled_again = grad_hidden_again * feedforward_gain
    grad_mixed = cotangent_flat.astype(f32) + second_scale * (
        scaled_again - normed_again * jnp.mean(scaled_again * normed_again, axis=-1, keepdims=True)
    )

    grad_branch = gather_tokens(grad_mixed.astype(bf16)).reshape(all_tokens, width)
    grad_branch = after(grad_branch, first_gradients[0])
    attended_gradient = dot_nn(grad_branch, out_full).astype(bf16)
    feed_sums = partial_products(
        functools.partial(sum_of_products, inners, fulls, 2, tokens), tokens
    )
    attended_gradient = after(attended_gradient, *feed_sums)
    feed_out = finish_scatter(fence(feed_sums, grad_branch), tokens)
    outputs = (mixed + feed_out).astype(bf16).reshape(rows, slots, width)
    grad_queries, grad_keys_values, query_gain_sums, key_gain_sums = attend_back(
        base_array,
        lengths,
        raw,
        *gains,
        cosine,
        sine,
        attended,
        attended_gradient.reshape(parts, rows, slots, query_cols),
        log_total,
    )
    query_gain_local, key_gain_local = query_gain_sums.sum(axis=1), key_gain_sums.sum(axis=1)
    grad_raw = jnp.concatenate(
        [
            grad_queries.reshape(all_tokens, query_cols),
            grad_keys_values.reshape(all_tokens, 2 * HEAD_SIZE),
        ],
        axis=1,
    )
    attention_partial = jnp.concatenate(
        [dot_tn(hidden, grad_raw), dot_tn(grad_branch, attended_rows)], axis=1
    ).astype(bf16)
    first_collected = [collect_columns(after(g, attended_gradient)) for g in first_gradients]
    attention_partial = after(attention_partial, feed_out, *first_collected)
    early = collect_early(after(attention_partial, last_gradients[1]))
    attention_collected = lax.psum_scatter(
        after(early, last_gradients[0]), "dp", scatter_dimension=0, tiled=True
    )
    attention_collected = jnp.swapaxes(
        attention_collected.reshape(parts, weight_rows, -1), 0, 1
    ).astype(f32)
    sums = partial_products(
        functools.partial(sum_of_products, [grad_raw], [qkv_full], 0, tokens), tokens
    )
    grad_hidden = finish_scatter(fence(sums, early), tokens)
    collected = [
        first_collected,
        [collect_columns(g) for g in last_gradients],
    ]
    gate_weight_gradient, up_weight_gradient = [
        jnp.concatenate([c[0][:, :, start : start + units] for c in collected], axis=2).reshape(
            weight_rows, parts * feed
        )
        for start in (0, units)
    ]
    down_weight_gradient = jnp.concatenate([c[1] for c in collected], axis=2).reshape(
        weight_rows, parts * feed
    )
    query_weight_gradient = attention_collected[:, :, :query_cols].reshape(weight_rows, -1)
    key_weight_gradient, value_weight_gradient = [
        attention_collected[:, :, start : start + HEAD_SIZE]
        .reshape(weight_rows, KEY_VALUE_HEADS, share, HEAD_SIZE)
        .sum(axis=2)
        .reshape(weight_rows, KEY_VALUE_HEADS * HEAD_SIZE)
        for start in (query_cols, query_cols + HEAD_SIZE)
    ]

    out_weight_gradient = attention_collected[:, :, query_cols + 2 * HEAD_SIZE :].reshape(
        weight_rows, -1
    )

    attention_gain_local = jnp.sum(grad_hidden * normed, axis=0)
    scaled_first = grad_hidden * attention_gain
    input_gradient = (
        grad_mixed
        + first_scale
        * (scaled_first - normed * jnp.mean(scaled_first * normed, axis=-1, keepdims=True))
    ).astype(bf16)
    gain_sums = sum_everywhere(
        jnp.concatenate(
            [attention_gain_local, feedforward_gain_local, query_gain_local, key_gain_local]
        )
    )
    attention_gain_gradient, feedforward_gain_gradient = gain_sums[:width], gain_sums[width : 2 * width]
    query_gain_gradient = gain_sums[2 * width : 2 * width + HEAD_SIZE]
    key_gain_gradient = gain_sums[2 * width + HEAD_SIZE :]
    return (
        outputs,
        input_gradient.reshape(rows, slots, width),
        attention_gain_gradient,
        query_weight_gradient,
        key_weight_gradient,
        value_weight_gradient,
        out_weight_gradient,
        query_gain_gradient,
        key_gain_gradient,
        feedforward_gain_gradient,
        gate_weight_gradient,
        up_weight_gradient,
        down_weight_gradient,
    )


def solution(mesh):
    weight = P(("dp", "ctx"), None)
    token = P("dp", "ctx", None)
    placed = (
        token, P("dp"), P(), weight, weight, weight, weight, P(), P(), P(), weight, weight, weight, token,
    )
    returned = (
        token, token, P(), weight, weight, weight, weight, P(), P(), P(), weight, weight, weight,
    )
    return jax.shard_map(
        body, mesh=mesh, in_specs=placed, out_specs=returned, check_vma=False
    )
```

time: 880 us -> 754 us (0.86)
  waiting for transfers between devices: 330 us -> 175 us
  Pallas kernels: 49.1 us -> 175 us
  matrix products: 151 us -> 71.1 us
  blocking collectives: 75.7 us -> 48.2 us
  starting transfers between devices: 65.4 us -> 89.9 us
  local copies, waits for them, and re-layouts: 125 us -> 115 us
    pallas_call x1 -> x37, Pallas kernels: 21.8 us -> 142 us  [the longest x16 81.3 us: sum_of_products(): pl.pallas_call(functools.partial(product_kernel, len(lefts), int(add is n...]
    reduce_scatter x3 -> x5, waiting for transfers between devices: 90 us -> 0.01 us  [the longest x4 0.01 us: scatter_rows(): return lax.psum_scatter(gradient, 'dp', scatter_dimension=0, tiled=True)]
    ppermute x64 -> x67, waiting for transfers between devices: 207 us -> 130 us  [hop(): lax.ppermute(value, 'ctx', [(i, i ^ bit) for i in range(lax.axis_size('ct...]
    psum x1 -> x0, blocking collectives: 59.4 us -> none  [body(): lax.psum((attention_gain_local, query_gain_local, key_gain_local, feedfor...]
    dot_general x4 -> x2, matrix products: 59.2 us -> 14.1 us  [dot_nn(): return jnp.dot(left, right, preferred_element_type=f32)]
    dot_general x4 -> x0, matrix products: 45 us -> none  [dot_nt(): lax.dot_general(left, right, (((1,), (1,)), ((), ())), preferred_element_...]
    all_to_all x0 -> x1, blocking collectives: none -> 34.7 us  [collect_early(): lax.all_to_all(block, 'ctx', split_axis=1, concat_axis=1, tiled=True)]
    all_to_all x2 -> x3, waiting for transfers between devices: 0.01 us -> 26.4 us  [spread_columns(): lax.all_to_all(packed.reshape(rows, parts * columns), 'ctx', split_axis=1...]
  transfers between devices with their start and end apart: 75 -> 85, of which waited for: 28 -> 28; matrix products, arithmetic and copies ran while one was open for 31% -> 27% of each run, Pallas kernels for 6% -> 24%
where the time goes in v2:
time: 754 us; the launch traced here: 746 us
  waiting for transfers between devices  175 us (23%)
  Pallas kernels  175 us (23%)
  local copies, waits for them, and re-layouts  115 us (15%)
  starting transfers between devices  89.9 us (12%)
  matrix products  71.1 us (9%)
  other arithmetic  55.3 us (7%)
  blocking collectives  48.2 us (6%)
  between operations  15.8 us (2%)
    ppermute x67, waiting for transfers between devices, hop(): lax.ppermute(value, 'ctx', [(i, i ^ bit) for i in range(lax.axis_size('ct...  130 us
    unnamed x243, local copies, waits for them, and re-layouts  82.6 us
    pallas_call x16, Pallas kernels, sum_of_products(): pl.pallas_call(functools.partial(product_kernel, len(lefts), int(add is n...  81.3 us
    dot_general x6, matrix products, dot_tn(): lax.dot_general(left, right, (((0,), (0,)), ((), ())), preferred_element_...  57 us
    ppermute x67, starting transfers between devices, hop(): lax.ppermute(value, 'ctx', [(i, i ^ bit) for i in range(lax.axis_size('ct...  51.8 us
    pallas_call x2, Pallas kernels, feed_forward(): pl.pallas_call(feed_kernel, grid=(count // tile,), in_specs=[rows, rows,...  39.2 us
    all_to_all x1, blocking collectives, collect_early(): lax.all_to_all(block, 'ctx', split_axis=1, concat_axis=1, tiled=True)  34.7 us
    pallas_call x1, Pallas kernels, attend_back(): pl.pallas_call(functools.partial(attend_back_kernel, blocks, slots, heads...  33 us
  transfers between devices with their start and end apart: 85, of which 28 were waited for; matrix products, arithmetic and copies ran while one was open for 27% of the time, Pallas kernels for 24%

profile of v2, /device:TPU:0, one launch (start us, length us, event | category | flops | bytes accessed | tf_op | source)
XLA Modules:
  0.0 745.9 jit_solution(10086290726759599505)
XLA Ops:
  10.5 13.5 %all_to_all.124 = bf16[64,8,384]{2,0,1:T(8,128)(2,1)} all-to-all(bf16[64,8,384]{2,0,1:T(8,128)(2,1)S(1)} %pad_maximum_fusion.7), channel_id=1, replica_groups=mesh['dp'=4,'ctx'=8] {'ctx'}, dimensions={1} | all-to-all | bytes 786432 | tf_op jit(solution)/shard_map/all_to_all | solution.py:132
  27.5 3.6 all-to-all-start
  40.4 15.0 %all-to-all-done = bf16[64,8,256]{2,0,1:T(8,128)(2,1)S(1)} async-done(((bf16[64,8,256]{2,0,1:T(8,128)(2,1)}), bf16[64,8,256]{2,0,1:T(8,128)(2,1)S(1)}, u32[]{:S(2)}, u32[]{:S(2)}) %all-to-all-start) | async-done | bytes 262176 | tf_op jit(solution)/shard_map/all_to_all | solution.py:132
  57.8 3.0 copy.102
  60.8 3.7 all-to-all-start.1
  74.8 11.2 %all-to-all-done.1 = bf16[64,8,1536]{2,0,1:T(8,128)(2,1)S(1)} async-done(((bf16[64,8,1536]{2,0,1:T(8,128)(2,1)}), bf16[64,8,1536]{2,0,1:T(8,128)(2,1)S(1)}, u32[]{:S(2)}, u32[]{:S(2)}) %all-to-all-start.1) | async-done | bytes 1572896 | tf_op jit(solution)/shard_map/all_to_all | solution.py:132
  89.5 6.4 collective-permute-done.5
  104.1 7.4 fusion.12
  111.5 21.8 %attend.1 = (bf16[8,2,128,256]{3,2,1,0:T(8,128)(2,1)S(1)}, f32[8,2,1,512]{3,2,1,0:T(1,128)S(1)}) custom-call(s32[1]{0:T(128)} %bitcast.1.base_ref, s32[2]{0:T(128)S(1)} %copy-done.54, f32[8,2,128,384]{3,2,1,0:T(8,128)S(1)} %bitcast.180, f32[8,2,128,384]{3,2,1,0:T(8,128)S(1)} %bitcast.181, f32[64,1]{1,0:T(8,128)S(1)} %copy.106.qg_ref, ...), custom_call_target="tpu_custom_call" | custom-call | tf_op jit(solution)/shard_map/attend/pallas_call | solution.py:376
  142.6 3.1 sum_of_products.18
  151.5 21.1 %collective-permute-done.11.refs_2_ = bf16[256,2048]{1,0:T(8,128)(2,1)} collective-permute-done((bf16[256,2048]{1,0:T(8,128)(2,1)}, bf16[256,2048]{1,0:T(8,128)(2,1)}, u32[]{:S(2)}, u32[]{:S(2)}) %collective-permute-start.11) | collective-permute-done | bytes 1048608 | tf_op jit(solution)/shard_map/ppermute | solution.py:75
  172.7 3.0 copy.108
  175.7 4.5 all-to-all-start.3
  190.2 3.2 copy-done.64
  194.0 4.4 sum_of_products.19
  204.8 7.3 collective-permute-done.29
  217.9 4.8 collective-permute-done.13
  224.0 4.8 collective-permute-done.15
  235.2 5.0 collective-permute-done.12
  240.2 9.4 %collective-permute-done.14 = bf16[128,2048]{1,0:T(8,128)(2,1)S(1)} collective-permute-done((bf16[128,2048]{1,0:T(8,128)(2,1)}, bf16[128,2048]{1,0:T(8,128)(2,1)S(1)}, u32[]{:S(2)}, u32[]{:S(2)}) %collective-permute-start.14) | collective-permute-done | bytes 524320 | tf_op jit(solution)/shard_map/ppermute | solution.py:75
  259.5 18.2 %collective-permute-done.19 = bf16[256,2048]{1,0:T(8,128)(2,1)S(1)} collective-permute-done((bf16[256,2048]{1,0:T(8,128)(2,1)}, bf16[256,2048]{1,0:T(8,128)(2,1)S(1)}, u32[]{:S(2)}, u32[]{:S(2)}) %collective-permute-start.19) | collective-permute-done | bytes 1048608 | tf_op jit(solution)/shard_map/ppermute | solution.py:75
  281.6 10.8 %collective-permute-done.23 = bf16[128,2048]{1,0:T(8,128)(2,1)S(1)} collective-permute-done((bf16[128,2048]{1,0:T(8,128)(2,1)S(1)}, bf16[128,2048]{1,0:T(8,128)(2,1)S(1)}, u32[]{:S(2)}, u32[]{:S(2)}) %collective-permute-start.23) | collective-permute-done | bytes 524320 | tf_op jit(solution)/shard_map/ppermute | solution.py:75
  295.4 3.3 copy-done.63
  298.7 19.5 %feed_forward.2 = (bf16[2048,512]{1,0:T(8,128)(2,1)S(1)}, bf16[2048,1024]{1,0:T(8,128)(2,1)}) custom-call(bf16[2048,2048]{1,0:T(8,128)(2,1)} %bitcast.196, bf16[2048,2048]{1,0:T(8,128)(2,1)} %bitcast.200, bf16[2048,1536]{1,0:T(8,128)(2,1)} %all-gather.9.cloned.1.call-done.refs_1_.weight_ref.refs_2_), custom_call_target="tpu_custom_call" | custom-call | tf_op jit(solution)/shard_map/feed_forward/pallas_call | solution.py:456
  318.2 10.2 %convolution_convert_fusion.3.refs_2_ = bf16[2048,512]{1,0:T(8,128)(2,1)} fusion(bf16[2048,2048]{1,0:T(8,128)(2,1)} %bitcast.201, bf16[2048,512]{1,0:T(8,128)(2,1)S(1)} %get-tuple-element.87.refs_0_), kind=kOutput, calls=%fused_computation.3 | convolution fusion | flops 4296015872 | bytes 12582912 | tf_op jit(solution)/shard_map/dot_general | solution.py:38
  328.5 14.0 %convolution_convert_fusion.1.refs_1_ = bf16[2048,1024]{1,0:T(8,128)(2,1)} fusion(bf16[2048,2048]{1,0:T(8,128)(2,1)} %bitcast.197, bf16[2048,1024]{1,0:T(8,128)(2,1)} %get-tuple-element.88.refs_0_), kind=kOutput, calls=%fused_computation.1 | convolution fusion | flops 8592031744 | bytes 16777216 | tf_op jit(solution)/shard_map/dot_general | solution.py:38
  342.7 2.8 all-gather.11.cloned.1.call-done.refs_0_
  345.6 19.6 %feed_forward.3 = (bf16[2048,512]{1,0:T(8,128)(2,1)S(1)}, bf16[2048,1024]{1,0:T(8,128)(2,1)}) custom-call(bf16[2048,2048]{1,0:T(8,128)(2,1)} %bitcast.198, bf16[2048,2048]{1,0:T(8,128)(2,1)} %bitcast.202, bf16[2048,1536]{1,0:T(8,128)(2,1)} %fence.25.weight_ref.refs_3_), custom_call_target="tpu_custom_call" | custom-call | tf_op jit(solution)/shard_map/feed_forward/pallas_call | solution.py:456
  365.2 6.4 sum_of_products.24
  374.4 5.9 sum_of_products.25
  380.2 10.1 %sum_of_products.26 = bf16[768,2048]{1,0:T(8,128)(2,1)S(1)} custom-call(bf16[2048,1024]{1,0:T(8,128)(2,1)} %get-tuple-element.88.refs_0_, bf16[2048,1024]{1,0:T(8,128)(2,1)} %get-tuple-element.97.refs_1_, bf16[2048,1536]{1,0:T(8,128)(2,1)} %all-gather.9.cloned.1.call-done.refs_1_.weight_ref.refs_2_, bf16[2048,1536]{1,0:T(8,128)(2,1)} %fence.25.weight_ref.refs_3_, ...), custom_call_target="tpu_custom_call" | custom-call | tf_op jit(solution)/shard_map/sum_of_products/pallas_call | solution.py:498
  393.6 4.8 sum_of_products.20
  400.1 11.7 %sum_of_products.27 = (f32[256,2048]{1,0:T(8,128)S(1)}, bf16[128,2048]{1,0:T(8,128)(2,1)}, bf16[128,2048]{1,0:T(8,128)(2,1)S(1)}, bf16[128,2048]{1,0:T(8,128)(2,1)S(1)}, bf16[128,2048]{1,0:T(8,128)(2,1)}) custom-call(bf16[2048,1024]{1,0:T(8,128)(2,1)} %get-tuple-element.88.refs_0_, bf16[2048,1024]{1,0:T(8,128)(2,1)} %get-tuple-element.97.refs_1_, ...), custom_call_target="tpu_custom_call" | custom-call | tf_op jit(solution)/shard_map/sum_of_products/pallas_call | solution.py:498
  421.1 9.4 %convolution_convert_fusion.2 = bf16[2048,512]{1,0:T(8,128)(2,1)} fusion(bf16[2048,2048]{1,0:T(8,128)(2,1)} %bitcast.203, bf16[2048,512]{1,0:T(8,128)(2,1)S(1)} %get-tuple-element.89.refs_1_), kind=kOutput, calls=%fused_computation.2 | convolution fusion | flops 4296015872 | bytes 12582912 | tf_op jit(solution)/shard_map/dot_general | solution.py:38
  431.0 4.3 sum_of_products.21
  436.1 7.0 sum_of_products.22
  444.4 3.3 convert_add_fusion.2.refs_0_
  449.3 2.9 multiply_reduce_fusion
  455.5 12.8 %convolution_convert_fusion = bf16[2048,1024]{1,0:T(8,128)(2,1)} fusion(bf16[2048,2048]{1,0:T(8,128)(2,1)} %bitcast.199, bf16[2048,1024]{1,0:T(8,128)(2,1)S(1)} %copy-done.60), kind=kOutput, calls=%fused_computation | convolution fusion | flops 8592031744 | bytes 16777216 | tf_op jit(solution)/shard_map/dot_general | solution.py:38
  468.3 7.0 sum_of_products.23
  475.4 3.3 collective-permute-done.43
  484.3 7.2 collective-permute-done.47
  497.3 6.8 convolution_convert_fusion.6.refs_0_
  504.1 4.6 all-to-all-start.5
  515.3 33.0 %attend_back.1 = (bf16[8,2,128,256]{3,2,1,0:T(8,128)(2,1)S(1)}, bf16[8,2,128,128]{3,2,1,0:T(8,128)(2,1)S(1)}, f32[64,128]{1,0:T(8,128)S(1)}, f32[64,128]{1,0:T(8,128)S(1)}) custom-call(s32[1]{0:T(128)} %bitcast.1.base_ref, s32[2]{0:T(128)S(1)} %copy-done.55, f32[8,2,128,384]{3,2,1,0:T(8,128)S(1)} %bitcast.182, f32[8,2,128,384]{3,2,1,0:T(8,128)S(1)} %bitcast.183, ...), custom_call_target="tpu_custom_call" | custom-call | tf_op jit(solution)/shard_map/attend_back/pallas_call | solution.py:408
  548.3 6.0 convolution_convert_fusion.5
  554.4 4.6 convolution_convert_fusion.4
  564.6 4.3 all-to-all-start.4
  579.2 5.7 all-to-all-done.4
  584.9 3.2 convert_bitcast_fusion.1.refs_2_
  588.0 3.0 sum_of_products.29
  591.9 3.7 sum_of_products.30
  595.7 3.9 add_convert_fusion.1
  601.6 34.7 %all_to_all.125 = bf16[4,8,64,640]{3,2,0,1:T(8,128)(2,1)S(1)} all-to-all(bf16[4,8,64,640]{3,2,0,1:T(8,128)(2,1)S(1)} %copy.115), channel_id=1, replica_groups=mesh['dp'=4,'ctx'=8] {'ctx'}, dimensions={1} | all-to-all | bytes 5242880 | tf_op jit(solution)/shard_map/all_to_all | solution.py:155
  639.6 4.2 all-to-all-start.8
  643.7 5.0 sum_of_products.31
  659.6 4.0 all-to-all-start.7
  675.7 5.7 all-to-all-done.7
  683.4 9.7 %collective-permute-done.58 = bf16[128,2048]{1,0:T(8,128)(2,1)} collective-permute-done((bf16[128,2048]{1,0:T(8,128)(2,1)S(1)}, bf16[128,2048]{1,0:T(8,128)(2,1)}, u32[]{:S(2)}, u32[]{:S(2)}) %collective-permute-start.58) | collective-permute-done | bytes 524320 | tf_op jit(solution)/shard_map/ppermute | solution.py:75
  693.1 10.1 %collective-permute-done.60 = bf16[128,2048]{1,0:T(8,128)(2,1)} collective-permute-done((bf16[128,2048]{1,0:T(8,128)(2,1)}, bf16[128,2048]{1,0:T(8,128)(2,1)}, u32[]{:S(2)}, u32[]{:S(2)}) %collective-permute-start.60) | collective-permute-done | bytes 524320 | tf_op jit(solution)/shard_map/ppermute | solution.py:75
  703.3 2.6 multiply_reduce_fusion.1
  716.8 3.8 collective-permute-done.67
  720.5 8.1 %collective-permute-start.68 = (f32[4224]{0:T(1024)S(1)}, f32[4224]{0:T(1024)S(1)}, u32[]{:S(2)}, u32[]{:S(2)}) collective-permute-start(f32[4224]{0:T(1024)S(1)} %add.127), channel_id=1, source_target_pairs={{0,16},{8,24},{16,0},{24,8},{1,17},{9,25},{17,1},{25,9},{2,18},{10... | collective-permute-start | bytes 50696 | tf_op jit(solution)/shard_map/ppermute | solution.py:126
  728.6 4.1 add_convert_fusion
  (500 shorter events, 208.4 us)
Async XLA Ops:
  7.2 96.9 %all-gather.5.cloned.1.call-start = ((), (), s32[]{:S(2)}) async-start(), calls=%async_computation.14 | async-start | bytes 1966080 | tf_op jit(solution)/shard_map/all_gather | solution.py:138
  25.7 61.5 %collective-permute-start.2 = (bf16[256,2048]{1,0:T(8,128)(2,1)}, bf16[256,2048]{1,0:T(8,128)(2,1)}, u32[]{:S(2)}, u32[]{:S(2)}) collective-permute-start(bf16[256,2048]{1,0:T(8,128)(2,1)} %multiply_convert_fusion.1), channel_id=1, source_target_pairs={{0,1},{1,0},{2,3},{3,2},{4,5},{5,4},{6,7},{7,6},{8,9},{9,8},{10,11... | collective-permute-start | bytes 3145736 | tf_op jit(solution)/shard_map/ppermute | solution.py:75
  25.7 31.1 %collective-permute-start.1 = (bf16[256,2048]{1,0:T(8,128)(2,1)}, bf16[256,2048]{1,0:T(8,128)(2,1)S(1)}, u32[]{:S(2)}, u32[]{:S(2)}) collective-permute-start(bf16[256,2048]{1,0:T(8,128)(2,1)} %multiply_convert_fusion.1), channel_id=1, source_target_pairs={{0,4},{1,5},{2,6},{3,7},{4,0},{5,1},{6,2},{7,3},{8,12},{9,13},{10,... | collective-permute-start | bytes 3145736 | tf_op jit(solution)/shard_map/ppermute | solution.py:75
  26.2 30.5 %collective-permute-start = (bf16[256,2048]{1,0:T(8,128)(2,1)}, bf16[256,2048]{1,0:T(8,128)(2,1)}, u32[]{:S(2)}, u32[]{:S(2)}) collective-permute-start(bf16[256,2048]{1,0:T(8,128)(2,1)} %multiply_convert_fusion.1), channel_id=1, source_target_pairs={{0,2},{1,3},{2,0},{3,1},{4,6},{5,7},{6,4},{7,5},{8,10},{9,11},{10,... | collective-permute-start | bytes 3145736 | tf_op jit(solution)/shard_map/ppermute | solution.py:75
  27.5 27.9 %all-to-all-start = ((bf16[64,8,256]{2,0,1:T(8,128)(2,1)}), bf16[64,8,256]{2,0,1:T(8,128)(2,1)S(1)}, u32[]{:S(2)}, u32[]{:S(2)}) async-start(bf16[64,8,256]{2,0,1:T(8,128)(2,1)} %bitcast.178), calls=%async_computation | async-start | bytes 524288 | tf_op jit(solution)/shard_map/all_to_all | solution.py:132
  31.1 103.9 %all-gather.7.cloned.1.call-start = ((), (), s32[]{:S(2)}) async-start(), calls=%async_computation.15 | async-start | bytes 1310720 | tf_op jit(solution)/shard_map/all_gather | solution.py:138
  60.8 25.2 %all-to-all-start.1 = ((bf16[64,8,1536]{2,0,1:T(8,128)(2,1)}), bf16[64,8,1536]{2,0,1:T(8,128)(2,1)S(1)}, u32[]{:S(2)}, u32[]{:S(2)}) async-start(bf16[64,8,1536]{2,0,1:T(8,128)(2,1)} %copy.102), calls=%async_computation.1 | async-start | bytes 3145728 | tf_op jit(solution)/shard_map/all_to_all | solution.py:132
  64.5 159.5 %all-gather.9.cloned.1.call-start = ((), (), s32[]{:S(2)}) async-start(), calls=%async_computation.16 | async-start | bytes 7864320 | tf_op jit(solution)/shard_map/all_gather | solution.py:138
  65.6 31.3 %collective-permute-start.6 = (bf16[128,2048]{1,0:T(8,128)(2,1)}, bf16[128,2048]{1,0:T(8,128)(2,1)S(1)}, u32[]{:S(2)}, u32[]{:S(2)}) collective-permute-start(bf16[128,2048]{1,0:T(8,128)(2,1)} %slice.105), channel_id=1, source_target_pairs={{0,2},{1,3},{2,0},{3,1},{4,6},{5,7},{6,4},{7,5},{8,10},{9,11},{10,... | collective-permute-start | bytes 1572872 | tf_op jit(solution)/shard_map/ppermute | solution.py:75
  69.4 26.4 %collective-permute-start.5 = (bf16[128,2048]{1,0:T(8,128)(2,1)}, bf16[128,2048]{1,0:T(8,128)(2,1)}, u32[]{:S(2)}, u32[]{:S(2)}) collective-permute-start(bf16[128,2048]{1,0:T(8,128)(2,1)} %slice.104), channel_id=1, source_target_pairs={{0,4},{1,5},{2,6},{3,7},{4,0},{5,1},{6,2},{7,3},{8,12},{9,13},{10,... | collective-permute-start | bytes 1572872 | tf_op jit(solution)/shard_map/ppermute | solution.py:75
  70.9 28.6 %collective-permute-start.4 = (bf16[256,2048]{1,0:T(8,128)(2,1)S(1)}, bf16[256,2048]{1,0:T(8,128)(2,1)}, u32[]{:S(2)}, u32[]{:S(2)}) collective-permute-start(bf16[256,2048]{1,0:T(8,128)(2,1)S(1)} %copy-done.82), channel_id=1, source_target_pairs={{0,1},{1,0},{2,3},{3,2},{4,5},{5,4},{6,7},{7,6},{8,9},{9,8},{10,11... | collective-permute-start | bytes 3145736 | tf_op jit(solution)/shard_map/ppermute | solution.py:75
  70.9 26.2 %collective-permute-start.3 = (bf16[256,2048]{1,0:T(8,128)(2,1)}, bf16[256,2048]{1,0:T(8,128)(2,1)}, u32[]{:S(2)}, u32[]{:S(2)}) collective-permute-start(bf16[256,2048]{1,0:T(8,128)(2,1)} %collective-permute-done.refs_2_), channel_id=1, source_target_pairs={{0,1},{1,0},{2,3},{3,2},{4,5},{5,4},{6,7},{7,6},{8,9},{9,8},{10,11... | collective-permute-start | bytes 3145736 | tf_op jit(solution)/shard_map/ppermute | solution.py:75
  145.8 44.4 %collective-permute-start.9 = (bf16[768,2048]{1,0:T(8,128)(2,1)}, bf16[768,2048]{1,0:T(8,128)(2,1)}, u32[]{:S(2)}, u32[]{:S(2)}) collective-permute-start(bf16[768,2048]{1,0:T(8,128)(2,1)} %sum_of_products.18), channel_id=1, source_target_pairs={{0,1},{1,0},{2,3},{3,2},{4,5},{5,4},{6,7},{7,6},{8,9},{9,8},{10,11... | collective-permute-start | bytes 9437192 | tf_op jit(solution)/shard_map/ppermute | solution.py:75
  147.1 25.5 %collective-permute-start.11 = (bf16[256,2048]{1,0:T(8,128)(2,1)}, bf16[256,2048]{1,0:T(8,128)(2,1)}, u32[]{:S(2)}, u32[]{:S(2)}) collective-permute-start(bf16[256,2048]{1,0:T(8,128)(2,1)} %fence.20), channel_id=1, source_target_pairs={{0,4},{1,5},{2,6},{3,7},{4,0},{5,1},{6,2},{7,3},{8,12},{9,13},{10,... | collective-permute-start | bytes 3145736 | tf_op jit(solution)/shard_map/ppermute | solution.py:75
  147.5 25.2 %collective-permute-start.10 = (bf16[256,2048]{1,0:T(8,128)(2,1)}, bf16[256,2048]{1,0:T(8,128)(2,1)}, u32[]{:S(2)}, u32[]{:S(2)}) collective-permute-start(bf16[256,2048]{1,0:T(8,128)(2,1)} %fence.20), channel_id=1, source_target_pairs={{0,2},{1,3},{2,0},{3,1},{4,6},{5,7},{6,4},{7,5},{8,10},{9,11},{10,... | collective-permute-start | bytes 3145736 | tf_op jit(solution)/shard_map/ppermute | solution.py:75
  151.5 50.3 %collective-permute-start.26 = (bf16[256,2048]{1,0:T(8,128)(2,1)S(1)}, bf16[256,2048]{1,0:T(8,128)(2,1)}, u32[]{:S(2)}, u32[]{:S(2)}) collective-permute-start(bf16[256,2048]{1,0:T(8,128)(2,1)S(1)} %copy-done.73), channel_id=1, source_target_pairs={{0,1},{1,0},{2,3},{3,2},{4,5},{5,4},{6,7},{7,6},{8,9},{9,8},{10,11... | collective-permute-start | bytes 3145736 | tf_op jit(solution)/shard_map/ppermute | solution.py:75
  175.7 26.0 %all-to-all-start.3 = ((bf16[64,8,1536]{2,0,1:T(8,128)(2,1)}), bf16[64,8,1536]{2,0,1:T(8,128)(2,1)}, u32[]{:S(2)}, u32[]{:S(2)}) async-start(bf16[64,8,1536]{2,0,1:T(8,128)(2,1)} %copy.108), calls=%async_computation.3 | async-start | bytes 3145728 | tf_op jit(solution)/shard_map/all_to_all | solution.py:132
  182.2 32.7 %collective-permute-start.30 = (bf16[128,2048]{1,0:T(8,128)(2,1)}, bf16[128,2048]{1,0:T(8,128)(2,1)}, u32[]{:S(2)}, u32[]{:S(2)}) collective-permute-start(bf16[128,2048]{1,0:T(8,128)(2,1)} %slice.115), channel_id=1, source_target_pairs={{0,2},{1,3},{2,0},{3,1},{4,6},{5,7},{6,4},{7,5},{8,10},{9,11},{10,... | collective-permute-start | bytes 1572872 | tf_op jit(solution)/shard_map/ppermute | solution.py:75
  186.1 26.0 %collective-permute-start.29 = (bf16[128,2048]{1,0:T(8,128)(2,1)}, bf16[128,2048]{1,0:T(8,128)(2,1)}, u32[]{:S(2)}, u32[]{:S(2)}) collective-permute-start(bf16[128,2048]{1,0:T(8,128)(2,1)} %slice.114), channel_id=1, source_target_pairs={{0,4},{1,5},{2,6},{3,7},{4,0},{5,1},{6,2},{7,3},{8,12},{9,13},{10,... | collective-permute-start | bytes 1572872 | tf_op jit(solution)/shard_map/ppermute | solution.py:75
  187.6 45.3 %collective-permute-start.28 = (bf16[256,2048]{1,0:T(8,128)(2,1)}, bf16[256,2048]{1,0:T(8,128)(2,1)}, u32[]{:S(2)}, u32[]{:S(2)}) collective-permute-start(bf16[256,2048]{1,0:T(8,128)(2,1)} %collective-permute-done.11.refs_2_), channel_id=1, source_target_pairs={{0,1},{1,0},{2,3},{3,2},{4,5},{5,4},{6,7},{7,6},{8,9},{9,8},{10,11... | collective-permute-start | bytes 3145736 | tf_op jit(solution)/shard_map/ppermute | solution.py:75
  193.4 36.5 %collective-permute-start.27 = (bf16[256,2048]{1,0:T(8,128)(2,1)}, bf16[256,2048]{1,0:T(8,128)(2,1)}, u32[]{:S(2)}, u32[]{:S(2)}) collective-permute-start(bf16[256,2048]{1,0:T(8,128)(2,1)} %collective-permute-done.10.refs_1_), channel_id=1, source_target_pairs={{0,1},{1,0},{2,3},{3,2},{4,5},{5,4},{6,7},{7,6},{8,9},{9,8},{10,11... | collective-permute-start | bytes 3145736 | tf_op jit(solution)/shard_map/ppermute | solution.py:75
  201.8 143.8 %all-gather.11.cloned.1.call-start = ((), (), s32[]{:S(2)}) async-start(), calls=%async_computation.17 | async-start | bytes 7864320 | tf_op jit(solution)/shard_map/all_gather | solution.py:138
  201.8 20.9 %collective-permute-start.13 = (bf16[128,2048]{1,0:T(8,128)(2,1)}, bf16[128,2048]{1,0:T(8,128)(2,1)S(1)}, u32[]{:S(2)}, u32[]{:S(2)}) collective-permute-start(bf16[128,2048]{1,0:T(8,128)(2,1)} %get-tuple-element.83), channel_id=1, source_target_pairs={{0,4},{1,5},{2,6},{3,7},{4,0},{5,1},{6,2},{7,3},{8,12},{9,13},{10,... | collective-permute-start | bytes 1572872 | tf_op jit(solution)/shard_map/ppermute | solution.py:75
  216.9 23.3 %collective-permute-start.12 = (bf16[128,2048]{1,0:T(8,128)(2,1)S(1)}, bf16[128,2048]{1,0:T(8,128)(2,1)}, u32[]{:S(2)}, u32[]{:S(2)}) collective-permute-start(bf16[128,2048]{1,0:T(8,128)(2,1)S(1)} %copy-done.40), channel_id=1, source_target_pairs={{0,2},{1,3},{2,0},{3,1},{4,6},{5,7},{6,4},{7,5},{8,10},{9,11},{10,... | collective-permute-start | bytes 1572872 | tf_op jit(solution)/shard_map/ppermute | solution.py:75
  222.7 17.5 %collective-permute-start.17 = (bf16[128,2048]{1,0:T(8,128)(2,1)S(1)}, bf16[128,2048]{1,0:T(8,128)(2,1)}, u32[]{:S(2)}, u32[]{:S(2)}) collective-permute-start(bf16[128,2048]{1,0:T(8,128)(2,1)S(1)} %copy-done.42), channel_id=1, source_target_pairs={{0,4},{1,5},{2,6},{3,7},{4,0},{5,1},{6,2},{7,3},{8,12},{9,13},{10,... | collective-permute-start | bytes 1572872 | tf_op jit(solution)/shard_map/ppermute | solution.py:75
  224.0 223.7 %reduce-scatter.6.cloned.1.call-start = ((), (), s32[]{:S(2)}) async-start(), calls=%async_computation.18 | async-start | bytes 2621440 | tf_op jit(solution)/shard_map/reduce_scatter | solution.py:142
  228.8 20.7 %collective-permute-start.14 = (bf16[128,2048]{1,0:T(8,128)(2,1)}, bf16[128,2048]{1,0:T(8,128)(2,1)S(1)}, u32[]{:S(2)}, u32[]{:S(2)}) collective-permute-start(bf16[128,2048]{1,0:T(8,128)(2,1)} %add_convert_fusion.9), channel_id=1, source_target_pairs={{0,2},{1,3},{2,0},{3,1},{4,6},{5,7},{6,4},{7,5},{8,10},{9,11},{10,... | collective-permute-start | bytes 1572872 | tf_op jit(solution)/shard_map/ppermute | solution.py:75
  229.9 19.6 %collective-permute-start.16 = (bf16[128,2048]{1,0:T(8,128)(2,1)S(1)}, bf16[128,2048]{1,0:T(8,128)(2,1)S(1)}, u32[]{:S(2)}, u32[]{:S(2)}) collective-permute-start(bf16[128,2048]{1,0:T(8,128)(2,1)S(1)} %add_convert_fusion.8), channel_id=1, source_target_pairs={{0,4},{1,5},{2,6},{3,7},{4,0},{5,1},{6,2},{7,3},{8,12},{9,13},{10,... | collective-permute-start | bytes 1572872 | tf_op jit(solution)/shard_map/ppermute | solution.py:75
  232.9 25.5 %collective-permute-start.31 = (bf16[256,2048]{1,0:T(8,128)(2,1)}, bf16[256,2048]{1,0:T(8,128)(2,1)S(1)}, u32[]{:S(2)}, u32[]{:S(2)}) collective-permute-start(bf16[256,2048]{1,0:T(8,128)(2,1)} %constant_dynamic-update-slice_fusion.4), channel_id=1, source_target_pairs={{0,1},{1,0},{2,3},{3,2},{4,5},{5,4},{6,7},{7,6},{8,9},{9,8},{10,11... | collective-permute-start | bytes 3145736 | tf_op jit(solution)/shard_map/ppermute | solution.py:75
  253.9 23.8 %collective-permute-start.19 = (bf16[256,2048]{1,0:T(8,128)(2,1)}, bf16[256,2048]{1,0:T(8,128)(2,1)S(1)}, u32[]{:S(2)}, u32[]{:S(2)}) collective-permute-start(bf16[256,2048]{1,0:T(8,128)(2,1)} %fence.23), channel_id=1, source_target_pairs={{0,4},{1,5},{2,6},{3,7},{4,0},{5,1},{6,2},{7,3},{8,12},{9,13},{10,... | collective-permute-start | bytes 3145736 | tf_op jit(solution)/shard_map/ppermute | solution.py:75
  254.3 26.0 %collective-permute-start.18 = (bf16[256,2048]{1,0:T(8,128)(2,1)}, bf16[256,2048]{1,0:T(8,128)(2,1)S(1)}, u32[]{:S(2)}, u32[]{:S(2)}) collective-permute-start(bf16[256,2048]{1,0:T(8,128)(2,1)} %fence.23), channel_id=1, source_target_pairs={{0,2},{1,3},{2,0},{3,1},{4,6},{5,7},{6,4},{7,5},{8,10},{9,11},{10,... | collective-permute-start | bytes 3145736 | tf_op jit(solution)/shard_map/ppermute | solution.py:75
  259.4 22.1 %collective-permute-start.20 = (bf16[256,2048]{1,0:T(8,128)(2,1)S(1)}, bf16[256,2048]{1,0:T(8,128)(2,1)S(1)}, u32[]{:S(2)}, u32[]{:S(2)}) collective-permute-start(bf16[256,2048]{1,0:T(8,128)(2,1)S(1)} %copy-done.78), channel_id=1, source_target_pairs={{0,1},{1,0},{2,3},{3,2},{4,5},{5,4},{6,7},{7,6},{8,9},{9,8},{10,11... | collective-permute-start | bytes 3145736 | tf_op jit(solution)/shard_map/ppermute | solution.py:75
  328.4 167.6 %reduce-scatter.8.cloned.1.call-start = ((), (), s32[]{:S(2)}) async-start(), calls=%async_computation.19 | async-start | bytes 5242880 | tf_op jit(solution)/shard_map/reduce_scatter | solution.py:142
  342.5 257.1 %reduce-scatter.10.cloned.1.call-start = ((), (), s32[]{:S(2)}) async-start(), calls=%async_computation.20 | async-start | bytes 2621440 | tf_op jit(solution)/shard_map/reduce_scatter | solution.py:142
  390.6 23.1 %collective-permute-start.37 = (bf16[128,2048]{1,0:T(8,128)(2,1)S(1)}, bf16[128,2048]{1,0:T(8,128)(2,1)}, u32[]{:S(2)}, u32[]{:S(2)}) collective-permute-start(bf16[128,2048]{1,0:T(8,128)(2,1)S(1)} %get-tuple-element.102), channel_id=1, source_target_pairs={{0,4},{1,5},{2,6},{3,7},{4,0},{5,1},{6,2},{7,3},{8,12},{9,13},{10,... | collective-permute-start | bytes 1572872 | tf_op jit(solution)/shard_map/ppermute | solution.py:75
  392.1 25.0 %collective-permute-start.39 = (bf16[128,2048]{1,0:T(8,128)(2,1)S(1)}, bf16[128,2048]{1,0:T(8,128)(2,1)}, u32[]{:S(2)}, u32[]{:S(2)}) collective-permute-start(bf16[128,2048]{1,0:T(8,128)(2,1)S(1)} %get-tuple-element.98.refs_4_), channel_id=1, source_target_pairs={{0,2},{1,3},{2,0},{3,1},{4,6},{5,7},{6,4},{7,5},{8,10},{9,11},{10,... | collective-permute-start | bytes 1572872 | tf_op jit(solution)/shard_map/ppermute | solution.py:75
  398.4 32.6 %collective-permute-start.32 = (bf16[256,2048]{1,0:T(8,128)(2,1)}, bf16[256,2048]{1,0:T(8,128)(2,1)S(1)}, u32[]{:S(2)}, u32[]{:S(2)}) collective-permute-start(bf16[256,2048]{1,0:T(8,128)(2,1)} %sum_of_products.20), channel_id=1, source_target_pairs={{0,1},{1,0},{2,3},{3,2},{4,5},{5,4},{6,7},{7,6},{8,9},{9,8},{10,11... | collective-permute-start | bytes 3145736 | tf_op jit(solution)/shard_map/ppermute | solution.py:75
  413.1 30.0 %collective-permute-start.36 = (bf16[128,2048]{1,0:T(8,128)(2,1)}, bf16[128,2048]{1,0:T(8,128)(2,1)}, u32[]{:S(2)}, u32[]{:S(2)}) collective-permute-start(bf16[128,2048]{1,0:T(8,128)(2,1)} %get-tuple-element.100), channel_id=1, source_target_pairs={{0,2},{1,3},{2,0},{3,1},{4,6},{5,7},{6,4},{7,5},{8,10},{9,11},{10,... | collective-permute-start | bytes 1572872 | tf_op jit(solution)/shard_map/ppermute | solution.py:75
  415.7 27.4 %collective-permute-start.38 = (bf16[128,2048]{1,0:T(8,128)(2,1)}, bf16[128,2048]{1,0:T(8,128)(2,1)}, u32[]{:S(2)}, u32[]{:S(2)}) collective-permute-start(bf16[128,2048]{1,0:T(8,128)(2,1)} %add_convert_fusion.7), channel_id=1, source_target_pairs={{0,2},{1,3},{2,0},{3,1},{4,6},{5,7},{6,4},{7,5},{8,10},{9,11},{10,... | collective-permute-start | bytes 1572872 | tf_op jit(solution)/shard_map/ppermute | solution.py:75
  419.0 24.1 %collective-permute-start.40 = (bf16[128,2048]{1,0:T(8,128)(2,1)}, bf16[128,2048]{1,0:T(8,128)(2,1)}, u32[]{:S(2)}, u32[]{:S(2)}) collective-permute-start(bf16[128,2048]{1,0:T(8,128)(2,1)} %add_convert_fusion.6), channel_id=1, source_target_pairs={{0,4},{1,5},{2,6},{3,7},{4,0},{5,1},{6,2},{7,3},{8,12},{9,13},{10,... | collective-permute-start | bytes 1572872 | tf_op jit(solution)/shard_map/ppermute | solution.py:75
  419.7 24.7 %collective-permute-start.41 = (bf16[128,2048]{1,0:T(8,128)(2,1)}, bf16[128,2048]{1,0:T(8,128)(2,1)}, u32[]{:S(2)}, u32[]{:S(2)}) collective-permute-start(bf16[128,2048]{1,0:T(8,128)(2,1)} %get-tuple-element.104), channel_id=1, source_target_pairs={{0,4},{1,5},{2,6},{3,7},{4,0},{5,1},{6,2},{7,3},{8,12},{9,13},{10,... | collective-permute-start | bytes 1572872 | tf_op jit(solution)/shard_map/ppermute | solution.py:75
  430.5 209.0 %reduce-scatter.12.cloned.1.call-start = ((), (), s32[]{:S(2)}) async-start(), calls=%async_computation.21 | async-start | bytes 5242880 | tf_op jit(solution)/shard_map/reduce_scatter | solution.py:142
  443.1 25.2 %collective-permute-start.33 = (bf16[768,2048]{1,0:T(8,128)(2,1)}, bf16[768,2048]{1,0:T(8,128)(2,1)}, u32[]{:S(2)}, u32[]{:S(2)}) collective-permute-start(bf16[768,2048]{1,0:T(8,128)(2,1)} %sum_of_products.22), channel_id=1, source_target_pairs={{0,1},{1,0},{2,3},{3,2},{4,5},{5,4},{6,7},{7,6},{8,9},{9,8},{10,11... | collective-permute-start | bytes 9437192 | tf_op jit(solution)/shard_map/ppermute | solution.py:75
  454.2 24.6 %collective-permute-start.43 = (bf16[256,2048]{1,0:T(8,128)(2,1)}, bf16[256,2048]{1,0:T(8,128)(2,1)S(1)}, u32[]{:S(2)}, u32[]{:S(2)}) collective-permute-start(bf16[256,2048]{1,0:T(8,128)(2,1)} %get-tuple-element.160), channel_id=1, source_target_pairs={{0,4},{1,5},{2,6},{3,7},{4,0},{5,1},{6,2},{7,3},{8,12},{9,13},{10,... | collective-permute-start | bytes 3145736 | tf_op jit(solution)/shard_map/ppermute | solution.py:75
  454.8 24.7 %collective-permute-start.42 = (bf16[256,2048]{1,0:T(8,128)(2,1)}, bf16[256,2048]{1,0:T(8,128)(2,1)S(1)}, u32[]{:S(2)}, u32[]{:S(2)}) collective-permute-start(bf16[256,2048]{1,0:T(8,128)(2,1)} %get-tuple-element.160), channel_id=1, source_target_pairs={{0,2},{1,3},{2,0},{3,1},{4,6},{5,7},{6,4},{7,5},{8,10},{9,11},{10,... | collective-permute-start | bytes 3145736 | tf_op jit(solution)/shard_map/ppermute | solution.py:75
  455.5 27.8 %collective-permute-start.44 = (bf16[256,2048]{1,0:T(8,128)(2,1)}, bf16[256,2048]{1,0:T(8,128)(2,1)S(1)}, u32[]{:S(2)}, u32[]{:S(2)}) collective-permute-start(bf16[256,2048]{1,0:T(8,128)(2,1)} %get-tuple-element.160), channel_id=1, source_target_pairs={{0,1},{1,0},{2,3},{3,2},{4,5},{5,4},{6,7},{7,6},{8,9},{9,8},{10,11... | collective-permute-start | bytes 3145736 | tf_op jit(solution)/shard_map/ppermute | solution.py:75
  504.1 60.5 %all-to-all-start.5 = ((bf16[8,64,512]{2,1,0:T(8,128)(2,1)}), bf16[8,64,512]{2,1,0:T(8,128)(2,1)}, u32[]{:S(2)}, u32[]{:S(2)}) async-start(bf16[8,64,512]{2,1,0:T(8,128)(2,1)} %bitcast.218), calls=%async_computation.7 | async-start | bytes 1048576 | tf_op jit(solution)/shard_map/all_to_all | solution.py:148
  508.7 86.9 %collective-permute-start.50 = (bf16[128,2048]{1,0:T(8,128)(2,1)}, bf16[128,2048]{1,0:T(8,128)(2,1)}, u32[]{:S(2)}, u32[]{:S(2)}) collective-permute-start(bf16[128,2048]{1,0:T(8,128)(2,1)} %get-tuple-element.106), channel_id=1, source_target_pairs={{0,2},{1,3},{2,0},{3,1},{4,6},{5,7},{6,4},{7,5},{8,10},{9,11},{10,... | collective-permute-start | bytes 1572872 | tf_op jit(solution)/shard_map/ppermute | solution.py:75
  510.7 58.4 %collective-permute-start.51 = (bf16[128,2048]{1,0:T(8,128)(2,1)}, bf16[128,2048]{1,0:T(8,128)(2,1)}, u32[]{:S(2)}, u32[]{:S(2)}) collective-permute-start(bf16[128,2048]{1,0:T(8,128)(2,1)} %get-tuple-element.108), channel_id=1, source_target_pairs={{0,4},{1,5},{2,6},{3,7},{4,0},{5,1},{6,2},{7,3},{8,12},{9,13},{10,... | collective-permute-start | bytes 1572872 | tf_op jit(solution)/shard_map/ppermute | solution.py:75
  512.2 61.1 %collective-permute-start.53 = (bf16[128,2048]{1,0:T(8,128)(2,1)}, bf16[128,2048]{1,0:T(8,128)(2,1)}, u32[]{:S(2)}, u32[]{:S(2)}) collective-permute-start(bf16[128,2048]{1,0:T(8,128)(2,1)} %get-tuple-element.110), channel_id=1, source_target_pairs={{0,2},{1,3},{2,0},{3,1},{4,6},{5,7},{6,4},{7,5},{8,10},{9,11},{10,... | collective-permute-start | bytes 1572872 | tf_op jit(solution)/shard_map/ppermute | solution.py:75
  512.8 82.8 %collective-permute-start.55 = (bf16[128,2048]{1,0:T(8,128)(2,1)}, bf16[128,2048]{1,0:T(8,128)(2,1)}, u32[]{:S(2)}, u32[]{:S(2)}) collective-permute-start(bf16[128,2048]{1,0:T(8,128)(2,1)} %get-tuple-element.111), channel_id=1, source_target_pairs={{0,4},{1,5},{2,6},{3,7},{4,0},{5,1},{6,2},{7,3},{8,12},{9,13},{10,... | collective-permute-start | bytes 1572872 | tf_op jit(solution)/shard_map/ppermute | solution.py:75
  562.8 25.2 %collective-permute-start.56 = (bf16[256,2048]{1,0:T(8,128)(2,1)}, bf16[256,2048]{1,0:T(8,128)(2,1)}, u32[]{:S(2)}, u32[]{:S(2)}) collective-permute-start(bf16[256,2048]{1,0:T(8,128)(2,1)} %sum_of_products.28), channel_id=1, source_target_pairs={{0,1},{1,0},{2,3},{3,2},{4,5},{5,4},{6,7},{7,6},{8,9},{9,8},{10,11... | collective-permute-start | bytes 3145736 | tf_op jit(solution)/shard_map/ppermute | solution.py:75
  564.6 20.3 %all-to-all-start.4 = ((bf16[8,64,1024]{2,1,0:T(8,128)(2,1)}), bf16[8,64,1024]{2,1,0:T(8,128)(2,1)}, u32[]{:S(2)}, u32[]{:S(2)}) async-start(bf16[8,64,1024]{2,1,0:T(8,128)(2,1)} %bitcast.212), calls=%async_computation.6 | async-start | bytes 2097152 | tf_op jit(solution)/shard_map/all_to_all | solution.py:148
  568.9 165.1 %reduce-scatter.14.cloned.1.call-start = ((), (), s32[]{:S(2)}) async-start(), calls=%async_computation.22 | async-start | bytes 3276800 | tf_op jit(solution)/shard_map/reduce_scatter | solution.py:648
  571.3 24.3 %collective-permute-start.52 = (bf16[128,2048]{1,0:T(8,128)(2,1)}, bf16[128,2048]{1,0:T(8,128)(2,1)}, u32[]{:S(2)}, u32[]{:S(2)}) collective-permute-start(bf16[128,2048]{1,0:T(8,128)(2,1)} %add_convert_fusion.5), channel_id=1, source_target_pairs={{0,2},{1,3},{2,0},{3,1},{4,6},{5,7},{6,4},{7,5},{8,10},{9,11},{10,... | collective-permute-start | bytes 1572872 | tf_op jit(solution)/shard_map/ppermute | solution.py:75
  575.4 20.2 %collective-permute-start.54 = (bf16[128,2048]{1,0:T(8,128)(2,1)}, bf16[128,2048]{1,0:T(8,128)(2,1)}, u32[]{:S(2)}, u32[]{:S(2)}) collective-permute-start(bf16[128,2048]{1,0:T(8,128)(2,1)} %add_convert_fusion.4), channel_id=1, source_target_pairs={{0,4},{1,5},{2,6},{3,7},{4,0},{5,1},{6,2},{7,3},{8,12},{9,13},{10,... | collective-permute-start | bytes 1572872 | tf_op jit(solution)/shard_map/ppermute | solution.py:75
  595.6 48.1 %collective-permute-start.57 = (bf16[768,2048]{1,0:T(8,128)(2,1)}, bf16[768,2048]{1,0:T(8,128)(2,1)}, u32[]{:S(2)}, u32[]{:S(2)}) collective-permute-start(bf16[768,2048]{1,0:T(8,128)(2,1)} %sum_of_products.30), channel_id=1, source_target_pairs={{0,1},{1,0},{2,3},{3,2},{4,5},{5,4},{6,7},{7,6},{8,9},{9,8},{10,11... | collective-permute-start | bytes 9437192 | tf_op jit(solution)/shard_map/ppermute | solution.py:75
  651.9 15.2 %collective-permute-start.59 = (bf16[128,2048]{1,0:T(8,128)(2,1)}, bf16[128,2048]{1,0:T(8,128)(2,1)}, u32[]{:S(2)}, u32[]{:S(2)}) collective-permute-start(bf16[128,2048]{1,0:T(8,128)(2,1)} %get-tuple-element.125), channel_id=1, source_target_pairs={{0,4},{1,5},{2,6},{3,7},{4,0},{5,1},{6,2},{7,3},{8,12},{9,13},{10,... | collective-permute-start | bytes 1572872 | tf_op jit(solution)/shard_map/ppermute | solution.py:75
  655.4 15.2 %collective-permute-start.61 = (bf16[128,2048]{1,0:T(8,128)(2,1)}, bf16[128,2048]{1,0:T(8,128)(2,1)}, u32[]{:S(2)}, u32[]{:S(2)}) collective-permute-start(bf16[128,2048]{1,0:T(8,128)(2,1)} %get-tuple-element.127), channel_id=1, source_target_pairs={{0,2},{1,3},{2,0},{3,1},{4,6},{5,7},{6,4},{7,5},{8,10},{9,11},{10,... | collective-permute-start | bytes 1572872 | tf_op jit(solution)/shard_map/ppermute | solution.py:75
  659.6 21.8 %all-to-all-start.7 = ((bf16[8,64,1024]{2,1,0:T(8,128)(2,1)}), bf16[8,64,1024]{2,1,0:T(8,128)(2,1)S(1)}, u32[]{:S(2)}, u32[]{:S(2)}) async-start(bf16[8,64,1024]{2,1,0:T(8,128)(2,1)} %bitcast.220), calls=%async_computation.12 | async-start | bytes 2097152 | tf_op jit(solution)/shard_map/all_to_all | solution.py:148
  663.6 29.5 %collective-permute-start.58 = (bf16[128,2048]{1,0:T(8,128)(2,1)S(1)}, bf16[128,2048]{1,0:T(8,128)(2,1)}, u32[]{:S(2)}, u32[]{:S(2)}) collective-permute-start(bf16[128,2048]{1,0:T(8,128)(2,1)S(1)} %copy-done.45), channel_id=1, source_target_pairs={{0,2},{1,3},{2,0},{3,1},{4,6},{5,7},{6,4},{7,5},{8,10},{9,11},{10,... | collective-permute-start | bytes 1572872 | tf_op jit(solution)/shard_map/ppermute | solution.py:75
  665.6 27.4 %collective-permute-start.63 = (bf16[128,2048]{1,0:T(8,128)(2,1)S(1)}, bf16[128,2048]{1,0:T(8,128)(2,1)}, u32[]{:S(2)}, u32[]{:S(2)}) collective-permute-start(bf16[128,2048]{1,0:T(8,128)(2,1)S(1)} %copy-done.47), channel_id=1, source_target_pairs={{0,4},{1,5},{2,6},{3,7},{4,0},{5,1},{6,2},{7,3},{8,12},{9,13},{10,... | collective-permute-start | bytes 1572872 | tf_op jit(solution)/shard_map/ppermute | solution.py:75
  669.1 34.1 %collective-permute-start.60 = (bf16[128,2048]{1,0:T(8,128)(2,1)}, bf16[128,2048]{1,0:T(8,128)(2,1)}, u32[]{:S(2)}, u32[]{:S(2)}) collective-permute-start(bf16[128,2048]{1,0:T(8,128)(2,1)} %add_convert_fusion.3), channel_id=1, source_target_pairs={{0,2},{1,3},{2,0},{3,1},{4,6},{5,7},{6,4},{7,5},{8,10},{9,11},{10,... | collective-permute-start | bytes 1572872 | tf_op jit(solution)/shard_map/ppermute | solution.py:75
  672.6 30.6 %collective-permute-start.62 = (bf16[128,2048]{1,0:T(8,128)(2,1)}, bf16[128,2048]{1,0:T(8,128)(2,1)}, u32[]{:S(2)}, u32[]{:S(2)}) collective-permute-start(bf16[128,2048]{1,0:T(8,128)(2,1)} %add_convert_fusion.2), channel_id=1, source_target_pairs={{0,4},{1,5},{2,6},{3,7},{4,0},{5,1},{6,2},{7,3},{8,12},{9,13},{10,... | collective-permute-start | bytes 1572872 | tf_op jit(solution)/shard_map/ppermute | solution.py:75
  (123 other events, 1328.8 us)
Sparse Core Ops, SparseCore 0:
  24.1 36.4 all-gather.4
  62.2 26.7 all-gather.6
  91.2 114.8 all-gather.8
  224.1 121.3 all-gather.10
  348.3 42.0 reduce-scatter.5
  392.6 76.0 reduce-scatter.7
  471.0 44.3 reduce-scatter.9
  517.9 76.0 reduce-scatter.11
  639.7 57.2 reduce-scatter.13

commit v3 on v2

--- a/solution.py
+++ b/solution.py
@@ -13,6 +13,10 @@
 FACTOR = HEAD_SIZE ** (-0.5)
 
 NO_COST = pl.CostEstimate(flops=0, bytes_accessed=0, transcendentals=0)
+
+
+def cost(flops, share):
+    return pl.CostEstimate(flops=int(flops * share), bytes_accessed=0, transcendentals=0)
 
 
 epsilon = 1e-06
@@ -60,71 +64,129 @@
     return fence((value,), *earlier)[0]
 
 
-RELATIVE = (0, 2, 4, 1, 3, 5, 6, 7)
+def stack_kernel(*refs):
+    for k, ref in enumerate(refs[:-1]):
+
+        @pl.when(pl.program_id(0) == k)
+        def _():
+            refs[-1][...] = ref[...]
+
+
+def stack(pieces):
+    if len(pieces) == 1:
+        return pieces[0]
+    shape = pieces[0].shape
+    return pl.pallas_call(
+        stack_kernel,
+        grid=(len(pieces),),
+        in_specs=[pl.BlockSpec(shape, lambda i: (0, 0))] * len(pieces),
+        out_specs=pl.BlockSpec(shape, lambda i: (i, 0)),
+        out_shape=jax.ShapeDtypeStruct((len(pieces) * shape[0], shape[1]), pieces[0].dtype),
+        compiler_params=pltpu.CompilerParams(vmem_limit_bytes=32 * 2**20),
+        cost_estimate=cost(10**9, len(pieces)),
+        name="stack",
+    )(*pieces)
+
+
+RELATIVE = (0, 2, 4, 6, 1, 3, 5, 7)
 
 
 def place_of(own, index, parts):
     if parts != 8:
         return index
     relative = lax.bitwise_xor(own, index)
-    near = lax.shift_right_logical(relative, 1) + 3 * lax.bitwise_and(relative, 1)
-    return jnp.where(relative < 6, near, relative)
+    return lax.bitwise_or(
+        lax.shift_right_logical(relative, 1), lax.shift_left(lax.bitwise_and(relative, 1), 2)
+    )
 
 
 def hop(value, bit):
     return lax.ppermute(value, "ctx", [(i, i ^ bit) for i in range(lax.axis_size("ctx"))])
 
 
-def gather_tokens(value):
-    return gather_tokens_and_start(value)[0]
-
-
-def gather_tokens_and_start(value):
+def halves_kernel(by_x_ref, by_y_ref, *refs):
+    refs[-2][...] = by_x_ref[...]
+    refs[-1][...] = by_y_ref[...]
+
+
+def halves(by_x, by_y, before):
+    rows, width = by_x.shape
+    half = (rows // 2, width)
+    return pl.pallas_call(
+        halves_kernel,
+        grid=(1,),
+        in_specs=[pl.BlockSpec(half, lambda i: (0, 0)), pl.BlockSpec(half, lambda i: (1, 0))]
+        + [pl.BlockSpec(memory_space=pl.ANY)] * len(before),
+        out_specs=[pl.BlockSpec(half, lambda i: (0, 0))] * 2,
+        out_shape=[jax.ShapeDtypeStruct(half, by_x.dtype)] * 2,
+        cost_estimate=cost(10**9, 1),
+        name="halves",
+    )(by_x, by_y, *before)
+
+
+def gather_pieces(value, middle=()):
     if lax.axis_size("ctx") != 8:
-        whole = lax.all_gather(value, "ctx", axis=0)
-        return whole, (whole, whole)
-    half = value.shape[0] // 2
+        whole = lax.all_gather(value, "ctx", axis=0, tiled=True)
+        return (whole,), (whole,)
     by_x, by_y = hop(value, 2), hop(value, 4)
-    far = jnp.concatenate([hop(by_x[:half], 4), hop(by_y[half:], 2)], axis=0)
-    whole = jnp.stack(
-        [value, by_x, by_y, hop(value, 1), hop(by_x, 1), hop(by_y, 1), far, hop(far, 1)], axis=0
-    )
-    return whole, (by_x, by_y)
-
-
-def partial_products(product, tokens):
+    first, second = halves(by_x, by_y, middle)
+    far = stack((hop(first, 4), hop(second, 2)))
+    others = [hop(piece, 1) for piece in (value, by_x, by_y)]
+    return (value, by_x, by_y, far, *others, hop(far, 1)), (by_x, by_y)
+
+
+def partial_products(product, tokens, before=()):
     parts = lax.axis_size("ctx")
     if parts != 8:
-        return product(0, parts, [(parts * tokens, bf16)], None, ())
+        return product(0, parts, [(parts * tokens, bf16)], None, before)
     half = (tokens // 2, bf16)
-    (far_other,) = product(7, 1, [(tokens, bf16)], None, ())
-    far = product(6, 1, [half] * 2, hop(far_other, 1), ())
-    (near_other,) = product(3, 3, [(3 * tokens, bf16)], None, (far[0],))
-    own, *near = product(0, 3, [(tokens, f32)] + [half] * 4, hop(near_other, 1), ())
+    near_other, far_other = product(4, 4, [(3 * tokens, bf16), (tokens, bf16)], None, before)
+    far_other = hop(far_other, 1)
+    near_other = after(near_other, far_other)
+    far = product(3, 1, [half] * 2, far_other, ())
+    own, *near = product(
+        0, 3, [(tokens, f32)] + [(tokens, bf16)] * 2, hop(near_other, 1), (far[0],)
+    )
     return (own, *near, *far)
 
 
-def finish_scatter(sums, tokens):
+def far_step(sums, far_after=(), near_after=()):
+    if lax.axis_size("ctx") != 8:
+        return fence(sums, *far_after, *near_after) if far_after or near_after else sums
+    own, *near, far_first, far_last = sums
+    if far_after:
+        far_first, far_last = fence((far_first, far_last), *far_after)
+    if near_after:
+        near = fence(near, *near_after)
+    from_x, from_y = hop(far_first, 2), hop(far_last, 4)
+    by_x, by_y = near
+    rows = by_x.shape[0] // 2
+    by_x = by_x + jnp.pad(from_y, ((rows, 0), (0, 0)))
+    by_y = by_y + jnp.pad(from_x, ((0, rows), (0, 0)))
+    return own, by_x, by_y
+
+
+def near_hops(sums):
     if lax.axis_size("ctx") != 8:
         (whole,) = sums
-        return lax.psum_scatter(whole, "ctx", scatter_dimension=0, tiled=True).astype(f32)
-    own, x_first, x_last, y_first, y_last, far_first, far_last = sums
-    from_x, from_y = hop(far_first, 2), hop(far_last, 4)
-    x_last = (x_last.astype(f32) + from_y.astype(f32)).astype(bf16)
-    y_first = (y_first.astype(f32) + from_x.astype(f32)).astype(bf16)
-    x_part = jnp.concatenate([hop(x_first, 2), hop(x_last, 2)], axis=0)
-    y_part = jnp.concatenate([hop(y_first, 4), hop(y_last, 4)], axis=0)
-    return own + x_part.astype(f32) + y_part.astype(f32)
+        return (lax.psum_scatter(whole, "ctx", scatter_dimension=0, tiled=True),)
+    own, by_x, by_y = sums
+    return own, hop(by_x, 2), hop(by_y, 4)
+
+
+def near_step(sums):
+    return sum(part.astype(f32) for part in near_hops(sums))
 
 
 def sum_everywhere(value):
     if lax.axis_size("ctx") != 8 or lax.axis_size("dp") != 4:
         return lax.psum(value, ("dp", "ctx"))
-    for bit in (1, 2, 4):
-        value = value + hop(value, bit)
-    for bit in (1, 2):
-        value = value + lax.ppermute(value, "dp", [(i, i ^ bit) for i in range(4)])
-    return value
+    value = value + hop(value, 1)
+    value = value + (hop(value, 2) + hop(value, 4) + hop(value, 6))
+    shifted = [
+        lax.ppermute(value, "dp", [(i, i ^ bits) for i in range(4)]) for bits in (1, 2, 3)
+    ]
+    return (value + shifted[0]) + (shifted[1] + shifted[2])
 
 
 def spread_columns(packed):
@@ -143,17 +205,63 @@
 
 
 def collect_columns(block):
-    parts = lax.axis_size("ctx")
-    columns = block.shape[1]
-    out = lax.all_to_all(block, "ctx", split_axis=0, concat_axis=1, tiled=True)
-    return out.reshape(out.shape[0], parts, columns).astype(f32)
-
-
-def collect_early(gradient):
-    groups, parts = lax.axis_size("dp"), lax.axis_size("ctx")
-    block = gradient.reshape(groups, parts, -1, gradient.shape[1])
-    block = lax.all_to_all(block, "ctx", split_axis=1, concat_axis=1, tiled=True)
-    return block.reshape(-1, gradient.shape[1])
+    return lax.all_to_all(block, "ctx", split_axis=0, concat_axis=0, tiled=True)
+
+
+def place_units_kernel(first_ref, last_ref, *out_refs):
+    units = first_ref.shape[1] // 3
+    for which, out_ref in enumerate(out_refs):
+        for half, ref in enumerate((first_ref, last_ref)):
+            out_ref[:, half * units : (half + 1) * units] = ref[
+                :, which * units : (which + 1) * units
+            ].astype(f32)
+
+
+def place_units(first, last, parts):
+    rows, columns = first.shape[0] // parts, first.shape[1]
+    units = columns // 3
+    return pl.pallas_call(
+        place_units_kernel,
+        grid=(parts,),
+        in_specs=[pl.BlockSpec((rows, columns), lambda i: (i, 0))] * 2,
+        out_specs=[pl.BlockSpec((rows, 2 * units), lambda i: (0, i))] * 3,
+        out_shape=[jax.ShapeDtypeStruct((rows, 2 * units * parts), f32)] * 3,
+        compiler_params=pltpu.CompilerParams(vmem_limit_bytes=16 * 2**20),
+        cost_estimate=cost(10**7, 800),
+        name="place_units",
+    )(first, last)
+
+
+def place_heads_kernel(parts, share, block_ref, query_ref, key_ref, value_ref, out_ref):
+    rows = query_ref.shape[0]
+    width = query_ref.shape[1] // parts
+    for part in range(parts):
+        block = block_ref[part * rows : (part + 1) * rows, :].astype(f32)
+        here = slice(part * width, (part + 1) * width)
+        query_ref[:, here] = block[:, :width]
+        out_ref[:, here] = block[:, width + 2 * HEAD_SIZE :]
+        head = part // share
+        for ref, start in ((key_ref, width), (value_ref, width + HEAD_SIZE)):
+            columns = slice(head * HEAD_SIZE, (head + 1) * HEAD_SIZE)
+            piece = block[:, start : start + HEAD_SIZE]
+            ref[:, columns] = piece if part % share == 0 else ref[:, columns] + piece
+
+
+def place_heads(block, parts, share):
+    rows = block.shape[0] // parts
+    width = (block.shape[1] - 2 * HEAD_SIZE) // 2 * parts
+    whole = pl.BlockSpec(memory_space=pltpu.VMEM)
+    shapes = [(rows, width), (rows, parts // share * HEAD_SIZE)]
+    shapes += [shapes[1], shapes[0]]
+    return pl.pallas_call(
+        functools.partial(place_heads_kernel, parts, share),
+        in_specs=[whole],
+        out_specs=[whole] * 4,
+        out_shape=[jax.ShapeDtypeStruct(shape, f32) for shape in shapes],
+        compiler_params=pltpu.CompilerParams(vmem_limit_bytes=16 * 2**20),
+        cost_estimate=cost(10**7, 400),
+        name="place_heads",
+    )(block)
 
 
 def heads_to_columns(block, heads):
@@ -223,11 +331,12 @@
 
 
 def attend_kernel(
-    blocks, slots, heads, chunk,
+    row, blocks, slots, heads, chunk,
     base_ref, len_ref, q_ref, kv_ref, qg_ref, kg_ref, cos_ref, sin_ref,
-    o_ref, lse_ref, k_all, v_t,
+    *refs,
 ):
-    row, query_block = pl.program_id(0), pl.program_id(1)
+    o_ref, lse_ref, k_all, v_t = refs[-4:]
+    query_block = pl.program_id(0)
     base, length = base_ref[0], len_ref[row]
 
     @pl.when(query_block == 0)
@@ -279,20 +388,18 @@
 
 
 def attend_back_kernel(
-    blocks, slots, heads, chunk,
+    row, blocks, slots, heads, chunk,
     base_ref, len_ref, q_ref, kv_ref, qg_ref, kg_ref, cos_ref, sin_ref, o_ref, do_ref, lse_ref,
-    dq_ref, dkv_ref, dqg_ref, dkg_ref, k_all, v_all, k_t, dk_all, dv_all,
+    *refs,
 ):
-    row, query_block = pl.program_id(0), pl.program_id(1)
+    dq_ref, dkv_ref, dqg_ref, dkg_ref, k_all, v_all, k_t, dk_all, dv_all = refs[-9:]
+    query_block = pl.program_id(0)
     base, length = base_ref[0], len_ref[row]
 
-    @pl.when((row == 0) & (query_block == 0))
+    @pl.when(query_block == 0)
     def _():
         dqg_ref[...] = jnp.zeros_like(dqg_ref)
         dkg_ref[...] = jnp.zeros_like(dkg_ref)
-
-    @pl.when(query_block == 0)
-    def _():
         for j in range(blocks):
             at = place_of(base, jnp.int32(j), blocks)
             here = slice(j * slots, (j + 1) * slots)
@@ -350,14 +457,14 @@
             dkv_ref[at, 0] = jnp.concatenate([raw_term.T, dv_all[here, :]], axis=1).astype(bf16)
 
 
-def attention_specs(blocks, slots, width, total):
-    own = lambda r, i, base, lens: (place_of(base[0], i, blocks), r, 0, 0)
-    constant = lambda r, i, base, lens: (0, 0)
+def attention_specs(row, blocks, slots, width, total):
+    own = lambda i, base, lens: (place_of(base[0], i, blocks), row, 0, 0)
+    constant = lambda i, base, lens: (0, 0)
     both = 2 * HEAD_SIZE
     return (
         pl.BlockSpec((1, 1, slots, width), own),
-        pl.BlockSpec((blocks, 1, slots, both), lambda r, i, base, lens: (0, r, 0, width // both)),
-        pl.BlockSpec((blocks, 1, slots, both), lambda r, i, base, lens: (0, r, 0, 0)),
+        pl.BlockSpec((blocks, 1, slots, both), lambda i, base, lens: (0, row, 0, width // both)),
+        pl.BlockSpec((blocks, 1, slots, both), lambda i, base, lens: (0, row, 0, 0)),
         pl.BlockSpec((HEAD_SIZE, 1), constant),
         pl.BlockSpec((HEAD_SIZE // 2, total), constant),
         pl.BlockSpec((1, 1, 1, width // HEAD_SIZE * slots), own),
@@ -365,20 +472,22 @@
     )
 
 
-def attend(base, lengths, raw, query_gain, key_gain, cosine, sine):
+def attend(row, previous, base, lengths, raw, query_gain, key_gain, cosine, sine):
     blocks, rows, slots, columns = raw.shape
     width = columns - 2 * HEAD_SIZE
     heads = width // HEAD_SIZE
     total = blocks * slots
     query_spec, raw_key_spec, _, gain_spec, table_spec, lse_spec, _ = attention_specs(
-        blocks, slots, width, total
-    )
-    return pl.pallas_call(
-        functools.partial(attend_kernel, blocks, slots, heads, 2 * slots),
+        row, blocks, slots, width, total
+    )
+    operands = (base, lengths, raw, raw, query_gain, key_gain, cosine, sine)
+    return pl.pallas_call(
+        functools.partial(attend_kernel, row, blocks, slots, heads, 2 * slots),
         grid_spec=pltpu.PrefetchScalarGridSpec(
             num_scalar_prefetch=2,
-            grid=(rows, blocks),
-            in_specs=[query_spec, raw_key_spec, gain_spec, gain_spec, table_spec, table_spec],
+            grid=(blocks,),
+            in_specs=[query_spec, raw_key_spec, gain_spec, gain_spec, table_spec, table_spec]
+            + [pl.BlockSpec(memory_space=pl.ANY)] * len(previous),
             out_specs=[query_spec, lse_spec],
             scratch_shapes=[
                 pltpu.VMEM((total, HEAD_SIZE), bf16),
@@ -389,29 +498,33 @@
             jax.ShapeDtypeStruct((blocks, rows, slots, width), bf16),
             jax.ShapeDtypeStruct((blocks, rows, 1, heads * slots), f32),
         ],
+        input_output_aliases={len(operands) + i: i for i in range(len(previous))},
         compiler_params=pltpu.CompilerParams(vmem_limit_bytes=32 * 2**20),
-        cost_estimate=NO_COST,
+        cost_estimate=cost(2 * HEAD_SIZE * heads * total * total, 24),
         name="attend",
-    )(base, lengths, raw, raw, query_gain, key_gain, cosine, sine)
+    )(*operands, *previous)
 
 
 def attend_back(
-    base, lengths, raw, query_gain, key_gain, cosine, sine, attended, gradient, log_total
+    row, previous, base, lengths, raw, query_gain, key_gain, cosine, sine, attended, gradient, log_total
 ):
     blocks, rows, slots, columns = raw.shape
     width = columns - 2 * HEAD_SIZE
     heads = width // HEAD_SIZE
     total = blocks * slots
     query_spec, raw_key_spec, key_spec, gain_spec, table_spec, lse_spec, sum_spec = (
-        attention_specs(blocks, slots, width, total)
-    )
-    return pl.pallas_call(
-        functools.partial(attend_back_kernel, blocks, slots, heads, 2 * slots),
+        attention_specs(row, blocks, slots, width, total)
+    )
+    operands = (base, lengths, raw, raw, query_gain, key_gain, cosine, sine)
+    operands += (attended, gradient, log_total)
+    return pl.pallas_call(
+        functools.partial(attend_back_kernel, row, blocks, slots, heads, 2 * slots),
         grid_spec=pltpu.PrefetchScalarGridSpec(
             num_scalar_prefetch=2,
-            grid=(rows, blocks),
+            grid=(blocks,),
             in_specs=[query_spec, raw_key_spec, gain_spec, gain_spec, table_spec, table_spec]
-            + [query_spec, query_spec, lse_spec],
+            + [query_spec, query_spec, lse_spec]
+            + [pl.BlockSpec(memory_space=pl.ANY)] * len(previous),
             out_specs=[query_spec, key_spec, sum_spec, sum_spec],
             scratch_shapes=[
                 pltpu.VMEM((total, HEAD_SIZE), bf16),
@@ -427,10 +540,11 @@
             jax.ShapeDtypeStruct((HEAD_SIZE, 128), f32),
             jax.ShapeDtypeStruct((HEAD_SIZE, 128), f32),
         ],
+        input_output_aliases={len(operands) + i: i for i in range(len(previous))},
         compiler_params=pltpu.CompilerParams(vmem_limit_bytes=32 * 2**20),
-        cost_estimate=NO_COST,
+        cost_estimate=cost(5 * HEAD_SIZE * heads * total * total, 16),
         name="attend_back",
-    )(base, lengths, raw, raw, query_gain, key_gain, cosine, sine, attended, gradient, log_total)
+    )(*operands, *previous)
 
 
 def feed_kernel(hidden_ref, cotangent_ref, weight_ref, inner_ref, grad_ref):
@@ -466,9 +580,33 @@
             jax.ShapeDtypeStruct((count, 2 * units), bf16),
         ],
         compiler_params=pltpu.CompilerParams(vmem_limit_bytes=48 * 2**20),
-        cost_estimate=NO_COST,
+        cost_estimate=cost(6 * count * width * units, 1.7),
         name="feed_forward",
     )(hidden, cotangents, weights)
+
+
+def feed_gradient_kernel(hidden_ref, cotangent_ref, grad_ref, inner_ref, out_ref):
+    split = grad_ref.shape[1]
+    out_ref[:, :split] = dot_tn(hidden_ref[...], grad_ref[...]).astype(bf16)
+    out_ref[:, split:] = dot_tn(cotangent_ref[...], inner_ref[...]).astype(bf16)
+
+
+def feed_gradient(hidden, cotangents, grad, inner):
+    count, width = hidden.shape
+    tile = 256
+    columns = pl.BlockSpec((count, tile), lambda i: (0, i))
+    total = grad.shape[1] + inner.shape[1]
+    return pl.pallas_call(
+        feed_gradient_kernel,
+        grid=(width // tile,),
+        in_specs=[columns, columns]
+        + [pl.BlockSpec(v.shape, lambda i: (0, 0)) for v in (grad, inner)],
+        out_specs=pl.BlockSpec((tile, total), lambda i: (i, 0)),
+        out_shape=jax.ShapeDtypeStruct((width, total), bf16),
+        compiler_params=pltpu.CompilerParams(vmem_limit_bytes=48 * 2**20),
+        cost_estimate=cost(2 * count * width * total, 1.6),
+        name="feed_gradient",
+    )(hidden, cotangents, grad, inner)
 
 
 def product_kernel(count, adds, outs, *refs):
@@ -482,7 +620,7 @@
         start += out_ref.shape[0]
 
 
-def sum_of_products(lefts, weights, column, tokens, first, count, splits, add, before):
+def sum_of_products(share, lefts, weights, column, tokens, first, count, splits, add, before):
     rows = count * tokens
     width = weights[0].shape[0]
     tile = 512
@@ -502,7 +640,7 @@
         out_specs=[pl.BlockSpec((r, tile), lambda i: (0, i)) for r, _ in splits],
         out_shape=[jax.ShapeDtypeStruct((r, width), dtype) for r, dtype in splits],
         compiler_params=pltpu.CompilerParams(vmem_limit_bytes=48 * 2**20),
-        cost_estimate=NO_COST,
+        cost_estimate=cost(2 * rows * width * sum(v.shape[1] for v in lefts), share),
         name="sum_of_products",
     )(*operands)
 
@@ -558,79 +696,98 @@
     flat = inputs.reshape(tokens, width).astype(f32)
     first_scale = rms_scale(flat)
     normed = flat * first_scale
-    hidden, hidden_start = gather_tokens_and_start((normed * attention_gain).astype(bf16))
-    hidden = hidden.reshape(all_tokens, width)
+    hidden_pieces, hidden_start = gather_pieces((normed * attention_gain).astype(bf16))
+    hidden = stack(hidden_pieces)
     first_block = spread_columns(after(feed_packs[0], out_block, *hidden_start))
     qkv_full = gather_rows(qkv_block)
     out_full = gather_rows(out_block)
     first_full = gather_rows(first_block)
-    hidden = after(hidden, first_block)
-
-    raw = dot_nn(hidden, qkv_full).reshape(parts, rows, slots, query_cols + 2 * HEAD_SIZE)
+
+    raw = jnp.concatenate([dot_nn(piece, qkv_full) for piece in hidden_pieces], axis=0)
     cotangent_flat = cotangent.reshape(tokens, width)
-    cotangents, cotangents_start = gather_tokens_and_start(after(cotangent_flat, first_block))
-    cotangents = cotangents.reshape(all_tokens, width)
+    cotangent_pieces, cotangents_start = gather_pieces(after(cotangent_flat, first_block))
+    cotangents = stack(cotangent_pieces)
+    raw = after(raw, *cotangents_start).reshape(parts, rows, slots, query_cols + 2 * HEAD_SIZE)
     last_block = spread_columns(after(feed_packs[1], *cotangents_start))
     cosine, sine = [
         t.T for t in rotary_tables(jnp.arange(parts * slots, dtype=jnp.int32), HEAD_SIZE)
     ]
     base_array = base.reshape(1)
     gains = [g.astype(f32).reshape(HEAD_SIZE, 1) for g in (query_gain, key_gain)]
-    attended, log_total = attend(base_array, lengths, raw, *gains, cosine, sine)
+    results = ()
+    for row in range(rows):
+        if row == rows - 1:
+            results = fence(results, last_block) if results else results
+        results = attend(row, results, base_array, lengths, raw, *gains, cosine, sine)
+    attended, log_total = results
     attended_rows = attended.reshape(all_tokens, query_cols)
     sums = partial_products(
-        functools.partial(sum_of_products, [attended_rows], [out_full], 0, tokens), tokens
-    )
-    mixed = flat + finish_scatter(fence(sums, last_block), tokens)
+        functools.partial(sum_of_products, 2.4, [attended_rows], [out_full], 0, tokens), tokens
+    )
+    mixed = flat + near_step(far_step(sums, (), cotangent_pieces[-1:]))
 
     second_scale = rms_scale(mixed)
     normed_again = mixed * second_scale
-    hidden_again = gather_tokens(
-        after((normed_again * feedforward_gain).astype(bf16), first_full)
-    ).reshape(all_tokens, width)
+    pieces, _ = gather_pieces((normed_again * feedforward_gain).astype(bf16))
+    hidden_again = after(stack(pieces), first_full)
     last_full = gather_rows(after(last_block, first_full))
     fulls = [first_full, last_full]
     inners, grads, partials = [], [], []
     for which in range(2):
         if which == 1:
-            fulls[1] = after(last_full, *partials[0])
+            fulls[1] = after(last_full, partials[0])
         inner, grad = feed_forward(hidden_again, cotangents, fulls[which])
         inners.append(inner)
         grads.append(grad)
-        partials.append(
-            (dot_tn(hidden_again, grad).astype(bf16), dot_tn(cotangents, inner).astype(bf16))
-        )
-    first_gradients, last_gradients = [[scatter_rows(p) for p in pair] for pair in partials]
+        partials.append(feed_gradient(hidden_again, cotangents, grad, inner))
+    first_gradient = scatter_rows(partials[0])
+    last_gradient = scatter_rows(after(partials[1], first_gradient))
     sums = partial_products(
-        functools.partial(sum_of_products, grads, fulls, 0, tokens), tokens
-    )
-    grad_hidden_again = after(finish_scatter(sums, tokens), first_gradients[1])
+        functools.partial(sum_of_products, 0, grads, fulls, 0, tokens), tokens
+    )
+    feed_sums = partial_products(
+        functools.partial(sum_of_products, 2.4, inners, fulls, 2, tokens), tokens, (sums[0],)
+    )
+    grad_hidden_again = after(near_step(far_step(sums)), feed_sums[-1])
     feedforward_gain_local = jnp.sum(grad_hidden_again * normed_again, axis=0)
     scaled_again = grad_hidden_again * feedforward_gain
     grad_mixed = cotangent_flat.astype(f32) + second_scale * (
         scaled_again - normed_again * jnp.mean(scaled_again * normed_again, axis=-1, keepdims=True)
     )
 
-    grad_branch = gather_tokens(grad_mixed.astype(bf16)).reshape(all_tokens, width)
-    grad_branch = after(grad_branch, first_gradients[0])
-    attended_gradient = dot_nn(grad_branch, out_full).astype(bf16)
-    feed_sums = partial_products(
-        functools.partial(sum_of_products, inners, fulls, 2, tokens), tokens
-    )
-    attended_gradient = after(attended_gradient, *feed_sums)
-    feed_out = finish_scatter(fence(feed_sums, grad_branch), tokens)
+    pieces, _ = gather_pieces(grad_mixed.astype(bf16), (feed_sums[0], first_gradient))
+    grad_branch = stack(pieces)
+    attended_gradient = jnp.concatenate(
+        [dot_nn(piece, out_full).astype(bf16) for piece in pieces], axis=0
+    )
+    first_collected = collect_columns(after(first_gradient, attended_gradient))
+    feed_sums = far_step(feed_sums, (attended_gradient,))
+    feed_parts = near_hops(feed_sums)
+    feed_out = sum(part.astype(f32) for part in feed_parts)
     outputs = (mixed + feed_out).astype(bf16).reshape(rows, slots, width)
-    grad_queries, grad_keys_values, query_gain_sums, key_gain_sums = attend_back(
-        base_array,
-        lengths,
-        raw,
-        *gains,
-        cosine,
-        sine,
-        attended,
-        attended_gradient.reshape(parts, rows, slots, query_cols),
-        log_total,
-    )
+    attended_gradient = attended_gradient.reshape(parts, rows, slots, query_cols)
+    grad_queries_keys_values, gain_sums = (), []
+    for row in range(rows):
+        if row == rows - 1 and grad_queries_keys_values:
+            grad_queries_keys_values = fence(
+                grad_queries_keys_values, first_collected, *feed_sums[1:]
+            )
+        *grad_queries_keys_values, query_gain_sums, key_gain_sums = attend_back(
+            row,
+            tuple(grad_queries_keys_values),
+            base_array,
+            lengths,
+            raw,
+            *gains,
+            cosine,
+            sine,
+            attended,
+            attended_gradient,
+            log_total,
+        )
+        gain_sums.append((query_gain_sums, key_gain_sums))
+    grad_queries, grad_keys_values = grad_queries_keys_values
+    query_gain_sums, key_gain_sums = [sum(g) for g in zip(*gain_sums)]
     query_gain_local, key_gain_local = query_gain_sums.sum(axis=1), key_gain_sums.sum(axis=1)
     grad_raw = jnp.concatenate(
         [
@@ -639,47 +796,26 @@
         ],
         axis=1,
     )
+    grad_raw = after(grad_raw, *feed_parts[1:])
     attention_partial = jnp.concatenate(
-        [dot_tn(hidden, grad_raw), dot_tn(grad_branch, attended_rows)], axis=1
+        [dot_tn(hidden, grad_raw), dot_tn(grad_branch, after(attended_rows, grad_raw))], axis=1
     ).astype(bf16)
-    first_collected = [collect_columns(after(g, attended_gradient)) for g in first_gradients]
-    attention_partial = after(attention_partial, feed_out, *first_collected)
-    early = collect_early(after(attention_partial, last_gradients[1]))
-    attention_collected = lax.psum_scatter(
-        after(early, last_gradients[0]), "dp", scatter_dimension=0, tiled=True
-    )
-    attention_collected = jnp.swapaxes(
-        attention_collected.reshape(parts, weight_rows, -1), 0, 1
-    ).astype(f32)
+    attention_gradient = scatter_rows(after(attention_partial, last_gradient))
+    attention_collected = collect_columns(attention_gradient)
+    query_weight_gradient, key_weight_gradient, value_weight_gradient, out_weight_gradient = (
+        place_heads(attention_collected, parts, share)
+    )
     sums = partial_products(
-        functools.partial(sum_of_products, [grad_raw], [qkv_full], 0, tokens), tokens
-    )
-    grad_hidden = finish_scatter(fence(sums, early), tokens)
-    collected = [
-        first_collected,
-        [collect_columns(g) for g in last_gradients],
-    ]
-    gate_weight_gradient, up_weight_gradient = [
-        jnp.concatenate([c[0][:, :, start : start + units] for c in collected], axis=2).reshape(
-            weight_rows, parts * feed
-        )
-        for start in (0, units)
-    ]
-    down_weight_gradient = jnp.concatenate([c[1] for c in collected], axis=2).reshape(
-        weight_rows, parts * feed
-    )
-    query_weight_gradient = attention_collected[:, :, :query_cols].reshape(weight_rows, -1)
-    key_weight_gradient, value_weight_gradient = [
-        attention_collected[:, :, start : start + HEAD_SIZE]
-        .reshape(weight_rows, KEY_VALUE_HEADS, share, HEAD_SIZE)
-        .sum(axis=2)
-        .reshape(weight_rows, KEY_VALUE_HEADS * HEAD_SIZE)
-        for start in (query_cols, query_cols + HEAD_SIZE)
-    ]
-
-    out_weight_gradient = attention_collected[:, :, query_cols + 2 * HEAD_SIZE :].reshape(
-        weight_rows, -1
-    )
+        functools.partial(sum_of_products, 2.4, [grad_raw], [qkv_full], 0, tokens),
+        tokens,
+        (attention_partial,),
+    )
+    last_collected = collect_columns(last_gradient)
+    grad_hidden = near_step(far_step(sums, (feed_out, last_collected), (feed_out,)))
+    gate_weight_gradient, up_weight_gradient, down_weight_gradient = place_units(
+        first_collected, last_collected, parts
+    )
+    grad_hidden = after(grad_hidden, attention_gradient)
 
     attention_gain_local = jnp.sum(grad_hidden * normed, axis=0)
     scaled_first = grad_hidden * attention_gain
@@ -689,8 +825,11 @@
         * (scaled_first - normed * jnp.mean(scaled_first * normed, axis=-1, keepdims=True))
     ).astype(bf16)
     gain_sums = sum_everywhere(
-        jnp.concatenate(
-            [attention_gain_local, feedforward_gain_local, query_gain_local, key_gain_local]
+        after(
+            jnp.concatenate(
+                [attention_gain_local, feedforward_gain_local, query_gain_local, key_gain_local]
+            ),
+            attention_collected,
         )
     )
     attention_gain_gradient, feedforward_gain_gradient = gain_sums[:width], gain_sums[width : 2 * width]

time: 754 us -> 727 us (0.964)
  Pallas kernels: 175 us -> 239 us
  blocking collectives: 48.2 us -> 13.5 us
  local copies, waits for them, and re-layouts: 115 us -> 80.6 us
  matrix products: 71.1 us -> 46.9 us
  waiting for transfers between devices: 175 us -> 198 us
  starting transfers between devices: 89.9 us -> 68.8 us
    pallas_call x2 -> x20, Pallas kernels: 54.8 us -> 129 us  [the longest x2 37.1 us: feed_gradient(): pl.pallas_call(feed_gradient_kernel, grid=(width // tile,), in_specs=[col...]
    dot_general x6 -> x2, matrix products: 57 us -> 14.3 us  [dot_tn(): lax.dot_general(left, right, (((0,), (0,)), ((), ())), preferred_element_...]
    all_to_all x1 -> x0, blocking collectives: 34.7 us -> none  [collect_early(): lax.all_to_all(block, 'ctx', split_axis=1, concat_axis=1, tiled=True)]
    ppermute x67 -> x60, waiting for transfers between devices: 130 us -> 164 us  [hop(): lax.ppermute(value, 'ctx', [(i, i ^ bit) for i in range(lax.axis_size('ct...]
    convert_element_type x16 -> x3, other arithmetic: 24.6 us -> 1.83 us  [the longest x1 1.59 us: body(): grad_mixed.astype(bf16)]
    dot_general x2 -> x16, matrix products: 14.1 us -> 32.5 us  [dot_nn(): return jnp.dot(left, right, preferred_element_type=f32)]
    add x6 -> x13, other arithmetic: 3.35 us -> 20.3 us  [the longest x2 7.37 us: near_step(): return sum((part.astype(f32) for part in near_hops(sums)))]
    unnamed x243 -> x248, local copies, waits for them, and re-layouts: 82.6 us -> 66.7 us
  transfers between devices with their start and end apart: 85 -> 76, of which waited for: 28 -> 29; matrix products, arithmetic and copies ran while one was open for 27% -> 16% of each run, Pallas kernels for 24% -> 34%
where the time goes in v3:
time: 727 us; the launch traced here: 714 us
  Pallas kernels  239 us (33%)
  waiting for transfers between devices  198 us (27%)
  local copies, waits for them, and re-layouts  80.6 us (11%)
  starting transfers between devices  68.8 us (9%)
  other arithmetic  51 us (7%)
  matrix products  46.9 us (6%)
  between operations  15.8 us (2%)
  blocking collectives  13.5 us (2%)
    ppermute x60, waiting for transfers between devices, hop(): lax.ppermute(value, 'ctx', [(i, i ^ bit) for i in range(lax.axis_size('ct...  164 us
    pallas_call x12, Pallas kernels, sum_of_products(): pl.pallas_call(functools.partial(product_kernel, len(lefts), int(add is n...  71.2 us
    unnamed x248, local copies, waits for them, and re-layouts  66.7 us
    pallas_call x2, Pallas kernels, feed_forward(): pl.pallas_call(feed_kernel, grid=(count // tile,), in_specs=[rows, rows,...  39.1 us
    ppermute x60, starting transfers between devices, hop(): lax.ppermute(value, 'ctx', [(i, i ^ bit) for i in range(lax.axis_size('ct...  38.2 us
    pallas_call x2, Pallas kernels, feed_gradient(): pl.pallas_call(feed_gradient_kernel, grid=(width // tile,), in_specs=[col...  37.1 us
    pallas_call x2, Pallas kernels, attend_back(): pl.pallas_call(functools.partial(attend_back_kernel, row, blocks, slots,...  35.6 us
    dot_general x16, matrix products, dot_nn(): return jnp.dot(left, right, preferred_element_type=f32)  32.5 us
  transfers between devices with their start and end apart: 76, of which 29 were waited for; matrix products, arithmetic and copies ran while one was open for 16% of the time, Pallas kernels for 34%

profile of v3, /device:TPU:0, one launch (start us, length us, event | category | flops | bytes accessed | tf_op | source)
XLA Modules:
  0.0 714.1 jit_solution(1073250801534934146)
XLA Ops:
  10.4 13.5 %all_to_all.100 = bf16[64,8,384]{2,0,1:T(8,128)(2,1)} all-to-all(bf16[64,8,384]{2,0,1:T(8,128)(2,1)S(1)} %pad_maximum_fusion.4), channel_id=1, replica_groups=mesh['dp'=4,'ctx'=8] {'ctx'}, dimensions={1} | all-to-all | bytes 786432 | tf_op jit(solution)/shard_map/all_to_all | solution.py:194
  27.5 3.8 all-to-all-start.1
  36.4 18.2 %all-to-all-done.1 = bf16[64,8,256]{2,0,1:T(8,128)(2,1)S(1)} async-done(((bf16[64,8,256]{2,0,1:T(8,128)(2,1)}), bf16[64,8,256]{2,0,1:T(8,128)(2,1)S(1)}, u32[]{:S(2)}, u32[]{:S(2)}) %all-to-all-start.1) | async-done | bytes 262176 | tf_op jit(solution)/shard_map/all_to_all | solution.py:194
  57.5 3.0 copy.82
  60.5 4.4 all-to-all-start.2
  75.7 20.5 %collective-permute-done.2.refs_0_ = bf16[128,2048]{1,0:T(8,128)(2,1)S(1)} collective-permute-done((bf16[128,2048]{1,0:T(8,128)(2,1)}, bf16[128,2048]{1,0:T(8,128)(2,1)S(1)}, u32[]{:S(2)}, u32[]{:S(2)}) %collective-permute-start.2) | collective-permute-done | bytes 524320 | tf_op jit(solution)/shard_map/ppermute | solution.py:104
  98.9 3.3 convolution_dynamic-update-slice_fusion.7
  117.9 5.4 collective-permute-done.9.refs_2_.by_y_ref
  123.3 8.5 %collective-permute-done.8.refs_1_.by_x_ref = bf16[256,2048]{1,0:T(8,128)(2,1)} collective-permute-done((bf16[256,2048]{1,0:T(8,128)(2,1)S(1)}, bf16[256,2048]{1,0:T(8,128)(2,1)}, u32[]{:S(2)}, u32[]{:S(2)}) %collective-permute-start.8) | collective-permute-done | bytes 1048608 | tf_op jit(solution)/shard_map/ppermute | solution.py:104
  131.8 3.0 copy.85
  134.8 4.5 all-to-all-start.3
  142.7 9.4 %attend.2 = (bf16[8,2,128,256]{3,2,1,0:T(8,128)(2,1)S(1)}, f32[8,2,1,512]{3,2,1,0:T(1,128)S(1)}) custom-call(s32[1]{0:T(128)} %bitcast.1.base_ref, s32[2]{0:T(128)S(1)} %copy-done.86, f32[8,2,128,384]{3,2,1,0:T(8,128)} %bitcast.10.q_ref.kv_ref, f32[8,2,128,384]{3,2,1,0:T(8,128)} %bitcast.10.q_ref.kv_ref, f32[64,1]{1,0:T(8,128)S(1)} %copy.86.qg_ref, ...), custom_call_target="tpu_custom_call" | custom-call | flops 12884901888 | tf_op jit(solution)/shard_map/attend/pallas_call | solution.py:484
  153.7 6.7 all-to-all-done.3
  162.4 14.9 %attend.3 = (bf16[8,2,128,256]{3,2,1,0:T(8,128)(2,1)S(1)}, f32[8,2,1,512]{3,2,1,0:T(1,128)S(1)}) custom-call(s32[1]{0:T(128)} %bitcast.1.base_ref, s32[2]{0:T(128)S(1)} %copy-done.86, f32[8,2,128,384]{3,2,1,0:T(8,128)} %bitcast.10.q_ref.kv_ref, f32[8,2,128,384]{3,2,1,0:T(8,128)} %bitcast.10.q_ref.kv_ref, ...), custom_call_target="tpu_custom_call", output_to_operand_aliasing={{0}: (8, {}), {1}: (9, {})} | custom-call | flops 12884901888 | tf_op jit(solution)/shard_map/attend/pallas_call | solution.py:484
  181.3 3.2 sum_of_products.12
  191.7 13.3 %collective-permute-done.12.refs_0_ = bf16[128,2048]{1,0:T(8,128)(2,1)S(1)} collective-permute-done((bf16[128,2048]{1,0:T(8,128)(2,1)}, bf16[128,2048]{1,0:T(8,128)(2,1)S(1)}, u32[]{:S(2)}, u32[]{:S(2)}) %collective-permute-start.12) | collective-permute-done | bytes 524320 | tf_op jit(solution)/shard_map/ppermute | solution.py:104
  209.6 4.4 sum_of_products.14
  216.9 5.2 collective-permute-done.17
  229.1 20.6 %collective-permute-done.18 = bf16[256,2048]{1,0:T(8,128)(2,1)} collective-permute-done((bf16[256,2048]{1,0:T(8,128)(2,1)}, bf16[256,2048]{1,0:T(8,128)(2,1)}, u32[]{:S(2)}, u32[]{:S(2)}) %collective-permute-start.18) | collective-permute-done | bytes 1048608 | tf_op jit(solution)/shard_map/ppermute | solution.py:104
  249.8 3.4 collective-permute-done.16
  253.2 2.8 multiply_reduce_fusion.2
  258.6 21.4 %collective-permute-done.20.by_y_ref.refs_2_ = bf16[256,2048]{1,0:T(8,128)(2,1)S(1)} collective-permute-done((bf16[256,2048]{1,0:T(8,128)(2,1)S(1)}, bf16[256,2048]{1,0:T(8,128)(2,1)S(1)}, u32[]{:S(2)}, u32[]{:S(2)}) %collective-permute-start.20) | collective-permute-done | bytes 1048608 | tf_op jit(solution)/shard_map/ppermute | solution.py:104
  284.5 10.4 %collective-permute-done.21.refs_0_ = bf16[128,2048]{1,0:T(8,128)(2,1)S(1)} collective-permute-done((bf16[128,2048]{1,0:T(8,128)(2,1)}, bf16[128,2048]{1,0:T(8,128)(2,1)S(1)}, u32[]{:S(2)}, u32[]{:S(2)}) %collective-permute-start.21) | collective-permute-done | bytes 524320 | tf_op jit(solution)/shard_map/ppermute | solution.py:104
  296.1 3.5 stack.12.cotangent_ref
  299.7 3.2 copy-done.90
  305.1 3.3 copy-done.8
  308.4 19.5 %feed_forward.2 = (bf16[2048,512]{1,0:T(8,128)(2,1)S(1)}, bf16[2048,1024]{1,0:T(8,128)(2,1)}) custom-call(bf16[2048,2048]{1,0:T(8,128)(2,1)} %fence.32.hidden_ref, bf16[2048,2048]{1,0:T(8,128)(2,1)} %copy-done.90, bf16[2048,1536]{1,0:T(8,128)(2,1)} %all-gather.9.cloned.1.call-done.refs_1_.weight_ref.refs_2_), custom_call_target="tpu_custom_call" | custom-call | flops 21904332800 | tf_op jit(solution)/shard_map/feed_forward/pallas_call | solution.py:570
  327.9 18.5 %feed_gradient.2.refs_1_ = bf16[2048,1536]{1,0:T(8,128)(2,1)} custom-call(bf16[2048,2048]{1,0:T(8,128)(2,1)} %fence.32.hidden_ref, bf16[2048,2048]{1,0:T(8,128)(2,1)} %copy-done.90, bf16[2048,1024]{1,0:T(8,128)(2,1)} %get-tuple-element.105.grad_ref.refs_0_, bf16[2048,512]{1,0:T(8,128)(2,1)S(1)} %get-tuple-element.104.inner_ref.refs_0_), custom_call_target="tpu_custom_call" | custom-call | flops 20615843840 | tf_op jit(solution)/shard_map/feed_gradient/pallas_call | solution.py:599
  348.2 19.5 %feed_forward.3 = (bf16[2048,512]{1,0:T(8,128)(2,1)S(1)}, bf16[2048,1024]{1,0:T(8,128)(2,1)}) custom-call(bf16[2048,2048]{1,0:T(8,128)(2,1)} %fence.32.hidden_ref, bf16[2048,2048]{1,0:T(8,128)(2,1)} %copy-done.90, bf16[2048,1536]{1,0:T(8,128)(2,1)} %fence.34.weight_ref.refs_3_), custom_call_target="tpu_custom_call" | custom-call | flops 21904332800 | tf_op jit(solution)/shard_map/feed_forward/pallas_call | solution.py:570
  369.1 12.7 %sum_of_products.15 = (bf16[768,2048]{1,0:T(8,128)(2,1)S(1)}, bf16[256,2048]{1,0:T(8,128)(2,1)S(1)}) custom-call(bf16[2048,1024]{1,0:T(8,128)(2,1)} %get-tuple-element.105.grad_ref.refs_0_, bf16[2048,1024]{1,0:T(8,128)(2,1)} %get-tuple-element.107.refs_1_.grad_ref, bf16[2048,1536]{1,0:T(8,128)(2,1)} %all-gather.9.cloned.1.call-done.refs_1_.weight_ref.refs_2_, ...), custom_call_target="tpu_custom_call" | custom-call | tf_op jit(solution)/shard_map/sum_of_products/pallas_call | solution.py:636
  388.5 5.9 sum_of_products.16
  398.1 11.2 %sum_of_products.17 = (f32[256,2048]{1,0:T(8,128)S(1)}, bf16[256,2048]{1,0:T(8,128)(2,1)S(1)}, bf16[256,2048]{1,0:T(8,128)(2,1)S(1)}) custom-call(bf16[2048,1024]{1,0:T(8,128)(2,1)} %get-tuple-element.105.grad_ref.refs_0_, bf16[2048,1024]{1,0:T(8,128)(2,1)} %get-tuple-element.107.refs_1_.grad_ref, ...), custom_call_target="tpu_custom_call" | custom-call | tf_op jit(solution)/shard_map/sum_of_products/pallas_call | solution.py:636
  412.6 7.4 %sum_of_products.18 = (bf16[768,2048]{1,0:T(8,128)(2,1)}, bf16[256,2048]{1,0:T(8,128)(2,1)S(1)}) custom-call(bf16[2048,512]{1,0:T(8,128)(2,1)S(1)} %copy-done.36, bf16[2048,512]{1,0:T(8,128)(2,1)S(1)} %copy-done.39, bf16[2048,1536]{1,0:T(8,128)(2,1)} %all-gather.9.cloned.1.call-done.refs_1_.weight_ref.refs_2_, bf16[2048,1536]{1,0:T(8,128)(2,1)} %fence.34.weight_ref.refs_3_, ...), custom_call_target="tpu_custom_call" | custom-call | flops 10307921920 | tf_op jit(solution)/shard_map/sum_of_products/pallas_call | solution.py:636
  422.8 4.1 stack.14
  426.9 3.3 copy-done.89
  434.4 4.2 sum_of_products.19
  438.6 8.4 %collective-permute-done.35 = bf16[256,2048]{1,0:T(8,128)(2,1)} collective-permute-done((bf16[256,2048]{1,0:T(8,128)(2,1)}, bf16[256,2048]{1,0:T(8,128)(2,1)}, u32[]{:S(2)}, u32[]{:S(2)}) %collective-permute-start.35) | collective-permute-done | bytes 1048608 | tf_op jit(solution)/shard_map/ppermute | solution.py:104
  447.0 3.4 convert_add_fusion.2.refs_0_
  451.1 3.5 multiply_reduce_fusion
  459.2 18.6 %feed_gradient.3.refs_0_ = bf16[2048,1536]{1,0:T(8,128)(2,1)} custom-call(bf16[2048,2048]{1,0:T(8,128)(2,1)} %fence.32.hidden_ref, bf16[2048,2048]{1,0:T(8,128)(2,1)} %copy-done.90, bf16[2048,1024]{1,0:T(8,128)(2,1)} %get-tuple-element.107.refs_1_.grad_ref, bf16[2048,512]{1,0:T(8,128)(2,1)S(1)} %copy-done.40), custom_call_target="tpu_custom_call" | custom-call | flops 20615843840 | tf_op jit(solution)/shard_map/feed_gradient/pallas_call | solution.py:599
  482.4 8.0 %sum_of_products.20 = (f32[256,2048]{1,0:T(8,128)S(1)}, bf16[256,2048]{1,0:T(8,128)(2,1)S(1)}, bf16[256,2048]{1,0:T(8,128)(2,1)S(1)}) custom-call(bf16[2048,512]{1,0:T(8,128)(2,1)} %copy-done.35, bf16[2048,512]{1,0:T(8,128)(2,1)} %copy-done.38, bf16[2048,1536]{1,0:T(8,128)(2,1)} %all-gather.9.cloned.1.call-done.refs_1_.weight_ref.refs_2_, ...), custom_call_target="tpu_custom_call" | custom-call | flops 7730940928 | tf_op jit(solution)/shard_map/sum_of_products/pallas_call | solution.py:636
  501.1 9.3 %collective-permute-done.40.refs_0_ = bf16[128,2048]{1,0:T(8,128)(2,1)S(1)} collective-permute-done((bf16[128,2048]{1,0:T(8,128)(2,1)}, bf16[128,2048]{1,0:T(8,128)(2,1)S(1)}, u32[]{:S(2)}, u32[]{:S(2)}) %collective-permute-start.40) | collective-permute-done | bytes 524320 | tf_op jit(solution)/shard_map/ppermute | solution.py:104
  518.6 4.5 all-to-all-start.4
  528.6 14.7 %attend_back.2 = (bf16[8,2,128,256]{3,2,1,0:T(8,128)(2,1)S(1)}, bf16[8,2,128,128]{3,2,1,0:T(8,128)(2,1)S(1)}, f32[64,128]{1,0:T(8,128)S(1)}, f32[64,128]{1,0:T(8,128)S(1)}) custom-call(s32[1]{0:T(128)} %bitcast.1.base_ref, s32[2]{0:T(128)S(1)} %copy-done.87, f32[8,2,128,384]{3,2,1,0:T(8,128)} %bitcast.10.q_ref.kv_ref, ...), custom_call_target="tpu_custom_call" | custom-call | flops 21474836480 | tf_op jit(solution)/shard_map/attend_back/pallas_call | solution.py:520
  545.2 3.9 stack.15
  549.1 3.2 copy-done.88
  563.1 20.9 %attend_back.3 = (bf16[8,2,128,256]{3,2,1,0:T(8,128)(2,1)S(1)}, bf16[8,2,128,128]{3,2,1,0:T(8,128)(2,1)S(1)}, f32[64,128]{1,0:T(8,128)S(1)}, f32[64,128]{1,0:T(8,128)S(1)}) custom-call(s32[1]{0:T(128)} %bitcast.1.base_ref, s32[2]{0:T(128)S(1)} %copy-done.87, ...), custom_call_target="tpu_custom_call", output_to_operand_aliasing={{0}: (11, {}), {1}: (12, {})} | custom-call | flops 21474836480 | tf_op jit(solution)/shard_map/attend_back/pallas_call | solution.py:520
  585.4 6.4 convolution_convert_fusion.1
  591.8 7.9 %convolution_convert_fusion = bf16[2048,384]{1,0:T(8,128)(2,1)S(1)} fusion(bf16[2048,2048]{1,0:T(8,128)(2,1)} %copy-done.89, bf16[2048,384]{1,0:T(8,128)(2,1)S(1)} %copy-done.1), kind=kOutput, calls=%fused_computation | convolution fusion | flops 3222011904 | bytes 11534336 | tf_op jit(solution)/shard_map/dot_general | solution.py:42
  601.5 4.0 sum_of_products.21
  608.4 4.3 all-to-all-start.5
  612.8 5.6 add_convert_fusion
  618.4 3.0 sum_of_products.22
  622.2 5.0 sum_of_products.23
  629.9 3.9 all-to-all-done.5
  635.0 11.7 %collective-permute-done.54 = bf16[128,2048]{1,0:T(8,128)(2,1)S(1)} collective-permute-done((bf16[128,2048]{1,0:T(8,128)(2,1)}, bf16[128,2048]{1,0:T(8,128)(2,1)S(1)}, u32[]{:S(2)}, u32[]{:S(2)}) %collective-permute-start.54) | collective-permute-done | bytes 524320 | tf_op jit(solution)/shard_map/ppermute | solution.py:104
  652.6 6.8 place_units.1
  661.3 3.9 all-to-all-start.6
  665.2 9.4 %collective-permute-done.55 = bf16[256,2048]{1,0:T(8,128)(2,1)} collective-permute-done((bf16[256,2048]{1,0:T(8,128)(2,1)S(1)}, bf16[256,2048]{1,0:T(8,128)(2,1)}, u32[]{:S(2)}, u32[]{:S(2)}) %collective-permute-start.55) | collective-permute-done | bytes 1048608 | tf_op jit(solution)/shard_map/ppermute | solution.py:104
  677.0 4.0 convert_add_fusion.refs_0_
  688.2 2.9 collective-permute-start.59
  691.7 5.2 fusion.9
  697.0 3.9 collective-permute-start.62
  702.7 2.9 collective-permute-done.61
  (476 shorter events, 188.7 us)
Async XLA Ops:
  7.2 91.7 %all-gather.5.cloned.1.call-start = ((), (), s32[]{:S(2)}) async-start(), calls=%async_computation.10 | async-start | bytes 1966080 | tf_op jit(solution)/shard_map/all_gather | solution.py:200
  25.7 30.9 %collective-permute-start.1 = (bf16[256,2048]{1,0:T(8,128)(2,1)}, bf16[256,2048]{1,0:T(8,128)(2,1)S(1)}, u32[]{:S(2)}, u32[]{:S(2)}) collective-permute-start(bf16[256,2048]{1,0:T(8,128)(2,1)} %fusion.4.refs_0_), channel_id=1, source_target_pairs={{0,4},{1,5},{2,6},{3,7},{4,0},{5,1},{6,2},{7,3},{8,12},{9,13},{10,... | collective-permute-start | bytes 3145736 | tf_op jit(solution)/shard_map/ppermute | solution.py:104
  26.2 30.3 %collective-permute-start = (bf16[256,2048]{1,0:T(8,128)(2,1)}, bf16[256,2048]{1,0:T(8,128)(2,1)}, u32[]{:S(2)}, u32[]{:S(2)}) collective-permute-start(bf16[256,2048]{1,0:T(8,128)(2,1)} %fusion.4.refs_0_), channel_id=1, source_target_pairs={{0,2},{1,3},{2,0},{3,1},{4,6},{5,7},{6,4},{7,5},{8,10},{9,11},{10,... | collective-permute-start | bytes 3145736 | tf_op jit(solution)/shard_map/ppermute | solution.py:104
  26.8 79.6 %collective-permute-start.4 = (bf16[256,2048]{1,0:T(8,128)(2,1)}, bf16[256,2048]{1,0:T(8,128)(2,1)}, u32[]{:S(2)}, u32[]{:S(2)}) collective-permute-start(bf16[256,2048]{1,0:T(8,128)(2,1)} %fusion.4.refs_0_), channel_id=1, source_target_pairs={{0,1},{1,0},{2,3},{3,2},{4,5},{5,4},{6,7},{7,6},{8,9},{9,8},{10,11... | collective-permute-start | bytes 3145736 | tf_op jit(solution)/shard_map/ppermute | solution.py:104
  27.5 27.0 %all-to-all-start.1 = ((bf16[64,8,256]{2,0,1:T(8,128)(2,1)}), bf16[64,8,256]{2,0,1:T(8,128)(2,1)S(1)}, u32[]{:S(2)}, u32[]{:S(2)}) async-start(bf16[64,8,256]{2,0,1:T(8,128)(2,1)} %bitcast.114), calls=%async_computation.1 | async-start | bytes 524288 | tf_op jit(solution)/shard_map/all_to_all | solution.py:194
  31.3 147.6 %all-gather.7.cloned.1.call-start = ((), (), s32[]{:S(2)}) async-start(), calls=%async_computation.11 | async-start | bytes 1310720 | tf_op jit(solution)/shard_map/all_gather | solution.py:200
  60.5 36.8 %all-to-all-start.2 = ((bf16[64,8,1536]{2,0,1:T(8,128)(2,1)}), bf16[64,8,1536]{2,0,1:T(8,128)(2,1)}, u32[]{:S(2)}, u32[]{:S(2)}) async-start(bf16[64,8,1536]{2,0,1:T(8,128)(2,1)} %copy.82), calls=%async_computation.2 | async-start | bytes 3145728 | tf_op jit(solution)/shard_map/all_to_all | solution.py:194
  65.0 164.0 %all-gather.9.cloned.1.call-start = ((), (), s32[]{:S(2)}) async-start(), calls=%async_computation.12 | async-start | bytes 7864320 | tf_op jit(solution)/shard_map/all_gather | solution.py:200
  67.4 28.8 %collective-permute-start.2 = (bf16[128,2048]{1,0:T(8,128)(2,1)}, bf16[128,2048]{1,0:T(8,128)(2,1)S(1)}, u32[]{:S(2)}, u32[]{:S(2)}) collective-permute-start(bf16[128,2048]{1,0:T(8,128)(2,1)} %get-tuple-element.84), channel_id=1, source_target_pairs={{0,4},{1,5},{2,6},{3,7},{4,0},{5,1},{6,2},{7,3},{8,12},{9,13},{10,... | collective-permute-start | bytes 1572872 | tf_op jit(solution)/shard_map/ppermute | solution.py:104
  69.2 27.0 %collective-permute-start.3 = (bf16[128,2048]{1,0:T(8,128)(2,1)}, bf16[128,2048]{1,0:T(8,128)(2,1)S(1)}, u32[]{:S(2)}, u32[]{:S(2)}) collective-permute-start(bf16[128,2048]{1,0:T(8,128)(2,1)} %get-tuple-element.85), channel_id=1, source_target_pairs={{0,2},{1,3},{2,0},{3,1},{4,6},{5,7},{6,4},{7,5},{8,10},{9,11},{10,... | collective-permute-start | bytes 1572872 | tf_op jit(solution)/shard_map/ppermute | solution.py:104
  75.2 40.0 %collective-permute-start.6 = (bf16[256,2048]{1,0:T(8,128)(2,1)S(1)}, bf16[256,2048]{1,0:T(8,128)(2,1)}, u32[]{:S(2)}, u32[]{:S(2)}) collective-permute-start(bf16[256,2048]{1,0:T(8,128)(2,1)S(1)} %copy-done.22), channel_id=1, source_target_pairs={{0,1},{1,0},{2,3},{3,2},{4,5},{5,4},{6,7},{7,6},{8,9},{9,8},{10,11... | collective-permute-start | bytes 3145736 | tf_op jit(solution)/shard_map/ppermute | solution.py:104
  75.2 37.2 %collective-permute-start.5 = (bf16[256,2048]{1,0:T(8,128)(2,1)}, bf16[256,2048]{1,0:T(8,128)(2,1)}, u32[]{:S(2)}, u32[]{:S(2)}) collective-permute-start(bf16[256,2048]{1,0:T(8,128)(2,1)} %collective-permute-done.by_x_ref.refs_2_.refs_1_), channel_id=1, source_target_pairs={{0,1},{1,0},{2,3},{3,2},{4,5},{5,4},{6,7},{7,6},{8,9},{9,8},{10,11... | collective-permute-start | bytes 3145736 | tf_op jit(solution)/shard_map/ppermute | solution.py:104
  97.3 42.0 %collective-permute-start.7 = (bf16[256,2048]{1,0:T(8,128)(2,1)}, bf16[256,2048]{1,0:T(8,128)(2,1)}, u32[]{:S(2)}, u32[]{:S(2)}) collective-permute-start(bf16[256,2048]{1,0:T(8,128)(2,1)} %stack.8.refs_3_), channel_id=1, source_target_pairs={{0,1},{1,0},{2,3},{3,2},{4,5},{5,4},{6,7},{7,6},{8,9},{9,8},{10,11... | collective-permute-start | bytes 3145736 | tf_op jit(solution)/shard_map/ppermute | solution.py:104
  97.4 26.0 %collective-permute-start.9 = (bf16[256,2048]{1,0:T(8,128)(2,1)}, bf16[256,2048]{1,0:T(8,128)(2,1)}, u32[]{:S(2)}, u32[]{:S(2)}) collective-permute-start(bf16[256,2048]{1,0:T(8,128)(2,1)} %fence.26.refs_0_), channel_id=1, source_target_pairs={{0,4},{1,5},{2,6},{3,7},{4,0},{5,1},{6,2},{7,3},{8,12},{9,13},{10,... | collective-permute-start | bytes 3145736 | tf_op jit(solution)/shard_map/ppermute | solution.py:104
  106.4 25.4 %collective-permute-start.8 = (bf16[256,2048]{1,0:T(8,128)(2,1)S(1)}, bf16[256,2048]{1,0:T(8,128)(2,1)}, u32[]{:S(2)}, u32[]{:S(2)}) collective-permute-start(bf16[256,2048]{1,0:T(8,128)(2,1)S(1)} %copy-done.16), channel_id=1, source_target_pairs={{0,2},{1,3},{2,0},{3,1},{4,6},{5,7},{6,4},{7,5},{8,10},{9,11},{10,... | collective-permute-start | bytes 3145736 | tf_op jit(solution)/shard_map/ppermute | solution.py:104
  134.8 25.6 %all-to-all-start.3 = ((bf16[64,8,1536]{2,0,1:T(8,128)(2,1)}), bf16[64,8,1536]{2,0,1:T(8,128)(2,1)}, u32[]{:S(2)}, u32[]{:S(2)}) async-start(bf16[64,8,1536]{2,0,1:T(8,128)(2,1)} %copy.85), calls=%async_computation.3 | async-start | bytes 3145728 | tf_op jit(solution)/shard_map/all_to_all | solution.py:194
  160.4 187.9 %all-gather.11.cloned.1.call-start = ((), (), s32[]{:S(2)}) async-start(), calls=%async_computation.13 | async-start | bytes 7864320 | tf_op jit(solution)/shard_map/all_gather | solution.py:200
  188.2 21.4 %collective-permute-start.11 = (bf16[768,2048]{1,0:T(8,128)(2,1)}, bf16[768,2048]{1,0:T(8,128)(2,1)}, u32[]{:S(2)}, u32[]{:S(2)}) collective-permute-start(bf16[768,2048]{1,0:T(8,128)(2,1)} %fence.30), channel_id=1, source_target_pairs={{0,1},{1,0},{2,3},{3,2},{4,5},{5,4},{6,7},{7,6},{8,9},{9,8},{10,11... | collective-permute-start | bytes 9437192 | tf_op jit(solution)/shard_map/ppermute | solution.py:104
  190.5 14.4 %collective-permute-start.12 = (bf16[128,2048]{1,0:T(8,128)(2,1)}, bf16[128,2048]{1,0:T(8,128)(2,1)S(1)}, u32[]{:S(2)}, u32[]{:S(2)}) collective-permute-start(bf16[128,2048]{1,0:T(8,128)(2,1)} %get-tuple-element.97), channel_id=1, source_target_pairs={{0,4},{1,5},{2,6},{3,7},{4,0},{5,1},{6,2},{7,3},{8,12},{9,13},{10,... | collective-permute-start | bytes 1572872 | tf_op jit(solution)/shard_map/ppermute | solution.py:104
  191.1 14.1 %collective-permute-start.13 = (bf16[128,2048]{1,0:T(8,128)(2,1)}, bf16[128,2048]{1,0:T(8,128)(2,1)S(1)}, u32[]{:S(2)}, u32[]{:S(2)}) collective-permute-start(bf16[128,2048]{1,0:T(8,128)(2,1)} %get-tuple-element.98), channel_id=1, source_target_pairs={{0,2},{1,3},{2,0},{3,1},{4,6},{5,7},{6,4},{7,5},{8,10},{9,11},{10,... | collective-permute-start | bytes 1572872 | tf_op jit(solution)/shard_map/ppermute | solution.py:104
  205.3 10.6 %collective-permute-start.14 = (bf16[256,2048]{1,0:T(8,128)(2,1)S(1)}, bf16[256,2048]{1,0:T(8,128)(2,1)S(1)}, u32[]{:S(2)}, u32[]{:S(2)}) collective-permute-start(bf16[256,2048]{1,0:T(8,128)(2,1)S(1)} %stack.9.refs_3_), channel_id=1, source_target_pairs={{0,1},{1,0},{2,3},{3,2},{4,5},{5,4},{6,7},{7,6},{8,9},{9,8},{10,11... | collective-permute-start | bytes 3145736 | tf_op jit(solution)/shard_map/ppermute | solution.py:104
  207.6 14.6 %collective-permute-start.17 = (bf16[128,2048]{1,0:T(8,128)(2,1)}, bf16[128,2048]{1,0:T(8,128)(2,1)}, u32[]{:S(2)}, u32[]{:S(2)}) collective-permute-start(bf16[128,2048]{1,0:T(8,128)(2,1)} %get-tuple-element.93.refs_3_), channel_id=1, source_target_pairs={{0,2},{1,3},{2,0},{3,1},{4,6},{5,7},{6,4},{7,5},{8,10},{9,11},{10,... | collective-permute-start | bytes 1572872 | tf_op jit(solution)/shard_map/ppermute | solution.py:104
  208.2 18.1 %collective-permute-start.15 = (bf16[128,2048]{1,0:T(8,128)(2,1)S(1)}, bf16[128,2048]{1,0:T(8,128)(2,1)}, u32[]{:S(2)}, u32[]{:S(2)}) collective-permute-start(bf16[128,2048]{1,0:T(8,128)(2,1)S(1)} %get-tuple-element.100), channel_id=1, source_target_pairs={{0,4},{1,5},{2,6},{3,7},{4,0},{5,1},{6,2},{7,3},{8,12},{9,13},{10,... | collective-permute-start | bytes 1572872 | tf_op jit(solution)/shard_map/ppermute | solution.py:104
  224.7 25.1 %collective-permute-start.18 = (bf16[256,2048]{1,0:T(8,128)(2,1)}, bf16[256,2048]{1,0:T(8,128)(2,1)}, u32[]{:S(2)}, u32[]{:S(2)}) collective-permute-start(bf16[256,2048]{1,0:T(8,128)(2,1)} %pad_add_fusion.6), channel_id=1, source_target_pairs={{0,4},{1,5},{2,6},{3,7},{4,0},{5,1},{6,2},{7,3},{8,12},{9,13},{10,... | collective-permute-start | bytes 3145736 | tf_op jit(solution)/shard_map/ppermute | solution.py:104
  228.5 24.8 %collective-permute-start.16 = (bf16[256,2048]{1,0:T(8,128)(2,1)}, bf16[256,2048]{1,0:T(8,128)(2,1)}, u32[]{:S(2)}, u32[]{:S(2)}) collective-permute-start(bf16[256,2048]{1,0:T(8,128)(2,1)} %pad_add_fusion.7), channel_id=1, source_target_pairs={{0,2},{1,3},{2,0},{3,1},{4,6},{5,7},{6,4},{7,5},{8,10},{9,11},{10,... | collective-permute-start | bytes 3145736 | tf_op jit(solution)/shard_map/ppermute | solution.py:104
  229.0 248.8 %reduce-scatter.4.cloned.1.call-start = ((), (), s32[]{:S(2)}) async-start(), calls=%async_computation.14 | async-start | bytes 7864320 | tf_op jit(solution)/shard_map/reduce_scatter | solution.py:204
  256.4 23.6 %collective-permute-start.20 = (bf16[256,2048]{1,0:T(8,128)(2,1)S(1)}, bf16[256,2048]{1,0:T(8,128)(2,1)S(1)}, u32[]{:S(2)}, u32[]{:S(2)}) collective-permute-start(bf16[256,2048]{1,0:T(8,128)(2,1)S(1)} %multiply_convert_fusion.refs_0_), channel_id=1, source_target_pairs={{0,4},{1,5},{2,6},{3,7},{4,0},{5,1},{6,2},{7,3},{8,12},{9,13},{10,... | collective-permute-start | bytes 3145736 | tf_op jit(solution)/shard_map/ppermute | solution.py:104
  257.3 23.7 %collective-permute-start.19 = (bf16[256,2048]{1,0:T(8,128)(2,1)S(1)}, bf16[256,2048]{1,0:T(8,128)(2,1)}, u32[]{:S(2)}, u32[]{:S(2)}) collective-permute-start(bf16[256,2048]{1,0:T(8,128)(2,1)S(1)} %multiply_convert_fusion.refs_0_), channel_id=1, source_target_pairs={{0,2},{1,3},{2,0},{3,1},{4,6},{5,7},{6,4},{7,5},{8,10},{9,11},{10,... | collective-permute-start | bytes 3145736 | tf_op jit(solution)/shard_map/ppermute | solution.py:104
  258.1 37.4 %collective-permute-start.27 = (bf16[256,2048]{1,0:T(8,128)(2,1)S(1)}, bf16[256,2048]{1,0:T(8,128)(2,1)}, u32[]{:S(2)}, u32[]{:S(2)}) collective-permute-start(bf16[256,2048]{1,0:T(8,128)(2,1)S(1)} %copy-done.17), channel_id=1, source_target_pairs={{0,1},{1,0},{2,3},{3,2},{4,5},{5,4},{6,7},{7,6},{8,9},{9,8},{10,11... | collective-permute-start | bytes 3145736 | tf_op jit(solution)/shard_map/ppermute | solution.py:104
  258.1 37.7 %collective-permute-start.29 = (bf16[256,2048]{1,0:T(8,128)(2,1)}, bf16[256,2048]{1,0:T(8,128)(2,1)}, u32[]{:S(2)}, u32[]{:S(2)}) collective-permute-start(bf16[256,2048]{1,0:T(8,128)(2,1)} %collective-permute-done.9.refs_2_.by_y_ref), channel_id=1, source_target_pairs={{0,1},{1,0},{2,3},{3,2},{4,5},{5,4},{6,7},{7,6},{8,9},{9,8},{10,11... | collective-permute-start | bytes 3145736 | tf_op jit(solution)/shard_map/ppermute | solution.py:104
  258.6 37.5 %collective-permute-start.28 = (bf16[256,2048]{1,0:T(8,128)(2,1)}, bf16[256,2048]{1,0:T(8,128)(2,1)}, u32[]{:S(2)}, u32[]{:S(2)}) collective-permute-start(bf16[256,2048]{1,0:T(8,128)(2,1)} %collective-permute-done.8.refs_1_.by_x_ref), channel_id=1, source_target_pairs={{0,1},{1,0},{2,3},{3,2},{4,5},{5,4},{6,7},{7,6},{8,9},{9,8},{10,11... | collective-permute-start | bytes 3145736 | tf_op jit(solution)/shard_map/ppermute | solution.py:104
  283.2 11.7 %collective-permute-start.21 = (bf16[128,2048]{1,0:T(8,128)(2,1)}, bf16[128,2048]{1,0:T(8,128)(2,1)S(1)}, u32[]{:S(2)}, u32[]{:S(2)}) collective-permute-start(bf16[128,2048]{1,0:T(8,128)(2,1)} %get-tuple-element.102), channel_id=1, source_target_pairs={{0,4},{1,5},{2,6},{3,7},{4,0},{5,1},{6,2},{7,3},{8,12},{9,13},{10,... | collective-permute-start | bytes 1572872 | tf_op jit(solution)/shard_map/ppermute | solution.py:104
  284.1 11.0 %collective-permute-start.22 = (bf16[128,2048]{1,0:T(8,128)(2,1)}, bf16[128,2048]{1,0:T(8,128)(2,1)S(1)}, u32[]{:S(2)}, u32[]{:S(2)}) collective-permute-start(bf16[128,2048]{1,0:T(8,128)(2,1)} %get-tuple-element.103), channel_id=1, source_target_pairs={{0,2},{1,3},{2,0},{3,1},{4,6},{5,7},{6,4},{7,5},{8,10},{9,11},{10,... | collective-permute-start | bytes 1572872 | tf_op jit(solution)/shard_map/ppermute | solution.py:104
  294.9 8.0 %collective-permute-start.23 = (bf16[256,2048]{1,0:T(8,128)(2,1)}, bf16[256,2048]{1,0:T(8,128)(2,1)S(1)}, u32[]{:S(2)}, u32[]{:S(2)}) collective-permute-start(bf16[256,2048]{1,0:T(8,128)(2,1)} %copy-done.56), channel_id=1, source_target_pairs={{0,1},{1,0},{2,3},{3,2},{4,5},{5,4},{6,7},{7,6},{8,9},{9,8},{10,11... | collective-permute-start | bytes 3145736 | tf_op jit(solution)/shard_map/ppermute | solution.py:104
  295.1 7.8 %collective-permute-start.25 = (bf16[256,2048]{1,0:T(8,128)(2,1)}, bf16[256,2048]{1,0:T(8,128)(2,1)S(1)}, u32[]{:S(2)}, u32[]{:S(2)}) collective-permute-start(bf16[256,2048]{1,0:T(8,128)(2,1)} %copy-done.80), channel_id=1, source_target_pairs={{0,1},{1,0},{2,3},{3,2},{4,5},{5,4},{6,7},{7,6},{8,9},{9,8},{10,11... | collective-permute-start | bytes 3145736 | tf_op jit(solution)/shard_map/ppermute | solution.py:104
  347.7 260.7 %reduce-scatter.6.cloned.1.call-start = ((), (), s32[]{:S(2)}) async-start(), calls=%async_computation.15 | async-start | bytes 7864320 | tf_op jit(solution)/shard_map/reduce_scatter | solution.py:204
  387.1 9.3 %collective-permute-start.31 = (bf16[768,2048]{1,0:T(8,128)(2,1)}, bf16[768,2048]{1,0:T(8,128)(2,1)S(1)}, u32[]{:S(2)}, u32[]{:S(2)}) collective-permute-start(bf16[768,2048]{1,0:T(8,128)(2,1)} %fence.35), channel_id=1, source_target_pairs={{0,1},{1,0},{2,3},{3,2},{4,5},{5,4},{6,7},{7,6},{8,9},{9,8},{10,11... | collective-permute-start | bytes 9437192 | tf_op jit(solution)/shard_map/ppermute | solution.py:104
  394.4 16.2 %collective-permute-start.36 = (bf16[128,2048]{1,0:T(8,128)(2,1)S(1)}, bf16[128,2048]{1,0:T(8,128)(2,1)S(1)}, u32[]{:S(2)}, u32[]{:S(2)}) collective-permute-start(bf16[128,2048]{1,0:T(8,128)(2,1)S(1)} %get-tuple-element.110.refs_5_), channel_id=1, source_target_pairs={{0,2},{1,3},{2,0},{3,1},{4,6},{5,7},{6,4},{7,5},{8,10},{9,11},{10,... | collective-permute-start | bytes 1572872 | tf_op jit(solution)/shard_map/ppermute | solution.py:104
  395.0 24.9 %collective-permute-start.34 = (bf16[128,2048]{1,0:T(8,128)(2,1)S(1)}, bf16[128,2048]{1,0:T(8,128)(2,1)S(1)}, u32[]{:S(2)}, u32[]{:S(2)}) collective-permute-start(bf16[128,2048]{1,0:T(8,128)(2,1)S(1)} %get-tuple-element.119), channel_id=1, source_target_pairs={{0,4},{1,5},{2,6},{3,7},{4,0},{5,1},{6,2},{7,3},{8,12},{9,13},{10,... | collective-permute-start | bytes 1572872 | tf_op jit(solution)/shard_map/ppermute | solution.py:104
  411.8 26.9 %collective-permute-start.37 = (bf16[256,2048]{1,0:T(8,128)(2,1)}, bf16[256,2048]{1,0:T(8,128)(2,1)}, u32[]{:S(2)}, u32[]{:S(2)}) collective-permute-start(bf16[256,2048]{1,0:T(8,128)(2,1)} %pad_add_fusion.4), channel_id=1, source_target_pairs={{0,4},{1,5},{2,6},{3,7},{4,0},{5,1},{6,2},{7,3},{8,12},{9,13},{10,... | collective-permute-start | bytes 3145736 | tf_op jit(solution)/shard_map/ppermute | solution.py:104
  419.9 10.3 %collective-permute-start.32 = (bf16[256,2048]{1,0:T(8,128)(2,1)S(1)}, bf16[256,2048]{1,0:T(8,128)(2,1)S(1)}, u32[]{:S(2)}, u32[]{:S(2)}) collective-permute-start(bf16[256,2048]{1,0:T(8,128)(2,1)S(1)} %get-tuple-element.113), channel_id=1, source_target_pairs={{0,1},{1,0},{2,3},{3,2},{4,5},{5,4},{6,7},{7,6},{8,9},{9,8},{10,11... | collective-permute-start | bytes 3145736 | tf_op jit(solution)/shard_map/ppermute | solution.py:104
  421.2 25.9 %collective-permute-start.35 = (bf16[256,2048]{1,0:T(8,128)(2,1)}, bf16[256,2048]{1,0:T(8,128)(2,1)}, u32[]{:S(2)}, u32[]{:S(2)}) collective-permute-start(bf16[256,2048]{1,0:T(8,128)(2,1)} %pad_add_fusion.5), channel_id=1, source_target_pairs={{0,2},{1,3},{2,0},{3,1},{4,6},{5,7},{6,4},{7,5},{8,10},{9,11},{10,... | collective-permute-start | bytes 3145736 | tf_op jit(solution)/shard_map/ppermute | solution.py:104
  431.2 51.2 %collective-permute-start.33 = (bf16[768,2048]{1,0:T(8,128)(2,1)}, bf16[768,2048]{1,0:T(8,128)(2,1)}, u32[]{:S(2)}, u32[]{:S(2)}) collective-permute-start(bf16[768,2048]{1,0:T(8,128)(2,1)} %fence.36), channel_id=1, source_target_pairs={{0,1},{1,0},{2,3},{3,2},{4,5},{5,4},{6,7},{7,6},{8,9},{9,8},{10,11... | collective-permute-start | bytes 9437192 | tf_op jit(solution)/shard_map/ppermute | solution.py:104
  456.3 25.1 %collective-permute-start.39 = (bf16[256,2048]{1,0:T(8,128)(2,1)}, bf16[256,2048]{1,0:T(8,128)(2,1)}, u32[]{:S(2)}, u32[]{:S(2)}) collective-permute-start(bf16[256,2048]{1,0:T(8,128)(2,1)} %fusion.20.refs_0_), channel_id=1, source_target_pairs={{0,4},{1,5},{2,6},{3,7},{4,0},{5,1},{6,2},{7,3},{8,12},{9,13},{10,... | collective-permute-start | bytes 3145736 | tf_op jit(solution)/shard_map/ppermute | solution.py:104
  457.5 24.8 %collective-permute-start.38 = (bf16[256,2048]{1,0:T(8,128)(2,1)}, bf16[256,2048]{1,0:T(8,128)(2,1)}, u32[]{:S(2)}, u32[]{:S(2)}) collective-permute-start(bf16[256,2048]{1,0:T(8,128)(2,1)} %fusion.20.refs_0_), channel_id=1, source_target_pairs={{0,2},{1,3},{2,0},{3,1},{4,6},{5,7},{6,4},{7,5},{8,10},{9,11},{10,... | collective-permute-start | bytes 3145736 | tf_op jit(solution)/shard_map/ppermute | solution.py:104
  477.8 33.2 %collective-permute-start.42 = (bf16[256,2048]{1,0:T(8,128)(2,1)}, bf16[256,2048]{1,0:T(8,128)(2,1)}, u32[]{:S(2)}, u32[]{:S(2)}) collective-permute-start(bf16[256,2048]{1,0:T(8,128)(2,1)} %fusion.20.refs_0_), channel_id=1, source_target_pairs={{0,1},{1,0},{2,3},{3,2},{4,5},{5,4},{6,7},{7,6},{8,9},{9,8},{10,11... | collective-permute-start | bytes 3145736 | tf_op jit(solution)/shard_map/ppermute | solution.py:104
  481.4 33.0 %collective-permute-start.44 = (bf16[256,2048]{1,0:T(8,128)(2,1)}, bf16[256,2048]{1,0:T(8,128)(2,1)}, u32[]{:S(2)}, u32[]{:S(2)}) collective-permute-start(bf16[256,2048]{1,0:T(8,128)(2,1)} %collective-permute-done.39.by_y_ref.refs_2_), channel_id=1, source_target_pairs={{0,1},{1,0},{2,3},{3,2},{4,5},{5,4},{6,7},{7,6},{8,9},{9,8},{10,11... | collective-permute-start | bytes 3145736 | tf_op jit(solution)/shard_map/ppermute | solution.py:104
  482.4 30.4 %collective-permute-start.43 = (bf16[256,2048]{1,0:T(8,128)(2,1)}, bf16[256,2048]{1,0:T(8,128)(2,1)}, u32[]{:S(2)}, u32[]{:S(2)}) collective-permute-start(bf16[256,2048]{1,0:T(8,128)(2,1)} %collective-permute-done.38.by_x_ref.refs_1_), channel_id=1, source_target_pairs={{0,1},{1,0},{2,3},{3,2},{4,5},{5,4},{6,7},{7,6},{8,9},{9,8},{10,11... | collective-permute-start | bytes 3145736 | tf_op jit(solution)/shard_map/ppermute | solution.py:104
  495.9 14.5 %collective-permute-start.40 = (bf16[128,2048]{1,0:T(8,128)(2,1)}, bf16[128,2048]{1,0:T(8,128)(2,1)S(1)}, u32[]{:S(2)}, u32[]{:S(2)}) collective-permute-start(bf16[128,2048]{1,0:T(8,128)(2,1)} %get-tuple-element.121), channel_id=1, source_target_pairs={{0,4},{1,5},{2,6},{3,7},{4,0},{5,1},{6,2},{7,3},{8,12},{9,13},{10,... | collective-permute-start | bytes 1572872 | tf_op jit(solution)/shard_map/ppermute | solution.py:104
  495.9 14.5 %collective-permute-start.41 = (bf16[128,2048]{1,0:T(8,128)(2,1)}, bf16[128,2048]{1,0:T(8,128)(2,1)S(1)}, u32[]{:S(2)}, u32[]{:S(2)}) collective-permute-start(bf16[128,2048]{1,0:T(8,128)(2,1)} %get-tuple-element.122), channel_id=1, source_target_pairs={{0,2},{1,3},{2,0},{3,1},{4,6},{5,7},{6,4},{7,5},{8,10},{9,11},{10,... | collective-permute-start | bytes 1572872 | tf_op jit(solution)/shard_map/ppermute | solution.py:104
  518.6 40.2 %all-to-all-start.4 = ((bf16[8,64,1536]{2,1,0:T(8,128)(2,1)}), bf16[8,64,1536]{2,1,0:T(8,128)(2,1)}, u32[]{:S(2)}, u32[]{:S(2)}) async-start(bf16[8,64,1536]{2,1,0:T(8,128)(2,1)} %bitcast.126), calls=%async_computation.5 | async-start | bytes 3145728 | tf_op jit(solution)/shard_map/all_to_all | solution.py:208
  523.1 138.2 %reduce-scatter.8.cloned.1.call-start = ((), (), s32[]{:S(2)}) async-start(), calls=%async_computation.16 | async-start | bytes 3276800 | tf_op jit(solution)/shard_map/reduce_scatter | solution.py:204
  523.1 34.2 %collective-permute-start.46 = (bf16[128,2048]{1,0:T(8,128)(2,1)S(1)}, bf16[128,2048]{1,0:T(8,128)(2,1)S(1)}, u32[]{:S(2)}, u32[]{:S(2)}) collective-permute-start(bf16[128,2048]{1,0:T(8,128)(2,1)S(1)} %copy-done.44), channel_id=1, source_target_pairs={{0,4},{1,5},{2,6},{3,7},{4,0},{5,1},{6,2},{7,3},{8,12},{9,13},{10,... | collective-permute-start | bytes 1572872 | tf_op jit(solution)/shard_map/ppermute | solution.py:104
  525.1 29.3 %collective-permute-start.48 = (bf16[128,2048]{1,0:T(8,128)(2,1)}, bf16[128,2048]{1,0:T(8,128)(2,1)S(1)}, u32[]{:S(2)}, u32[]{:S(2)}) collective-permute-start(bf16[128,2048]{1,0:T(8,128)(2,1)} %get-tuple-element.125), channel_id=1, source_target_pairs={{0,2},{1,3},{2,0},{3,1},{4,6},{5,7},{6,4},{7,5},{8,10},{9,11},{10,... | collective-permute-start | bytes 1572872 | tf_op jit(solution)/shard_map/ppermute | solution.py:104
  555.6 29.7 %collective-permute-start.49 = (bf16[256,2048]{1,0:T(8,128)(2,1)}, bf16[256,2048]{1,0:T(8,128)(2,1)}, u32[]{:S(2)}, u32[]{:S(2)}) collective-permute-start(bf16[256,2048]{1,0:T(8,128)(2,1)} %pad_add_fusion.2.refs_4_), channel_id=1, source_target_pairs={{0,4},{1,5},{2,6},{3,7},{4,0},{5,1},{6,2},{7,3},{8,12},{9,13},{10,... | collective-permute-start | bytes 3145736 | tf_op jit(solution)/shard_map/ppermute | solution.py:104
  558.5 26.8 %collective-permute-start.47 = (bf16[256,2048]{1,0:T(8,128)(2,1)}, bf16[256,2048]{1,0:T(8,128)(2,1)}, u32[]{:S(2)}, u32[]{:S(2)}) collective-permute-start(bf16[256,2048]{1,0:T(8,128)(2,1)} %pad_add_fusion.3.refs_3_), channel_id=1, source_target_pairs={{0,2},{1,3},{2,0},{3,1},{4,6},{5,7},{6,4},{7,5},{8,10},{9,11},{10,... | collective-permute-start | bytes 3145736 | tf_op jit(solution)/shard_map/ppermute | solution.py:104
  608.3 13.9 %collective-permute-start.51 = (bf16[768,2048]{1,0:T(8,128)(2,1)}, bf16[768,2048]{1,0:T(8,128)(2,1)}, u32[]{:S(2)}, u32[]{:S(2)}) collective-permute-start(bf16[768,2048]{1,0:T(8,128)(2,1)} %fence.43), channel_id=1, source_target_pairs={{0,1},{1,0},{2,3},{3,2},{4,5},{5,4},{6,7},{7,6},{8,9},{9,8},{10,11... | collective-permute-start | bytes 9437192 | tf_op jit(solution)/shard_map/ppermute | solution.py:104
  608.4 25.3 %all-to-all-start.5 = ((bf16[8,64,1536]{2,1,0:T(8,128)(2,1)}), bf16[8,64,1536]{2,1,0:T(8,128)(2,1)}, u32[]{:S(2)}, u32[]{:S(2)}) async-start(bf16[8,64,1536]{2,1,0:T(8,128)(2,1)} %bitcast.128), calls=%async_computation.7 | async-start | bytes 3145728 | tf_op jit(solution)/shard_map/all_to_all | solution.py:208
  633.8 12.9 %collective-permute-start.54 = (bf16[128,2048]{1,0:T(8,128)(2,1)}, bf16[128,2048]{1,0:T(8,128)(2,1)S(1)}, u32[]{:S(2)}, u32[]{:S(2)}) collective-permute-start(bf16[128,2048]{1,0:T(8,128)(2,1)} %get-tuple-element.143), channel_id=1, source_target_pairs={{0,2},{1,3},{2,0},{3,1},{4,6},{5,7},{6,4},{7,5},{8,10},{9,11},{10,... | collective-permute-start | bytes 1572872 | tf_op jit(solution)/shard_map/ppermute | solution.py:104
  634.3 15.1 %collective-permute-start.52 = (bf16[128,2048]{1,0:T(8,128)(2,1)}, bf16[128,2048]{1,0:T(8,128)(2,1)S(1)}, u32[]{:S(2)}, u32[]{:S(2)}) collective-permute-start(bf16[128,2048]{1,0:T(8,128)(2,1)} %get-tuple-element.141), channel_id=1, source_target_pairs={{0,4},{1,5},{2,6},{3,7},{4,0},{5,1},{6,2},{7,3},{8,12},{9,13},{10,... | collective-permute-start | bytes 1572872 | tf_op jit(solution)/shard_map/ppermute | solution.py:104
  649.0 25.6 %collective-permute-start.55 = (bf16[256,2048]{1,0:T(8,128)(2,1)S(1)}, bf16[256,2048]{1,0:T(8,128)(2,1)}, u32[]{:S(2)}, u32[]{:S(2)}) collective-permute-start(bf16[256,2048]{1,0:T(8,128)(2,1)S(1)} %pad_add_fusion), channel_id=1, source_target_pairs={{0,4},{1,5},{2,6},{3,7},{4,0},{5,1},{6,2},{7,3},{8,12},{9,13},{10,... | collective-permute-start | bytes 3145736 | tf_op jit(solution)/shard_map/ppermute | solution.py:104
  650.6 26.4 %collective-permute-start.53 = (bf16[256,2048]{1,0:T(8,128)(2,1)}, bf16[256,2048]{1,0:T(8,128)(2,1)}, u32[]{:S(2)}, u32[]{:S(2)}) collective-permute-start(bf16[256,2048]{1,0:T(8,128)(2,1)} %pad_add_fusion.1), channel_id=1, source_target_pairs={{0,2},{1,3},{2,0},{3,1},{4,6},{5,7},{6,4},{7,5},{8,10},{9,11},{10,... | collective-permute-start | bytes 3145736 | tf_op jit(solution)/shard_map/ppermute | solution.py:104
  661.3 24.0 %all-to-all-start.6 = ((bf16[8,64,640]{2,1,0:T(8,128)(2,1)}), bf16[8,64,640]{2,1,0:T(8,128)(2,1)S(1)}, u32[]{:S(2)}, u32[]{:S(2)}) async-start(bf16[8,64,640]{2,1,0:T(8,128)(2,1)} %bitcast.132), calls=%async_computation.9 | async-start | bytes 1310720 | tf_op jit(solution)/shard_map/all_to_all | solution.py:208
  688.2 8.7 %collective-permute-start.59 = (f32[4224]{0:T(1024)S(1)}, f32[4224]{0:T(1024)S(1)}, u32[]{:S(2)}, u32[]{:S(2)}) collective-permute-start(f32[4224]{0:T(1024)S(1)} %add.150), channel_id=1, source_target_pairs={{0,6},{1,7},{2,4},{3,5},{4,2},{5,3},{6,0},{7,1},{8,14},{9,15},{10,... | collective-permute-start | bytes 50696 | tf_op jit(solution)/shard_map/ppermute | solution.py:104
  (134 other events, 1056.1 us)
Sparse Core Ops, SparseCore 0:
  24.1 36.4 all-gather.4
  62.2 26.7 all-gather.6
  97.5 115.7 all-gather.8
  229.1 115.6 all-gather.10
  347.9 110.9 reduce-scatter.3
  478.0 110.2 reduce-scatter.5
  608.6 52.6 reduce-scatter.7

commit v4 on v3

--- a/solution.py
+++ b/solution.py
@@ -150,20 +150,30 @@
     return (own, *near, *far)
 
 
-def far_step(sums, far_after=(), near_after=()):
+def far_hops(sums, far_after=()):
     if lax.axis_size("ctx") != 8:
-        return fence(sums, *far_after, *near_after) if far_after or near_after else sums
-    own, *near, far_first, far_last = sums
+        return ()
+    far_first, far_last = sums[3:]
     if far_after:
         far_first, far_last = fence((far_first, far_last), *far_after)
+    return hop(far_first, 2), hop(far_last, 4)
+
+
+def far_add(sums, arrived, near_after=()):
+    if lax.axis_size("ctx") != 8:
+        return fence(sums, *near_after) if near_after else sums
+    own, by_x, by_y = sums[:3]
     if near_after:
-        near = fence(near, *near_after)
-    from_x, from_y = hop(far_first, 2), hop(far_last, 4)
-    by_x, by_y = near
+        by_x, by_y = fence((by_x, by_y), *near_after)
+    from_x, from_y = arrived
     rows = by_x.shape[0] // 2
     by_x = by_x + jnp.pad(from_y, ((rows, 0), (0, 0)))
     by_y = by_y + jnp.pad(from_x, ((0, rows), (0, 0)))
     return own, by_x, by_y
+
+
+def far_step(sums, far_after=(), near_after=()):
+    return far_add(sums, far_hops(sums, far_after), near_after)
 
 
 def near_hops(sums):
@@ -209,23 +219,25 @@
 
 
 def place_units_kernel(first_ref, last_ref, *out_refs):
-    units = first_ref.shape[1] // 3
     for which, out_ref in enumerate(out_refs):
-        for half, ref in enumerate((first_ref, last_ref)):
-            out_ref[:, half * units : (half + 1) * units] = ref[
+        start = 0
+        for ref in (first_ref, last_ref):
+            units = ref.shape[1] // 3
+            out_ref[:, start : start + units] = ref[
                 :, which * units : (which + 1) * units
             ].astype(f32)
+            start += units
 
 
 def place_units(first, last, parts):
-    rows, columns = first.shape[0] // parts, first.shape[1]
-    units = columns // 3
+    rows = first.shape[0] // parts
+    units = (first.shape[1] + last.shape[1]) // 3
     return pl.pallas_call(
         place_units_kernel,
         grid=(parts,),
-        in_specs=[pl.BlockSpec((rows, columns), lambda i: (i, 0))] * 2,
-        out_specs=[pl.BlockSpec((rows, 2 * units), lambda i: (0, i))] * 3,
-        out_shape=[jax.ShapeDtypeStruct((rows, 2 * units * parts), f32)] * 3,
+        in_specs=[pl.BlockSpec((rows, v.shape[1]), lambda i: (i, 0)) for v in (first, last)],
+        out_specs=[pl.BlockSpec((rows, units), lambda i: (0, i))] * 3,
+        out_shape=[jax.ShapeDtypeStruct((rows, units * parts), f32)] * 3,
         compiler_params=pltpu.CompilerParams(vmem_limit_bytes=16 * 2**20),
         cost_estimate=cost(10**7, 800),
         name="place_units",
@@ -388,18 +400,20 @@
 
 
 def attend_back_kernel(
-    row, blocks, slots, heads, chunk,
+    blocks, slots, heads, chunk,
     base_ref, len_ref, q_ref, kv_ref, qg_ref, kg_ref, cos_ref, sin_ref, o_ref, do_ref, lse_ref,
-    *refs,
+    dq_ref, dkv_ref, dqg_ref, dkg_ref, k_all, v_all, k_t, dk_all, dv_all,
 ):
-    dq_ref, dkv_ref, dqg_ref, dkg_ref, k_all, v_all, k_t, dk_all, dv_all = refs[-9:]
-    query_block = pl.program_id(0)
+    row, query_block = pl.program_id(0), pl.program_id(1)
     base, length = base_ref[0], len_ref[row]
 
-    @pl.when(query_block == 0)
+    @pl.when((row == 0) & (query_block == 0))
     def _():
         dqg_ref[...] = jnp.zeros_like(dqg_ref)
         dkg_ref[...] = jnp.zeros_like(dkg_ref)
+
+    @pl.when(query_block == 0)
+    def _():
         for j in range(blocks):
             at = place_of(base, jnp.int32(j), blocks)
             here = slice(j * slots, (j + 1) * slots)
@@ -458,16 +472,20 @@
 
 
 def attention_specs(row, blocks, slots, width, total):
-    own = lambda i, base, lens: (place_of(base[0], i, blocks), row, 0, 0)
-    constant = lambda i, base, lens: (0, 0)
+    def place(*grid):
+        (i, base, _), r = (grid, row) if row is not None else (grid[1:], grid[0])
+        return place_of(base[0], i, blocks), r, 0, 0
+
+    row_of = lambda *grid: grid[0] if row is None else row
+    constant = lambda *grid: (0, 0)
     both = 2 * HEAD_SIZE
     return (
-        pl.BlockSpec((1, 1, slots, width), own),
-        pl.BlockSpec((blocks, 1, slots, both), lambda i, base, lens: (0, row, 0, width // both)),
-        pl.BlockSpec((blocks, 1, slots, both), lambda i, base, lens: (0, row, 0, 0)),
+        pl.BlockSpec((1, 1, slots, width), place),
+        pl.BlockSpec((blocks, 1, slots, both), lambda *g: (0, row_of(*g), 0, width // both)),
+        pl.BlockSpec((blocks, 1, slots, both), lambda *g: (0, row_of(*g), 0, 0)),
         pl.BlockSpec((HEAD_SIZE, 1), constant),
         pl.BlockSpec((HEAD_SIZE // 2, total), constant),
-        pl.BlockSpec((1, 1, 1, width // HEAD_SIZE * slots), own),
+        pl.BlockSpec((1, 1, 1, width // HEAD_SIZE * slots), place),
         pl.BlockSpec((HEAD_SIZE, 128), constant),
     )
 
@@ -506,25 +524,24 @@
 
 
 def attend_back(
-    row, previous, base, lengths, raw, query_gain, key_gain, cosine, sine, attended, gradient, log_total
+    base, lengths, raw, query_gain, key_gain, cosine, sine, attended, gradient, log_total
 ):
     blocks, rows, slots, columns = raw.shape
     width = columns - 2 * HEAD_SIZE
     heads = width // HEAD_SIZE
     total = blocks * slots
     query_spec, raw_key_spec, key_spec, gain_spec, table_spec, lse_spec, sum_spec = (
-        attention_specs(row, blocks, slots, width, total)
+        attention_specs(None, blocks, slots, width, total)
     )
     operands = (base, lengths, raw, raw, query_gain, key_gain, cosine, sine)
     operands += (attended, gradient, log_total)
     return pl.pallas_call(
-        functools.partial(attend_back_kernel, row, blocks, slots, heads, 2 * slots),
+        functools.partial(attend_back_kernel, blocks, slots, heads, 2 * slots),
         grid_spec=pltpu.PrefetchScalarGridSpec(
             num_scalar_prefetch=2,
-            grid=(blocks,),
+            grid=(rows, blocks),
             in_specs=[query_spec, raw_key_spec, gain_spec, gain_spec, table_spec, table_spec]
-            + [query_spec, query_spec, lse_spec]
-            + [pl.BlockSpec(memory_space=pl.ANY)] * len(previous),
+            + [query_spec, query_spec, lse_spec],
             out_specs=[query_spec, key_spec, sum_spec, sum_spec],
             scratch_shapes=[
                 pltpu.VMEM((total, HEAD_SIZE), bf16),
@@ -540,11 +557,10 @@
             jax.ShapeDtypeStruct((HEAD_SIZE, 128), f32),
             jax.ShapeDtypeStruct((HEAD_SIZE, 128), f32),
         ],
-        input_output_aliases={len(operands) + i: i for i in range(len(previous))},
         compiler_params=pltpu.CompilerParams(vmem_limit_bytes=32 * 2**20),
-        cost_estimate=cost(5 * HEAD_SIZE * heads * total * total, 16),
+        cost_estimate=cost(5 * HEAD_SIZE * rows * heads * total * total, 16),
         name="attend_back",
-    )(*operands, *previous)
+    )(*operands)
 
 
 def feed_kernel(hidden_ref, cotangent_ref, weight_ref, inner_ref, grad_ref):
@@ -609,18 +625,24 @@
     )(hidden, cotangents, grad, inner)
 
 
-def product_kernel(count, adds, outs, *refs):
-    rows, weights, rest = refs[:count], refs[count : 2 * count], refs[2 * count : 2 * count + adds]
+def product_kernel(count, weighed, adds, outs, *refs):
+    rows, weights, rest = refs[:count], refs[count : 2 * count], refs[2 * count :]
+    out_refs = rest[-outs:]
     total = sum(dot_nt(r[...], w[...]) for r, w in zip(rows, weights))
-    for add_ref in rest:
-        total += add_ref[...].astype(f32)
+    if weighed:
+        *out_refs, sum_ref = out_refs
+        sum_ref[...] = jnp.sum(total * rest[0][...].astype(f32), axis=0, keepdims=True)
+    if adds:
+        total += rest[weighed][...].astype(f32)
     start = 0
-    for out_ref in refs[-outs:]:
+    for out_ref in out_refs:
         out_ref[...] = total[start : start + out_ref.shape[0]].astype(out_ref.dtype)
         start += out_ref.shape[0]
 
 
-def sum_of_products(share, lefts, weights, column, tokens, first, count, splits, add, before):
+def sum_of_products(
+    share, lefts, weights, column, tokens, first, count, splits, add, before, weigh=None
+):
     rows = count * tokens
     width = weights[0].shape[0]
     tile = 512
@@ -628,17 +650,30 @@
     specs = [pl.BlockSpec((rows, v.shape[1]), lambda i: (first // count, 0)) for v in lefts] + [
         pl.BlockSpec((tile, v.shape[1]), lambda i: (i, column)) for v in lefts
     ]
+    out_specs = [pl.BlockSpec((r, tile), lambda i: (0, i)) for r, _ in splits]
+    out_shape = [jax.ShapeDtypeStruct((r, width), dtype) for r, dtype in splits]
+    if weigh is not None:
+        operands.append(weigh)
+        specs.append(pl.BlockSpec((rows, tile), lambda i: (first // count, i)))
+        out_specs.append(pl.BlockSpec((1, tile), lambda i: (0, i)))
+        out_shape.append(jax.ShapeDtypeStruct((1, width), f32))
     if add is not None:
         operands.append(add)
         specs.append(pl.BlockSpec((rows, tile), lambda i: (0, i)))
     operands += before
     specs += [pl.BlockSpec(memory_space=pl.ANY)] * len(before)
     return pl.pallas_call(
-        functools.partial(product_kernel, len(lefts), int(add is not None), len(splits)),
+        functools.partial(
+            product_kernel,
+            len(lefts),
+            int(weigh is not None),
+            int(add is not None),
+            len(out_shape),
+        ),
         grid=(width // tile,),
         in_specs=specs,
-        out_specs=[pl.BlockSpec((r, tile), lambda i: (0, i)) for r, _ in splits],
-        out_shape=[jax.ShapeDtypeStruct((r, width), dtype) for r, dtype in splits],
+        out_specs=out_specs,
+        out_shape=out_shape,
         compiler_params=pltpu.CompilerParams(vmem_limit_bytes=48 * 2**20),
         cost_estimate=cost(2 * rows * width * sum(v.shape[1] for v in lefts), share),
         name="sum_of_products",
@@ -682,16 +717,16 @@
     )
     qkv_block = spread_columns(qkv_pack)
     out_block = spread_columns(out_weight.reshape(weight_rows, parts, query_cols))
-    units = feed // 2
+    first_units = feed * 4 // 8 // 128 * 128
     feed_packs = [
         jnp.concatenate(
             [
-                w.reshape(weight_rows, parts, feed)[:, :, start : start + units]
+                w.reshape(weight_rows, parts, feed)[:, :, start:stop]
                 for w in (gate_weight, up_weight, down_weight)
             ],
             axis=2,
         )
-        for start in (0, units)
+        for start, stop in ((0, first_units), (first_units, feed))
     ]
     flat = inputs.reshape(tokens, width).astype(f32)
     first_scale = rms_scale(flat)
@@ -717,18 +752,18 @@
     results = ()
     for row in range(rows):
         if row == rows - 1:
-            results = fence(results, last_block) if results else results
+            results = fence(results, last_block, cotangent_pieces[-1]) if results else results
         results = attend(row, results, base_array, lengths, raw, *gains, cosine, sine)
     attended, log_total = results
     attended_rows = attended.reshape(all_tokens, query_cols)
     sums = partial_products(
         functools.partial(sum_of_products, 2.4, [attended_rows], [out_full], 0, tokens), tokens
     )
-    mixed = flat + near_step(far_step(sums, (), cotangent_pieces[-1:]))
+    mixed = flat + near_step(far_step(sums))
 
     second_scale = rms_scale(mixed)
     normed_again = mixed * second_scale
-    pieces, _ = gather_pieces((normed_again * feedforward_gain).astype(bf16))
+    pieces, _ = gather_pieces((normed_again * feedforward_gain).astype(bf16), (cotangents,))
     hidden_again = after(stack(pieces), first_full)
     last_full = gather_rows(after(last_block, first_full))
     fulls = [first_full, last_full]
@@ -745,49 +780,43 @@
     sums = partial_products(
         functools.partial(sum_of_products, 0, grads, fulls, 0, tokens), tokens
     )
+    sums = far_step(sums)
     feed_sums = partial_products(
-        functools.partial(sum_of_products, 2.4, inners, fulls, 2, tokens), tokens, (sums[0],)
-    )
-    grad_hidden_again = after(near_step(far_step(sums)), feed_sums[-1])
+        functools.partial(sum_of_products, 2.4, inners, fulls, 2, tokens), tokens, tuple(sums[1:])
+    )
+    feed_arrived = far_hops(feed_sums)
+    own, *arrived = near_hops(sums)
+    if arrived:
+        arrived = fence(arrived, feed_sums[0])
+    grad_hidden_again = sum(part.astype(f32) for part in (own, *arrived))
     feedforward_gain_local = jnp.sum(grad_hidden_again * normed_again, axis=0)
     scaled_again = grad_hidden_again * feedforward_gain
     grad_mixed = cotangent_flat.astype(f32) + second_scale * (
         scaled_again - normed_again * jnp.mean(scaled_again * normed_again, axis=-1, keepdims=True)
     )
 
-    pieces, _ = gather_pieces(grad_mixed.astype(bf16), (feed_sums[0], first_gradient))
+    pieces, _ = gather_pieces(
+        after(grad_mixed.astype(bf16), first_gradient, *feed_arrived)
+    )
     grad_branch = stack(pieces)
     attended_gradient = jnp.concatenate(
         [dot_nn(piece, out_full).astype(bf16) for piece in pieces], axis=0
     )
     first_collected = collect_columns(after(first_gradient, attended_gradient))
-    feed_sums = far_step(feed_sums, (attended_gradient,))
-    feed_parts = near_hops(feed_sums)
+    feed_parts = near_hops(far_add(feed_sums, feed_arrived, (attended_gradient,)))
     feed_out = sum(part.astype(f32) for part in feed_parts)
     outputs = (mixed + feed_out).astype(bf16).reshape(rows, slots, width)
-    attended_gradient = attended_gradient.reshape(parts, rows, slots, query_cols)
-    grad_queries_keys_values, gain_sums = (), []
-    for row in range(rows):
-        if row == rows - 1 and grad_queries_keys_values:
-            grad_queries_keys_values = fence(
-                grad_queries_keys_values, first_collected, *feed_sums[1:]
-            )
-        *grad_queries_keys_values, query_gain_sums, key_gain_sums = attend_back(
-            row,
-            tuple(grad_queries_keys_values),
-            base_array,
-            lengths,
-            raw,
-            *gains,
-            cosine,
-            sine,
-            attended,
-            attended_gradient,
-            log_total,
-        )
-        gain_sums.append((query_gain_sums, key_gain_sums))
-    grad_queries, grad_keys_values = grad_queries_keys_values
-    query_gain_sums, key_gain_sums = [sum(g) for g in zip(*gain_sums)]
+    grad_queries, grad_keys_values, query_gain_sums, key_gain_sums = attend_back(
+        base_array,
+        lengths,
+        raw,
+        *gains,
+        cosine,
+        sine,
+        attended,
+        attended_gradient.reshape(parts, rows, slots, query_cols),
+        log_total,
+    )
     query_gain_local, key_gain_local = query_gain_sums.sum(axis=1), key_gain_sums.sum(axis=1)
     grad_raw = jnp.concatenate(
         [
@@ -796,7 +825,7 @@
         ],
         axis=1,
     )
-    grad_raw = after(grad_raw, *feed_parts[1:])
+    grad_raw = after(grad_raw, *feed_parts[1:], first_collected)
     attention_partial = jnp.concatenate(
         [dot_tn(hidden, grad_raw), dot_tn(grad_branch, after(attended_rows, grad_raw))], axis=1
     ).astype(bf16)
@@ -805,19 +834,24 @@
     query_weight_gradient, key_weight_gradient, value_weight_gradient, out_weight_gradient = (
         place_heads(attention_collected, parts, share)
     )
-    sums = partial_products(
-        functools.partial(sum_of_products, 2.4, [grad_raw], [qkv_full], 0, tokens),
-        tokens,
-        (attention_partial,),
-    )
+    weighed_sums = []
+
+    def hidden_product(*arguments):
+        *sums, weighed = sum_of_products(
+            2.4, [grad_raw], [qkv_full], 0, tokens, *arguments, weigh=hidden
+        )
+        weighed_sums.append(weighed[0])
+        return sums
+
+    sums = partial_products(hidden_product, tokens, (attention_partial,))
     last_collected = collect_columns(last_gradient)
-    grad_hidden = near_step(far_step(sums, (feed_out, last_collected), (feed_out,)))
+    sums = far_step(sums, (feed_out,), (last_collected,))
+    grad_hidden = after(near_step(sums), attention_collected)
     gate_weight_gradient, up_weight_gradient, down_weight_gradient = place_units(
         first_collected, last_collected, parts
     )
-    grad_hidden = after(grad_hidden, attention_gradient)
-
-    attention_gain_local = jnp.sum(grad_hidden * normed, axis=0)
+
+    attention_gain_local = sum(weighed_sums) / attention_gain.astype(f32)
     scaled_first = grad_hidden * attention_gain
     input_gradient = (
         grad_mixed
@@ -829,7 +863,7 @@
             jnp.concatenate(
                 [attention_gain_local, feedforward_gain_local, query_gain_local, key_gain_local]
             ),
-            attention_collected,
+            *sums[1:],
         )
     )
     attention_gain_gradient, feedforward_gain_gradient = gain_sums[:width], gain_sums[width : 2 * width]

time: 727 us -> 678 us (0.933)
  waiting for transfers between devices: 198 us -> 156 us
  local copies, waits for them, and re-layouts: 80.6 us -> 73.2 us
    ppermute x60, waiting for transfers between devices: 164 us -> 123 us  [hop(): lax.ppermute(value, 'ctx', [(i, i ^ bit) for i in range(lax.axis_size('ct...]
    unnamed x248 -> x176, local copies, waits for them, and re-layouts: 66.7 us -> 59.2 us
    pallas_call x14 -> x13, Pallas kernels: 107 us -> 109 us  [the longest x12 74.1 us: sum_of_products(): pl.pallas_call(functools.partial(product_kernel, len(lefts), int(weigh is...]
  transfers between devices with their start and end apart: 76 -> 76, of which waited for: 29 -> 31; matrix products, arithmetic and copies ran while one was open for 16% -> 16% of each run, Pallas kernels for 34% -> 36%
where the time goes in v4:
time: 678 us; the launch traced here: 670 us
  Pallas kernels  242 us (36%)
  waiting for transfers between devices  156 us (23%)
  starting transfers between devices  73.3 us (11%)
  local copies, waits for them, and re-layouts  73.2 us (11%)
  matrix products  49.8 us (7%)
  other arithmetic  46.9 us (7%)
  between operations  15.5 us (2%)
  blocking collectives  13.5 us (2%)
    ppermute x60, waiting for transfers between devices, hop(): lax.ppermute(value, 'ctx', [(i, i ^ bit) for i in range(lax.axis_size('ct...  123 us
    pallas_call x12, Pallas kernels, sum_of_products(): pl.pallas_call(functools.partial(product_kernel, len(lefts), int(weigh is...  74.1 us
    unnamed x176, local copies, waits for them, and re-layouts  59.2 us
    ppermute x60, starting transfers between devices, hop(): lax.ppermute(value, 'ctx', [(i, i ^ bit) for i in range(lax.axis_size('ct...  41.1 us
    pallas_call x2, Pallas kernels, feed_forward(): pl.pallas_call(feed_kernel, grid=(count // tile,), in_specs=[rows, rows,...  39.1 us
    pallas_call x2, Pallas kernels, feed_gradient(): pl.pallas_call(feed_gradient_kernel, grid=(width // tile,), in_specs=[col...  37 us
    dot_general x16, matrix products, dot_nn(): return jnp.dot(left, right, preferred_element_type=f32)  35.4 us
    pallas_call x1, Pallas kernels, attend_back(): pl.pallas_call(functools.partial(attend_back_kernel, blocks, slots, heads...  34.6 us
  transfers between devices with their start and end apart: 76, of which 31 were waited for; matrix products, arithmetic and copies ran while one was open for 16% of the time, Pallas kernels for 36%

profile of v4, /device:TPU:0, one launch (start us, length us, event | category | flops | bytes accessed | tf_op | source)
XLA Modules:
  0.0 669.9 jit_solution(4308102842942776234)
XLA Ops:
  10.5 13.5 %all_to_all.100 = bf16[64,8,384]{2,0,1:T(8,128)(2,1)} all-to-all(bf16[64,8,384]{2,0,1:T(8,128)(2,1)S(1)} %pad_maximum_fusion.4), channel_id=1, replica_groups=mesh['dp'=4,'ctx'=8] {'ctx'}, dimensions={1} | all-to-all | bytes 786432 | tf_op jit(solution)/shard_map/all_to_all | solution.py:204
  27.5 3.8 all-to-all-start.1
  36.7 17.8 %all-to-all-done.1 = bf16[64,8,256]{2,0,1:T(8,128)(2,1)S(1)} async-done(((bf16[64,8,256]{2,0,1:T(8,128)(2,1)}), bf16[64,8,256]{2,0,1:T(8,128)(2,1)S(1)}, u32[]{:S(2)}, u32[]{:S(2)}) %all-to-all-start.1) | async-done | bytes 262176 | tf_op jit(solution)/shard_map/all_to_all | solution.py:204
  58.7 3.0 copy.76
  61.7 4.4 all-to-all-start.2
  76.9 20.4 %collective-permute-done.2.refs_0_ = bf16[128,2048]{1,0:T(8,128)(2,1)S(1)} collective-permute-done((bf16[128,2048]{1,0:T(8,128)(2,1)}, bf16[128,2048]{1,0:T(8,128)(2,1)S(1)}, u32[]{:S(2)}, u32[]{:S(2)}) %collective-permute-start.2) | collective-permute-done | bytes 524320 | tf_op jit(solution)/shard_map/ppermute | solution.py:104
  100.6 3.3 convolution_dynamic-update-slice_fusion.7
  103.9 2.7 convolution_dynamic-update-slice_fusion.6
  108.0 2.8 convolution_dynamic-update-slice_fusion.4
  110.8 2.8 convolution_dynamic-update-slice_fusion.3
  116.3 7.2 %collective-permute-done.9.refs_2_.by_y_ref = bf16[256,2048]{1,0:T(8,128)(2,1)} collective-permute-done((bf16[256,2048]{1,0:T(8,128)(2,1)}, bf16[256,2048]{1,0:T(8,128)(2,1)}, u32[]{:S(2)}, u32[]{:S(2)}) %collective-permute-start.9) | collective-permute-done | bytes 1048608 | tf_op jit(solution)/shard_map/ppermute | solution.py:104
  131.9 2.7 convolution_dynamic-update-slice_fusion.refs_0_
  134.6 3.0 copy.79
  137.7 4.3 all-to-all-start.3
  144.5 9.4 %attend.2 = (bf16[8,2,128,256]{3,2,1,0:T(8,128)(2,1)S(1)}, f32[8,2,1,512]{3,2,1,0:T(1,128)S(1)}) custom-call(s32[1]{0:T(128)} %bitcast.1.base_ref, s32[2]{0:T(128)S(1)} %copy-done.56, f32[8,2,128,384]{3,2,1,0:T(8,128)} %bitcast.10.q_ref.kv_ref, f32[8,2,128,384]{3,2,1,0:T(8,128)} %bitcast.10.q_ref.kv_ref, f32[64,1]{1,0:T(8,128)S(1)} %copy.80.qg_ref, ...), custom_call_target="tpu_custom_call" | custom-call | flops 12884901888 | tf_op jit(solution)/shard_map/attend/pallas_call | solution.py:502
  155.5 7.5 %all-to-all-done.3 = bf16[64,8,1536]{2,0,1:T(8,128)(2,1)} async-done(((bf16[64,8,1536]{2,0,1:T(8,128)(2,1)}), bf16[64,8,1536]{2,0,1:T(8,128)(2,1)}, u32[]{:S(2)}, u32[]{:S(2)}) %all-to-all-start.3) | async-done | bytes 1572896 | tf_op jit(solution)/shard_map/all_to_all | solution.py:204
  166.0 14.9 %attend.3 = (bf16[8,2,128,256]{3,2,1,0:T(8,128)(2,1)S(1)}, f32[8,2,1,512]{3,2,1,0:T(1,128)S(1)}) custom-call(s32[1]{0:T(128)} %bitcast.1.base_ref, s32[2]{0:T(128)S(1)} %copy-done.56, f32[8,2,128,384]{3,2,1,0:T(8,128)} %bitcast.10.q_ref.kv_ref, f32[8,2,128,384]{3,2,1,0:T(8,128)} %bitcast.10.q_ref.kv_ref, ...), custom_call_target="tpu_custom_call", output_to_operand_aliasing={{0}: (8, {}), {1}: (9, {})} | custom-call | flops 12884901888 | tf_op jit(solution)/shard_map/attend/pallas_call | solution.py:502
  184.9 3.2 sum_of_products.12
  199.6 4.4 sum_of_products.14
  204.1 6.7 collective-permute-done.17
  217.3 19.5 %collective-permute-done.18 = bf16[256,2048]{1,0:T(8,128)(2,1)} collective-permute-done((bf16[256,2048]{1,0:T(8,128)(2,1)}, bf16[256,2048]{1,0:T(8,128)(2,1)}, u32[]{:S(2)}, u32[]{:S(2)}) %collective-permute-start.18) | collective-permute-done | bytes 1048608 | tf_op jit(solution)/shard_map/ppermute | solution.py:104
  238.2 3.1 multiply_reduce_fusion.2
  244.1 2.8 stack.10.refs_0_.cotangent_ref
  246.9 3.3 copy-done.8
  250.2 14.9 %collective-permute-done.20.by_y_ref.refs_2_ = bf16[256,2048]{1,0:T(8,128)(2,1)} collective-permute-done((bf16[256,2048]{1,0:T(8,128)(2,1)S(1)}, bf16[256,2048]{1,0:T(8,128)(2,1)}, u32[]{:S(2)}, u32[]{:S(2)}) %collective-permute-start.20) | collective-permute-done | bytes 1048608 | tf_op jit(solution)/shard_map/ppermute | solution.py:104
  270.2 9.3 %collective-permute-done.24.refs_0_ = bf16[128,2048]{1,0:T(8,128)(2,1)S(1)} collective-permute-done((bf16[128,2048]{1,0:T(8,128)(2,1)}, bf16[128,2048]{1,0:T(8,128)(2,1)S(1)}, u32[]{:S(2)}, u32[]{:S(2)}) %collective-permute-start.24) | collective-permute-done | bytes 524320 | tf_op jit(solution)/shard_map/ppermute | solution.py:104
  285.1 3.4 copy-done.12
  288.5 19.6 %feed_forward.2 = (bf16[2048,512]{1,0:T(8,128)(2,1)S(1)}, bf16[2048,1024]{1,0:T(8,128)(2,1)}) custom-call(bf16[2048,2048]{1,0:T(8,128)(2,1)} %fence.30.hidden_ref, bf16[2048,2048]{1,0:T(8,128)(2,1)} %copy-done.8, bf16[2048,1536]{1,0:T(8,128)(2,1)} %all-gather.9.cloned.1.call-done.refs_1_.weight_ref.refs_2_), custom_call_target="tpu_custom_call" | custom-call | flops 21904332800 | tf_op jit(solution)/shard_map/feed_forward/pallas_call | solution.py:586
  308.1 18.5 %feed_gradient.2.refs_1_ = bf16[2048,1536]{1,0:T(8,128)(2,1)} custom-call(bf16[2048,2048]{1,0:T(8,128)(2,1)} %fence.30.hidden_ref, bf16[2048,2048]{1,0:T(8,128)(2,1)} %copy-done.8, bf16[2048,1024]{1,0:T(8,128)(2,1)} %get-tuple-element.100.grad_ref.refs_0_, bf16[2048,512]{1,0:T(8,128)(2,1)S(1)} %get-tuple-element.99.inner_ref.refs_0_), custom_call_target="tpu_custom_call" | custom-call | flops 20615843840 | tf_op jit(solution)/shard_map/feed_gradient/pallas_call | solution.py:615
  328.5 2.9 all-gather.11.cloned.1.call-done.refs_0_
  331.3 19.5 %feed_forward.3 = (bf16[2048,512]{1,0:T(8,128)(2,1)S(1)}, bf16[2048,1024]{1,0:T(8,128)(2,1)}) custom-call(bf16[2048,2048]{1,0:T(8,128)(2,1)} %fence.30.hidden_ref, bf16[2048,2048]{1,0:T(8,128)(2,1)} %copy-done.8, bf16[2048,1536]{1,0:T(8,128)(2,1)} %fence.32.weight_ref.refs_3_), custom_call_target="tpu_custom_call" | custom-call | flops 21904332800 | tf_op jit(solution)/shard_map/feed_forward/pallas_call | solution.py:586
  352.2 12.7 %sum_of_products.15 = (bf16[768,2048]{1,0:T(8,128)(2,1)S(1)}, bf16[256,2048]{1,0:T(8,128)(2,1)S(1)}) custom-call(bf16[2048,1024]{1,0:T(8,128)(2,1)} %get-tuple-element.100.grad_ref.refs_0_, bf16[2048,1024]{1,0:T(8,128)(2,1)} %get-tuple-element.102.refs_1_.grad_ref, bf16[2048,1536]{1,0:T(8,128)(2,1)} %all-gather.9.cloned.1.call-done.refs_1_.weight_ref.refs_2_, ...), custom_call_target="tpu_custom_call" | custom-call | tf_op jit(solution)/shard_map/sum_of_products/pallas_call | solution.py:665
  366.6 2.7 collective-permute-done.30.refs_1_.refs_4_
  369.5 6.3 sum_of_products.16
  380.6 11.1 %sum_of_products.17 = (f32[256,2048]{1,0:T(8,128)S(1)}, bf16[256,2048]{1,0:T(8,128)(2,1)S(1)}, bf16[256,2048]{1,0:T(8,128)(2,1)S(1)}) custom-call(bf16[2048,1024]{1,0:T(8,128)(2,1)} %get-tuple-element.100.grad_ref.refs_0_, bf16[2048,1024]{1,0:T(8,128)(2,1)} %get-tuple-element.102.refs_1_.grad_ref, ...), custom_call_target="tpu_custom_call" | custom-call | tf_op jit(solution)/shard_map/sum_of_products/pallas_call | solution.py:665
  394.8 7.8 %sum_of_products.18 = (bf16[768,2048]{1,0:T(8,128)(2,1)}, bf16[256,2048]{1,0:T(8,128)(2,1)S(1)}) custom-call(bf16[2048,512]{1,0:T(8,128)(2,1)S(1)} %copy-done.31, bf16[2048,512]{1,0:T(8,128)(2,1)} %copy-done.28, bf16[2048,1536]{1,0:T(8,128)(2,1)} %all-gather.9.cloned.1.call-done.refs_1_.weight_ref.refs_2_, bf16[2048,1536]{1,0:T(8,128)(2,1)} %fence.32.weight_ref.refs_3_, ...), custom_call_target="tpu_custom_call" | custom-call | flops 10307921920 | tf_op jit(solution)/shard_map/sum_of_products/pallas_call | solution.py:665
  402.7 2.8 collective-permute-done.34.refs_1_.refs_4_
  408.0 4.2 stack.14.refs_2_
  412.3 3.4 copy-done.2
  415.7 5.1 sum_of_products.19
  425.3 7.2 %sum_of_products.20 = (f32[256,2048]{1,0:T(8,128)S(1)}, bf16[256,2048]{1,0:T(8,128)(2,1)S(1)}, bf16[256,2048]{1,0:T(8,128)(2,1)S(1)}) custom-call(bf16[2048,512]{1,0:T(8,128)(2,1)} %copy-done.30, bf16[2048,512]{1,0:T(8,128)(2,1)} %copy-done.28, bf16[2048,1536]{1,0:T(8,128)(2,1)} %all-gather.9.cloned.1.call-done.refs_1_.weight_ref.refs_2_, ...), custom_call_target="tpu_custom_call" | custom-call | flops 7730940928 | tf_op jit(solution)/shard_map/sum_of_products/pallas_call | solution.py:665
  436.5 3.8 multiply_reduce_fusion
  440.8 4.4 fusion.18
  448.0 18.5 %feed_gradient.3.refs_0_ = bf16[2048,1536]{1,0:T(8,128)(2,1)} custom-call(bf16[2048,2048]{1,0:T(8,128)(2,1)} %fence.30.hidden_ref, bf16[2048,2048]{1,0:T(8,128)(2,1)} %copy-done.8, bf16[2048,1024]{1,0:T(8,128)(2,1)} %get-tuple-element.102.refs_1_.grad_ref, bf16[2048,512]{1,0:T(8,128)(2,1)S(1)} %copy-done.29), custom_call_target="tpu_custom_call" | custom-call | flops 20615843840 | tf_op jit(solution)/shard_map/feed_gradient/pallas_call | solution.py:615
  480.0 5.9 collective-permute-done.42.refs_0_
  496.2 4.3 all-to-all-start.4
  506.9 34.6 %attend_back.1 = (bf16[8,2,128,256]{3,2,1,0:T(8,128)(2,1)S(1)}, bf16[8,2,128,128]{3,2,1,0:T(8,128)(2,1)S(1)}, f32[64,128]{1,0:T(8,128)S(1)}, f32[64,128]{1,0:T(8,128)S(1)}) custom-call(s32[1]{0:T(128)} %bitcast.1.base_ref, s32[2]{0:T(128)S(1)} %copy-done.56, f32[8,2,128,384]{3,2,1,0:T(8,128)} %bitcast.10.q_ref.kv_ref, ...), custom_call_target="tpu_custom_call" | custom-call | flops 42949672960 | tf_op jit(solution)/shard_map/attend_back/pallas_call | solution.py:538
  543.9 2.8 stack.15
  546.7 3.3 copy-done.57
  550.1 6.3 convolution_convert_fusion.1
  556.4 8.1 %convolution_convert_fusion = bf16[2048,384]{1,0:T(8,128)(2,1)S(1)} fusion(bf16[2048,2048]{1,0:T(8,128)(2,1)} %copy-done.2, bf16[2048,384]{1,0:T(8,128)(2,1)S(1)} %copy-done.1), kind=kOutput, calls=%fused_computation | convolution fusion | flops 3222011904 | bytes 11534336 | tf_op jit(solution)/shard_map/dot_general | solution.py:42
  566.2 5.9 sum_of_products.21
  572.1 2.8 collective-permute-done.50.refs_1_.refs_3_
  576.0 4.6 all-to-all-start.5
  580.6 5.2 add_convert_fusion
  585.8 3.3 sum_of_products.22
  589.9 5.9 sum_of_products.23
  601.9 10.9 %collective-permute-done.52 = bf16[128,2048]{1,0:T(8,128)(2,1)S(1)} collective-permute-done((bf16[128,2048]{1,0:T(8,128)(2,1)}, bf16[128,2048]{1,0:T(8,128)(2,1)S(1)}, u32[]{:S(2)}, u32[]{:S(2)}) %collective-permute-start.52) | collective-permute-done | bytes 524320 | tf_op jit(solution)/shard_map/ppermute | solution.py:104
  625.0 3.3 collective-permute-start.62
  631.3 6.8 %place_units.1 = (f32[64,8192]{1,0:T(8,128)}, f32[64,8192]{1,0:T(8,128)}, f32[64,8192]{1,0:T(8,128)}) custom-call(bf16[512,1536]{1,0:T(8,128)(2,1)} %bitcast.26.refs_3_.first_ref, bf16[512,1536]{1,0:T(8,128)(2,1)} %bitcast.28.refs_2_.last_ref), custom_call_target="tpu_custom_call" | custom-call | flops 8000000000 | tf_op jit(solution)/shard_map/place_units/pallas_call | solution.py:235
  639.3 3.5 all-to-all-start.6
  642.8 4.9 collective-permute-done.55
  648.8 4.0 convert_add_fusion.refs_0_
  659.6 3.2 fusion.8
  (403 shorter events, 180.2 us)
Async XLA Ops:
  7.2 93.3 %all-gather.5.cloned.1.call-start = ((), (), s32[]{:S(2)}) async-start(), calls=%async_computation.10 | async-start | bytes 1966080 | tf_op jit(solution)/shard_map/all_gather | solution.py:210
  25.6 32.1 %collective-permute-start.1 = (bf16[256,2048]{1,0:T(8,128)(2,1)}, bf16[256,2048]{1,0:T(8,128)(2,1)S(1)}, u32[]{:S(2)}, u32[]{:S(2)}) collective-permute-start(bf16[256,2048]{1,0:T(8,128)(2,1)} %fusion.3.refs_0_), channel_id=1, source_target_pairs={{0,4},{1,5},{2,6},{3,7},{4,0},{5,1},{6,2},{7,3},{8,12},{9,13},{10,... | collective-permute-start | bytes 3145736 | tf_op jit(solution)/shard_map/ppermute | solution.py:104
  26.2 31.5 %collective-permute-start = (bf16[256,2048]{1,0:T(8,128)(2,1)}, bf16[256,2048]{1,0:T(8,128)(2,1)}, u32[]{:S(2)}, u32[]{:S(2)}) collective-permute-start(bf16[256,2048]{1,0:T(8,128)(2,1)} %fusion.3.refs_0_), channel_id=1, source_target_pairs={{0,2},{1,3},{2,0},{3,1},{4,6},{5,7},{6,4},{7,5},{8,10},{9,11},{10,... | collective-permute-start | bytes 3145736 | tf_op jit(solution)/shard_map/ppermute | solution.py:104
  26.8 81.2 %collective-permute-start.4 = (bf16[256,2048]{1,0:T(8,128)(2,1)}, bf16[256,2048]{1,0:T(8,128)(2,1)}, u32[]{:S(2)}, u32[]{:S(2)}) collective-permute-start(bf16[256,2048]{1,0:T(8,128)(2,1)} %fusion.3.refs_0_), channel_id=1, source_target_pairs={{0,1},{1,0},{2,3},{3,2},{4,5},{5,4},{6,7},{7,6},{8,9},{9,8},{10,11... | collective-permute-start | bytes 3145736 | tf_op jit(solution)/shard_map/ppermute | solution.py:104
  27.5 27.0 %all-to-all-start.1 = ((bf16[64,8,256]{2,0,1:T(8,128)(2,1)}), bf16[64,8,256]{2,0,1:T(8,128)(2,1)S(1)}, u32[]{:S(2)}, u32[]{:S(2)}) async-start(bf16[64,8,256]{2,0,1:T(8,128)(2,1)} %bitcast.108), calls=%async_computation.1 | async-start | bytes 524288 | tf_op jit(solution)/shard_map/all_to_all | solution.py:204
  31.3 151.2 %all-gather.7.cloned.1.call-start = ((), (), s32[]{:S(2)}) async-start(), calls=%async_computation.11 | async-start | bytes 1310720 | tf_op jit(solution)/shard_map/all_gather | solution.py:210
  61.7 36.8 %all-to-all-start.2 = ((bf16[64,8,1536]{2,0,1:T(8,128)(2,1)}), bf16[64,8,1536]{2,0,1:T(8,128)(2,1)}, u32[]{:S(2)}, u32[]{:S(2)}) async-start(bf16[64,8,1536]{2,0,1:T(8,128)(2,1)} %copy.76), calls=%async_computation.2 | async-start | bytes 3145728 | tf_op jit(solution)/shard_map/all_to_all | solution.py:204
  66.2 150.1 %all-gather.9.cloned.1.call-start = ((), (), s32[]{:S(2)}) async-start(), calls=%async_computation.12 | async-start | bytes 7864320 | tf_op jit(solution)/shard_map/all_gather | solution.py:210
  68.7 28.7 %collective-permute-start.2 = (bf16[128,2048]{1,0:T(8,128)(2,1)}, bf16[128,2048]{1,0:T(8,128)(2,1)S(1)}, u32[]{:S(2)}, u32[]{:S(2)}) collective-permute-start(bf16[128,2048]{1,0:T(8,128)(2,1)} %get-tuple-element.81), channel_id=1, source_target_pairs={{0,4},{1,5},{2,6},{3,7},{4,0},{5,1},{6,2},{7,3},{8,12},{9,13},{10,... | collective-permute-start | bytes 1572872 | tf_op jit(solution)/shard_map/ppermute | solution.py:104
  70.6 26.8 %collective-permute-start.3 = (bf16[128,2048]{1,0:T(8,128)(2,1)}, bf16[128,2048]{1,0:T(8,128)(2,1)S(1)}, u32[]{:S(2)}, u32[]{:S(2)}) collective-permute-start(bf16[128,2048]{1,0:T(8,128)(2,1)} %get-tuple-element.82), channel_id=1, source_target_pairs={{0,2},{1,3},{2,0},{3,1},{4,6},{5,7},{6,4},{7,5},{8,10},{9,11},{10,... | collective-permute-start | bytes 1572872 | tf_op jit(solution)/shard_map/ppermute | solution.py:104
  76.4 52.8 %collective-permute-start.6 = (bf16[256,2048]{1,0:T(8,128)(2,1)S(1)}, bf16[256,2048]{1,0:T(8,128)(2,1)}, u32[]{:S(2)}, u32[]{:S(2)}) collective-permute-start(bf16[256,2048]{1,0:T(8,128)(2,1)S(1)} %copy-done.23), channel_id=1, source_target_pairs={{0,1},{1,0},{2,3},{3,2},{4,5},{5,4},{6,7},{7,6},{8,9},{9,8},{10,11... | collective-permute-start | bytes 3145736 | tf_op jit(solution)/shard_map/ppermute | solution.py:104
  76.4 37.2 %collective-permute-start.5 = (bf16[256,2048]{1,0:T(8,128)(2,1)}, bf16[256,2048]{1,0:T(8,128)(2,1)}, u32[]{:S(2)}, u32[]{:S(2)}) collective-permute-start(bf16[256,2048]{1,0:T(8,128)(2,1)} %collective-permute-done.by_x_ref.refs_2_.refs_1_), channel_id=1, source_target_pairs={{0,1},{1,0},{2,3},{3,2},{4,5},{5,4},{6,7},{7,6},{8,9},{9,8},{10,11... | collective-permute-start | bytes 3145736 | tf_op jit(solution)/shard_map/ppermute | solution.py:104
  98.5 25.0 %collective-permute-start.9 = (bf16[256,2048]{1,0:T(8,128)(2,1)}, bf16[256,2048]{1,0:T(8,128)(2,1)}, u32[]{:S(2)}, u32[]{:S(2)}) collective-permute-start(bf16[256,2048]{1,0:T(8,128)(2,1)} %fence.25.refs_0_), channel_id=1, source_target_pairs={{0,4},{1,5},{2,6},{3,7},{4,0},{5,1},{6,2},{7,3},{8,12},{9,13},{10,... | collective-permute-start | bytes 3145736 | tf_op jit(solution)/shard_map/ppermute | solution.py:104
  99.9 24.7 %collective-permute-start.8 = (bf16[256,2048]{1,0:T(8,128)(2,1)}, bf16[256,2048]{1,0:T(8,128)(2,1)}, u32[]{:S(2)}, u32[]{:S(2)}) collective-permute-start(bf16[256,2048]{1,0:T(8,128)(2,1)} %fence.25.refs_0_), channel_id=1, source_target_pairs={{0,2},{1,3},{2,0},{3,1},{4,6},{5,7},{6,4},{7,5},{8,10},{9,11},{10,... | collective-permute-start | bytes 3145736 | tf_op jit(solution)/shard_map/ppermute | solution.py:104
  108.0 23.9 %collective-permute-start.7 = (bf16[256,2048]{1,0:T(8,128)(2,1)}, bf16[256,2048]{1,0:T(8,128)(2,1)}, u32[]{:S(2)}, u32[]{:S(2)}) collective-permute-start(bf16[256,2048]{1,0:T(8,128)(2,1)} %stack.8.refs_3_), channel_id=1, source_target_pairs={{0,1},{1,0},{2,3},{3,2},{4,5},{5,4},{6,7},{7,6},{8,9},{9,8},{10,11... | collective-permute-start | bytes 3145736 | tf_op jit(solution)/shard_map/ppermute | solution.py:104
  126.9 15.1 %collective-permute-start.10 = (bf16[128,2048]{1,0:T(8,128)(2,1)}, bf16[128,2048]{1,0:T(8,128)(2,1)S(1)}, u32[]{:S(2)}, u32[]{:S(2)}) collective-permute-start(bf16[128,2048]{1,0:T(8,128)(2,1)} %get-tuple-element.85), channel_id=1, source_target_pairs={{0,4},{1,5},{2,6},{3,7},{4,0},{5,1},{6,2},{7,3},{8,12},{9,13},{10,... | collective-permute-start | bytes 1572872 | tf_op jit(solution)/shard_map/ppermute | solution.py:104
  127.5 14.5 %collective-permute-start.11 = (bf16[128,2048]{1,0:T(8,128)(2,1)}, bf16[128,2048]{1,0:T(8,128)(2,1)}, u32[]{:S(2)}, u32[]{:S(2)}) collective-permute-start(bf16[128,2048]{1,0:T(8,128)(2,1)} %get-tuple-element.86), channel_id=1, source_target_pairs={{0,2},{1,3},{2,0},{3,1},{4,6},{5,7},{6,4},{7,5},{8,10},{9,11},{10,... | collective-permute-start | bytes 1572872 | tf_op jit(solution)/shard_map/ppermute | solution.py:104
  137.7 25.3 %all-to-all-start.3 = ((bf16[64,8,1536]{2,0,1:T(8,128)(2,1)}), bf16[64,8,1536]{2,0,1:T(8,128)(2,1)}, u32[]{:S(2)}, u32[]{:S(2)}) async-start(bf16[64,8,1536]{2,0,1:T(8,128)(2,1)} %copy.79), calls=%async_computation.3 | async-start | bytes 3145728 | tf_op jit(solution)/shard_map/all_to_all | solution.py:204
  144.1 18.9 %collective-permute-start.12 = (bf16[256,2048]{1,0:T(8,128)(2,1)}, bf16[256,2048]{1,0:T(8,128)(2,1)S(1)}, u32[]{:S(2)}, u32[]{:S(2)}) collective-permute-start(bf16[256,2048]{1,0:T(8,128)(2,1)} %stack.9.refs_3_), channel_id=1, source_target_pairs={{0,1},{1,0},{2,3},{3,2},{4,5},{5,4},{6,7},{7,6},{8,9},{9,8},{10,11... | collective-permute-start | bytes 3145736 | tf_op jit(solution)/shard_map/ppermute | solution.py:104
  164.0 167.3 %all-gather.11.cloned.1.call-start = ((), (), s32[]{:S(2)}) async-start(), calls=%async_computation.13 | async-start | bytes 7864320 | tf_op jit(solution)/shard_map/all_gather | solution.py:210
  196.7 14.0 %collective-permute-start.17 = (bf16[128,2048]{1,0:T(8,128)(2,1)S(1)}, bf16[128,2048]{1,0:T(8,128)(2,1)S(1)}, u32[]{:S(2)}, u32[]{:S(2)}) collective-permute-start(bf16[128,2048]{1,0:T(8,128)(2,1)S(1)} %get-tuple-element.92.refs_3_), channel_id=1, source_target_pairs={{0,2},{1,3},{2,0},{3,1},{4,6},{5,7},{6,4},{7,5},{8,10},{9,11},{10,... | collective-permute-start | bytes 1572872 | tf_op jit(solution)/shard_map/ppermute | solution.py:104
  197.2 15.2 %collective-permute-start.15 = (bf16[128,2048]{1,0:T(8,128)(2,1)S(1)}, bf16[128,2048]{1,0:T(8,128)(2,1)S(1)}, u32[]{:S(2)}, u32[]{:S(2)}) collective-permute-start(bf16[128,2048]{1,0:T(8,128)(2,1)S(1)} %get-tuple-element.95), channel_id=1, source_target_pairs={{0,4},{1,5},{2,6},{3,7},{4,0},{5,1},{6,2},{7,3},{8,12},{9,13},{10,... | collective-permute-start | bytes 1572872 | tf_op jit(solution)/shard_map/ppermute | solution.py:104
  211.9 24.8 %collective-permute-start.18 = (bf16[256,2048]{1,0:T(8,128)(2,1)}, bf16[256,2048]{1,0:T(8,128)(2,1)}, u32[]{:S(2)}, u32[]{:S(2)}) collective-permute-start(bf16[256,2048]{1,0:T(8,128)(2,1)} %pad_add_fusion.6), channel_id=1, source_target_pairs={{0,4},{1,5},{2,6},{3,7},{4,0},{5,1},{6,2},{7,3},{8,12},{9,13},{10,... | collective-permute-start | bytes 3145736 | tf_op jit(solution)/shard_map/ppermute | solution.py:104
  213.7 24.5 %collective-permute-start.16 = (bf16[256,2048]{1,0:T(8,128)(2,1)}, bf16[256,2048]{1,0:T(8,128)(2,1)}, u32[]{:S(2)}, u32[]{:S(2)}) collective-permute-start(bf16[256,2048]{1,0:T(8,128)(2,1)} %pad_add_fusion.7), channel_id=1, source_target_pairs={{0,2},{1,3},{2,0},{3,1},{4,6},{5,7},{6,4},{7,5},{8,10},{9,11},{10,... | collective-permute-start | bytes 3145736 | tf_op jit(solution)/shard_map/ppermute | solution.py:104
  216.3 228.9 %reduce-scatter.4.cloned.1.call-start = ((), (), s32[]{:S(2)}) async-start(), calls=%async_computation.14 | async-start | bytes 7864320 | tf_op jit(solution)/shard_map/reduce_scatter | solution.py:214
  216.6 27.1 %collective-permute-start.21 = (bf16[256,2048]{1,0:T(8,128)(2,1)}, bf16[256,2048]{1,0:T(8,128)(2,1)S(1)}, u32[]{:S(2)}, u32[]{:S(2)}) collective-permute-start(bf16[256,2048]{1,0:T(8,128)(2,1)} %fence.25.refs_0_), channel_id=1, source_target_pairs={{0,1},{1,0},{2,3},{3,2},{4,5},{5,4},{6,7},{7,6},{8,9},{9,8},{10,11... | collective-permute-start | bytes 3145736 | tf_op jit(solution)/shard_map/ppermute | solution.py:104
  216.7 27.0 %collective-permute-start.23 = (bf16[256,2048]{1,0:T(8,128)(2,1)}, bf16[256,2048]{1,0:T(8,128)(2,1)S(1)}, u32[]{:S(2)}, u32[]{:S(2)}) collective-permute-start(bf16[256,2048]{1,0:T(8,128)(2,1)} %collective-permute-done.9.refs_2_.by_y_ref), channel_id=1, source_target_pairs={{0,1},{1,0},{2,3},{3,2},{4,5},{5,4},{6,7},{7,6},{8,9},{9,8},{10,11... | collective-permute-start | bytes 3145736 | tf_op jit(solution)/shard_map/ppermute | solution.py:104
  217.2 26.5 %collective-permute-start.22 = (bf16[256,2048]{1,0:T(8,128)(2,1)}, bf16[256,2048]{1,0:T(8,128)(2,1)S(1)}, u32[]{:S(2)}, u32[]{:S(2)}) collective-permute-start(bf16[256,2048]{1,0:T(8,128)(2,1)} %collective-permute-done.8.refs_1_.by_x_ref), channel_id=1, source_target_pairs={{0,1},{1,0},{2,3},{3,2},{4,5},{5,4},{6,7},{7,6},{8,9},{9,8},{10,11... | collective-permute-start | bytes 3145736 | tf_op jit(solution)/shard_map/ppermute | solution.py:104
  241.7 23.4 %collective-permute-start.20 = (bf16[256,2048]{1,0:T(8,128)(2,1)S(1)}, bf16[256,2048]{1,0:T(8,128)(2,1)}, u32[]{:S(2)}, u32[]{:S(2)}) collective-permute-start(bf16[256,2048]{1,0:T(8,128)(2,1)S(1)} %multiply_convert_fusion.refs_0_), channel_id=1, source_target_pairs={{0,4},{1,5},{2,6},{3,7},{4,0},{5,1},{6,2},{7,3},{8,12},{9,13},{10,... | collective-permute-start | bytes 3145736 | tf_op jit(solution)/shard_map/ppermute | solution.py:104
  243.2 23.1 %collective-permute-start.19 = (bf16[256,2048]{1,0:T(8,128)(2,1)S(1)}, bf16[256,2048]{1,0:T(8,128)(2,1)}, u32[]{:S(2)}, u32[]{:S(2)}) collective-permute-start(bf16[256,2048]{1,0:T(8,128)(2,1)S(1)} %multiply_convert_fusion.refs_0_), channel_id=1, source_target_pairs={{0,2},{1,3},{2,0},{3,1},{4,6},{5,7},{6,4},{7,5},{8,10},{9,11},{10,... | collective-permute-start | bytes 3145736 | tf_op jit(solution)/shard_map/ppermute | solution.py:104
  268.5 11.0 %collective-permute-start.24 = (bf16[128,2048]{1,0:T(8,128)(2,1)}, bf16[128,2048]{1,0:T(8,128)(2,1)S(1)}, u32[]{:S(2)}, u32[]{:S(2)}) collective-permute-start(bf16[128,2048]{1,0:T(8,128)(2,1)} %get-tuple-element.97), channel_id=1, source_target_pairs={{0,4},{1,5},{2,6},{3,7},{4,0},{5,1},{6,2},{7,3},{8,12},{9,13},{10,... | collective-permute-start | bytes 1572872 | tf_op jit(solution)/shard_map/ppermute | solution.py:104
  269.1 10.8 %collective-permute-start.25 = (bf16[128,2048]{1,0:T(8,128)(2,1)}, bf16[128,2048]{1,0:T(8,128)(2,1)S(1)}, u32[]{:S(2)}, u32[]{:S(2)}) collective-permute-start(bf16[128,2048]{1,0:T(8,128)(2,1)} %get-tuple-element.98), channel_id=1, source_target_pairs={{0,2},{1,3},{2,0},{3,1},{4,6},{5,7},{6,4},{7,5},{8,10},{9,11},{10,... | collective-permute-start | bytes 1572872 | tf_op jit(solution)/shard_map/ppermute | solution.py:104
  269.7 10.3 %collective-permute-start.26 = (bf16[256,2048]{1,0:T(8,128)(2,1)}, bf16[256,2048]{1,0:T(8,128)(2,1)S(1)}, u32[]{:S(2)}, u32[]{:S(2)}) collective-permute-start(bf16[256,2048]{1,0:T(8,128)(2,1)} %copy-done.39), channel_id=1, source_target_pairs={{0,1},{1,0},{2,3},{3,2},{4,5},{5,4},{6,7},{7,6},{8,9},{9,8},{10,11... | collective-permute-start | bytes 3145736 | tf_op jit(solution)/shard_map/ppermute | solution.py:104
  269.7 10.3 %collective-permute-start.28 = (bf16[256,2048]{1,0:T(8,128)(2,1)}, bf16[256,2048]{1,0:T(8,128)(2,1)S(1)}, u32[]{:S(2)}, u32[]{:S(2)}) collective-permute-start(bf16[256,2048]{1,0:T(8,128)(2,1)} %collective-permute-done.20.by_y_ref.refs_2_), channel_id=1, source_target_pairs={{0,1},{1,0},{2,3},{3,2},{4,5},{5,4},{6,7},{7,6},{8,9},{9,8},{10,11... | collective-permute-start | bytes 3145736 | tf_op jit(solution)/shard_map/ppermute | solution.py:104
  270.2 9.8 %collective-permute-start.27 = (bf16[256,2048]{1,0:T(8,128)(2,1)}, bf16[256,2048]{1,0:T(8,128)(2,1)S(1)}, u32[]{:S(2)}, u32[]{:S(2)}) collective-permute-start(bf16[256,2048]{1,0:T(8,128)(2,1)} %collective-permute-done.19.by_x_ref.refs_1_), channel_id=1, source_target_pairs={{0,1},{1,0},{2,3},{3,2},{4,5},{5,4},{6,7},{7,6},{8,9},{9,8},{10,11... | collective-permute-start | bytes 3145736 | tf_op jit(solution)/shard_map/ppermute | solution.py:104
  328.0 247.7 %reduce-scatter.6.cloned.1.call-start = ((), (), s32[]{:S(2)}) async-start(), calls=%async_computation.15 | async-start | bytes 7864320 | tf_op jit(solution)/shard_map/reduce_scatter | solution.py:214
  369.4 9.5 %collective-permute-start.31 = (bf16[768,2048]{1,0:T(8,128)(2,1)}, bf16[768,2048]{1,0:T(8,128)(2,1)S(1)}, u32[]{:S(2)}, u32[]{:S(2)}) collective-permute-start(bf16[768,2048]{1,0:T(8,128)(2,1)} %fence.33), channel_id=1, source_target_pairs={{0,1},{1,0},{2,3},{3,2},{4,5},{5,4},{6,7},{7,6},{8,9},{9,8},{10,11... | collective-permute-start | bytes 9437192 | tf_op jit(solution)/shard_map/ppermute | solution.py:104
  375.8 15.9 %collective-permute-start.32 = (bf16[128,2048]{1,0:T(8,128)(2,1)S(1)}, bf16[128,2048]{1,0:T(8,128)(2,1)S(1)}, u32[]{:S(2)}, u32[]{:S(2)}) collective-permute-start(bf16[128,2048]{1,0:T(8,128)(2,1)S(1)} %get-tuple-element.107), channel_id=1, source_target_pairs={{0,4},{1,5},{2,6},{3,7},{4,0},{5,1},{6,2},{7,3},{8,12},{9,13},{10,... | collective-permute-start | bytes 1572872 | tf_op jit(solution)/shard_map/ppermute | solution.py:104
  377.4 14.6 %collective-permute-start.33 = (bf16[128,2048]{1,0:T(8,128)(2,1)S(1)}, bf16[128,2048]{1,0:T(8,128)(2,1)S(1)}, u32[]{:S(2)}, u32[]{:S(2)}) collective-permute-start(bf16[128,2048]{1,0:T(8,128)(2,1)S(1)} %get-tuple-element.105.refs_5_), channel_id=1, source_target_pairs={{0,2},{1,3},{2,0},{3,1},{4,6},{5,7},{6,4},{7,5},{8,10},{9,11},{10,... | collective-permute-start | bytes 1572872 | tf_op jit(solution)/shard_map/ppermute | solution.py:104
  405.4 18.2 %collective-permute-start.35 = (bf16[768,2048]{1,0:T(8,128)(2,1)}, bf16[768,2048]{1,0:T(8,128)(2,1)S(1)}, u32[]{:S(2)}, u32[]{:S(2)}) collective-permute-start(bf16[768,2048]{1,0:T(8,128)(2,1)} %fence.34), channel_id=1, source_target_pairs={{0,1},{1,0},{2,3},{3,2},{4,5},{5,4},{6,7},{7,6},{8,9},{9,8},{10,11... | collective-permute-start | bytes 9437192 | tf_op jit(solution)/shard_map/ppermute | solution.py:104
  405.6 30.2 %collective-permute-start.37 = (bf16[256,2048]{1,0:T(8,128)(2,1)}, bf16[256,2048]{1,0:T(8,128)(2,1)}, u32[]{:S(2)}, u32[]{:S(2)}) collective-permute-start(bf16[256,2048]{1,0:T(8,128)(2,1)} %copy-done.42), channel_id=1, source_target_pairs={{0,4},{1,5},{2,6},{3,7},{4,0},{5,1},{6,2},{7,3},{8,12},{9,13},{10,... | collective-permute-start | bytes 3145736 | tf_op jit(solution)/shard_map/ppermute | solution.py:104
  406.2 29.5 %collective-permute-start.36 = (bf16[256,2048]{1,0:T(8,128)(2,1)}, bf16[256,2048]{1,0:T(8,128)(2,1)}, u32[]{:S(2)}, u32[]{:S(2)}) collective-permute-start(bf16[256,2048]{1,0:T(8,128)(2,1)} %copy-done.41), channel_id=1, source_target_pairs={{0,2},{1,3},{2,0},{3,1},{4,6},{5,7},{6,4},{7,5},{8,10},{9,11},{10,... | collective-permute-start | bytes 3145736 | tf_op jit(solution)/shard_map/ppermute | solution.py:104
  420.8 24.4 %collective-permute-start.39 = (bf16[128,2048]{1,0:T(8,128)(2,1)}, bf16[128,2048]{1,0:T(8,128)(2,1)}, u32[]{:S(2)}, u32[]{:S(2)}) collective-permute-start(bf16[128,2048]{1,0:T(8,128)(2,1)} %get-tuple-element.118), channel_id=1, source_target_pairs={{0,4},{1,5},{2,6},{3,7},{4,0},{5,1},{6,2},{7,3},{8,12},{9,13},{10,... | collective-permute-start | bytes 1572872 | tf_op jit(solution)/shard_map/ppermute | solution.py:104
  422.3 22.9 %collective-permute-start.38 = (bf16[128,2048]{1,0:T(8,128)(2,1)S(1)}, bf16[128,2048]{1,0:T(8,128)(2,1)}, u32[]{:S(2)}, u32[]{:S(2)}) collective-permute-start(bf16[128,2048]{1,0:T(8,128)(2,1)S(1)} %get-tuple-element.111.refs_5_), channel_id=1, source_target_pairs={{0,2},{1,3},{2,0},{3,1},{4,6},{5,7},{6,4},{7,5},{8,10},{9,11},{10,... | collective-permute-start | bytes 1572872 | tf_op jit(solution)/shard_map/ppermute | solution.py:104
  445.2 24.8 %collective-permute-start.41 = (bf16[256,2048]{1,0:T(8,128)(2,1)}, bf16[256,2048]{1,0:T(8,128)(2,1)}, u32[]{:S(2)}, u32[]{:S(2)}) collective-permute-start(bf16[256,2048]{1,0:T(8,128)(2,1)} %fence.36.refs_0_), channel_id=1, source_target_pairs={{0,4},{1,5},{2,6},{3,7},{4,0},{5,1},{6,2},{7,3},{8,12},{9,13},{10,... | collective-permute-start | bytes 3145736 | tf_op jit(solution)/shard_map/ppermute | solution.py:104
  446.0 24.3 %collective-permute-start.40 = (bf16[256,2048]{1,0:T(8,128)(2,1)}, bf16[256,2048]{1,0:T(8,128)(2,1)}, u32[]{:S(2)}, u32[]{:S(2)}) collective-permute-start(bf16[256,2048]{1,0:T(8,128)(2,1)} %fence.36.refs_0_), channel_id=1, source_target_pairs={{0,2},{1,3},{2,0},{3,1},{4,6},{5,7},{6,4},{7,5},{8,10},{9,11},{10,... | collective-permute-start | bytes 3145736 | tf_op jit(solution)/shard_map/ppermute | solution.py:104
  466.5 22.1 %collective-permute-start.44 = (bf16[256,2048]{1,0:T(8,128)(2,1)}, bf16[256,2048]{1,0:T(8,128)(2,1)}, u32[]{:S(2)}, u32[]{:S(2)}) collective-permute-start(bf16[256,2048]{1,0:T(8,128)(2,1)} %fence.36.refs_0_), channel_id=1, source_target_pairs={{0,1},{1,0},{2,3},{3,2},{4,5},{5,4},{6,7},{7,6},{8,9},{9,8},{10,11... | collective-permute-start | bytes 3145736 | tf_op jit(solution)/shard_map/ppermute | solution.py:104
  472.8 13.1 %collective-permute-start.42 = (bf16[128,2048]{1,0:T(8,128)(2,1)}, bf16[128,2048]{1,0:T(8,128)(2,1)S(1)}, u32[]{:S(2)}, u32[]{:S(2)}) collective-permute-start(bf16[128,2048]{1,0:T(8,128)(2,1)} %get-tuple-element.119), channel_id=1, source_target_pairs={{0,4},{1,5},{2,6},{3,7},{4,0},{5,1},{6,2},{7,3},{8,12},{9,13},{10,... | collective-permute-start | bytes 1572872 | tf_op jit(solution)/shard_map/ppermute | solution.py:104
  474.1 13.2 %collective-permute-start.43 = (bf16[128,2048]{1,0:T(8,128)(2,1)}, bf16[128,2048]{1,0:T(8,128)(2,1)S(1)}, u32[]{:S(2)}, u32[]{:S(2)}) collective-permute-start(bf16[128,2048]{1,0:T(8,128)(2,1)} %get-tuple-element.120), channel_id=1, source_target_pairs={{0,2},{1,3},{2,0},{3,1},{4,6},{5,7},{6,4},{7,5},{8,10},{9,11},{10,... | collective-permute-start | bytes 1572872 | tf_op jit(solution)/shard_map/ppermute | solution.py:104
  474.6 17.4 %collective-permute-start.46 = (bf16[256,2048]{1,0:T(8,128)(2,1)}, bf16[256,2048]{1,0:T(8,128)(2,1)S(1)}, u32[]{:S(2)}, u32[]{:S(2)}) collective-permute-start(bf16[256,2048]{1,0:T(8,128)(2,1)} %collective-permute-done.41.by_y_ref.refs_2_), channel_id=1, source_target_pairs={{0,1},{1,0},{2,3},{3,2},{4,5},{5,4},{6,7},{7,6},{8,9},{9,8},{10,11... | collective-permute-start | bytes 3145736 | tf_op jit(solution)/shard_map/ppermute | solution.py:104
  474.6 16.3 %collective-permute-start.45 = (bf16[256,2048]{1,0:T(8,128)(2,1)}, bf16[256,2048]{1,0:T(8,128)(2,1)S(1)}, u32[]{:S(2)}, u32[]{:S(2)}) collective-permute-start(bf16[256,2048]{1,0:T(8,128)(2,1)} %collective-permute-done.40.by_x_ref.refs_1_), channel_id=1, source_target_pairs={{0,1},{1,0},{2,3},{3,2},{4,5},{5,4},{6,7},{7,6},{8,9},{9,8},{10,11... | collective-permute-start | bytes 3145736 | tf_op jit(solution)/shard_map/ppermute | solution.py:104
  496.2 53.8 %all-to-all-start.4 = ((bf16[8,64,1536]{2,1,0:T(8,128)(2,1)}), bf16[8,64,1536]{2,1,0:T(8,128)(2,1)}, u32[]{:S(2)}, u32[]{:S(2)}) async-start(bf16[8,64,1536]{2,1,0:T(8,128)(2,1)} %bitcast.118), calls=%async_computation.5 | async-start | bytes 3145728 | tf_op jit(solution)/shard_map/all_to_all | solution.py:218
  500.5 138.8 %reduce-scatter.8.cloned.1.call-start = ((), (), s32[]{:S(2)}) async-start(), calls=%async_computation.16 | async-start | bytes 3276800 | tf_op jit(solution)/shard_map/reduce_scatter | solution.py:214
  502.2 47.8 %collective-permute-start.49 = (bf16[256,2048]{1,0:T(8,128)(2,1)S(1)}, bf16[256,2048]{1,0:T(8,128)(2,1)}, u32[]{:S(2)}, u32[]{:S(2)}) collective-permute-start(bf16[256,2048]{1,0:T(8,128)(2,1)S(1)} %pad_add_fusion.2), channel_id=1, source_target_pairs={{0,4},{1,5},{2,6},{3,7},{4,0},{5,1},{6,2},{7,3},{8,12},{9,13},{10,... | collective-permute-start | bytes 3145736 | tf_op jit(solution)/shard_map/ppermute | solution.py:104
  505.4 44.7 %collective-permute-start.48 = (bf16[256,2048]{1,0:T(8,128)(2,1)S(1)}, bf16[256,2048]{1,0:T(8,128)(2,1)}, u32[]{:S(2)}, u32[]{:S(2)}) collective-permute-start(bf16[256,2048]{1,0:T(8,128)(2,1)S(1)} %pad_add_fusion.3), channel_id=1, source_target_pairs={{0,2},{1,3},{2,0},{3,1},{4,6},{5,7},{6,4},{7,5},{8,10},{9,11},{10,... | collective-permute-start | bytes 3145736 | tf_op jit(solution)/shard_map/ppermute | solution.py:104
  574.9 15.0 %collective-permute-start.51 = (bf16[768,2048]{1,0:T(8,128)(2,1)}, bf16[768,2048]{1,0:T(8,128)(2,1)}, u32[]{:S(2)}, u32[]{:S(2)}) collective-permute-start(bf16[768,2048]{1,0:T(8,128)(2,1)} %fence.41), channel_id=1, source_target_pairs={{0,1},{1,0},{2,3},{3,2},{4,5},{5,4},{6,7},{7,6},{8,9},{9,8},{10,11... | collective-permute-start | bytes 9437192 | tf_op jit(solution)/shard_map/ppermute | solution.py:104
  576.0 25.9 %all-to-all-start.5 = ((bf16[8,64,1536]{2,1,0:T(8,128)(2,1)}), bf16[8,64,1536]{2,1,0:T(8,128)(2,1)}, u32[]{:S(2)}, u32[]{:S(2)}) async-start(bf16[8,64,1536]{2,1,0:T(8,128)(2,1)} %bitcast.119), calls=%async_computation.7 | async-start | bytes 3145728 | tf_op jit(solution)/shard_map/all_to_all | solution.py:218
  597.7 15.0 %collective-permute-start.52 = (bf16[128,2048]{1,0:T(8,128)(2,1)}, bf16[128,2048]{1,0:T(8,128)(2,1)S(1)}, u32[]{:S(2)}, u32[]{:S(2)}) collective-permute-start(bf16[128,2048]{1,0:T(8,128)(2,1)} %get-tuple-element.134), channel_id=1, source_target_pairs={{0,4},{1,5},{2,6},{3,7},{4,0},{5,1},{6,2},{7,3},{8,12},{9,13},{10,... | collective-permute-start | bytes 1572872 | tf_op jit(solution)/shard_map/ppermute | solution.py:104
  599.7 15.5 %collective-permute-start.54 = (bf16[128,2048]{1,0:T(8,128)(2,1)}, bf16[128,2048]{1,0:T(8,128)(2,1)S(1)}, u32[]{:S(2)}, u32[]{:S(2)}) collective-permute-start(bf16[128,2048]{1,0:T(8,128)(2,1)} %get-tuple-element.136), channel_id=1, source_target_pairs={{0,2},{1,3},{2,0},{3,1},{4,6},{5,7},{6,4},{7,5},{8,10},{9,11},{10,... | collective-permute-start | bytes 1572872 | tf_op jit(solution)/shard_map/ppermute | solution.py:104
  622.0 25.7 %collective-permute-start.55 = (bf16[256,2048]{1,0:T(8,128)(2,1)}, bf16[256,2048]{1,0:T(8,128)(2,1)}, u32[]{:S(2)}, u32[]{:S(2)}) collective-permute-start(bf16[256,2048]{1,0:T(8,128)(2,1)} %pad_add_fusion.refs_2_), channel_id=1, source_target_pairs={{0,4},{1,5},{2,6},{3,7},{4,0},{5,1},{6,2},{7,3},{8,12},{9,13},{10,... | collective-permute-start | bytes 3145736 | tf_op jit(solution)/shard_map/ppermute | solution.py:104
  623.1 25.6 %collective-permute-start.53 = (bf16[256,2048]{1,0:T(8,128)(2,1)S(1)}, bf16[256,2048]{1,0:T(8,128)(2,1)}, u32[]{:S(2)}, u32[]{:S(2)}) collective-permute-start(bf16[256,2048]{1,0:T(8,128)(2,1)S(1)} %copy-done.65), channel_id=1, source_target_pairs={{0,2},{1,3},{2,0},{3,1},{4,6},{5,7},{6,4},{7,5},{8,10},{9,11},{10,... | collective-permute-start | bytes 3145736 | tf_op jit(solution)/shard_map/ppermute | solution.py:104
  625.0 13.1 %collective-permute-start.62 = (f32[4224]{0:T(1024)S(1)}, f32[4224]{0:T(1024)S(1)}, u32[]{:S(2)}, u32[]{:S(2)}) collective-permute-start(f32[4224]{0:T(1024)S(1)} %add_add_fusion.1), channel_id=1, source_target_pairs={{0,24},{8,16},{16,8},{24,0},{1,25},{9,17},{17,9},{25,1},{2,26},{10... | collective-permute-start | bytes 50696 | tf_op jit(solution)/shard_map/ppermute | solution.py:197
  628.3 9.8 %collective-permute-start.61 = (f32[4224]{0:T(1024)S(1)}, f32[4224]{0:T(1024)S(1)}, u32[]{:S(2)}, u32[]{:S(2)}) collective-permute-start(f32[4224]{0:T(1024)S(1)} %add_add_fusion.1), channel_id=1, source_target_pairs={{0,16},{8,24},{16,0},{24,8},{1,17},{9,25},{17,1},{25,9},{2,18},{10... | collective-permute-start | bytes 50696 | tf_op jit(solution)/shard_map/ppermute | solution.py:197
  639.3 15.5 %all-to-all-start.6 = ((bf16[8,64,640]{2,1,0:T(8,128)(2,1)}), bf16[8,64,640]{2,1,0:T(8,128)(2,1)S(1)}, u32[]{:S(2)}, u32[]{:S(2)}) async-start(bf16[8,64,640]{2,1,0:T(8,128)(2,1)} %bitcast.133), calls=%async_computation.9 | async-start | bytes 1310720 | tf_op jit(solution)/shard_map/all_to_all | solution.py:218
  (98 other events, 437.1 us)
Sparse Core Ops, SparseCore 0:
  24.1 36.4 all-gather.4
  62.2 26.7 all-gather.6
  100.6 115.6 all-gather.8
  217.7 113.5 all-gather.10
  333.5 108.9 reduce-scatter.3
  466.6 109.0 reduce-scatter.5
  578.1 52.8 reduce-scatter.7
